TPU v7x, 512 devices: a whole 4x4x16 slice. The times are simulated.
512 devices in a mesh: scene: 32 (over x, z_hi, core), view: 16 (over z_lo, y).
Axes of the slice: x: 4, y: 4, z: 16 (z_hi: 4, z_lo: 4; z = z_hi * 4 + z_lo), core: 2. Of those that a mesh axis runs over, the one named last changes fastest.
Arguments:
- query_rows: bfloat16 [32, 16, 256, 512], P('scene', 'view'), may hold values from -270 to 270, as said below
- key_rows: bfloat16 [32, 16, 256, 512], P('scene', 'view'), may hold values from -7 to 7, as said below
- value_rows: bfloat16 [32, 16, 256, 512], P('scene', 'view'), may hold values from -24 to 24
- grad_out: bfloat16 [32, 16, 256, 1024], P('scene', 'view'), may hold values from -24 to 24
- out_weight: bfloat16 [512, 1024], replicated, may hold values from -0.25 to 0.25
- fetch_list: int32 [32, 16, 16], P('scene'), may hold values from 0 to 1
- read_mask: int32 [32, 16, 2, 16], P('scene', 'view'), may hold values 0 or 1
Outputs:
- layer_out: bfloat16 [32, 16, 256, 1024], P('scene', 'view')
- grad_query: bfloat16 [32, 16, 256, 512], P('scene', 'view')
- grad_key: bfloat16 [32, 16, 256, 512], P('scene', 'view')
- grad_value: bfloat16 [32, 16, 256, 512], P('scene', 'view')
- grad_weight: float32 [512, 1024], P('scene', 'view')
Inputs may be any that keep to these rules, and one draw needn't show every extreme that they name: `query_rows`: queries of order one; some rows may be large multiples of other rows of keys. `key_rows`: keys of order one.
All inputs are finite; a program needn't handle non-finite values. No bound on the sum of `read_mask` on one device may be relied on, other than what follows from the above.
Results may differ from a plain program's by a relative error of at most 0.029.
Values may be sent and summed in bfloat16 or wider, within the bound.
No kernel may reach another device: no remote copies, remote signals or barrier semaphores. Data moves between devices by JAX's collectives and lax.ppermute only.
A program may use at most 128 MiB of HBM per device.

v0:
```python
import jax
import jax.numpy as jnp
from jax import lax
from jax.sharding import PartitionSpec as P

HEADS = 8
HEAD_DIM = 64
BLK = 128


def head_pass(query_head, key_head, value_head, grad_head, visible, score_scale):
    scores = jnp.dot(query_head, key_head.T, preferred_element_type=jnp.float32) * score_scale
    scores = jnp.where(visible, scores, -jnp.inf)
    row_max = jnp.max(scores, axis=1, keepdims=True)
    weights_raw = jnp.exp(scores - row_max)
    attn_prob = weights_raw / jnp.sum(weights_raw, axis=1, keepdims=True)
    prob_low = attn_prob.astype(jnp.bfloat16)
    head_out = jnp.dot(prob_low, value_head, preferred_element_type=jnp.float32)
    grad_prob = jnp.dot(grad_head, value_head.T, preferred_element_type=jnp.float32)
    row_delta = jnp.sum(attn_prob * grad_prob, axis=1, keepdims=True)
    grad_score = (attn_prob * (grad_prob - row_delta) * score_scale).astype(jnp.bfloat16)
    grad_qhead = jnp.dot(grad_score, key_head, preferred_element_type=jnp.float32)
    grad_khead = jnp.dot(grad_score.T, query_head, preferred_element_type=jnp.float32)
    grad_vhead = jnp.dot(prob_low.T, grad_head, preferred_element_type=jnp.float32)
    return (head_out, grad_qhead, grad_khead, grad_vhead)


def split_heads(rows):
    return rows.reshape(rows.shape[0], HEADS, HEAD_DIM).transpose(1, 0, 2)


def join_heads(rows):
    return rows.transpose(1, 0, 2).reshape(rows.shape[1], HEADS * HEAD_DIM)


def view_pass(query_own, keys_all, values_all, grad_attn, visible):
    score_scale = HEAD_DIM ** (-0.5)

    def one_head(head_items):
        return head_pass(
            head_items[0], head_items[1], head_items[2], head_items[3], visible, score_scale
        )

    results = lax.map(
        one_head,
        (
            split_heads(query_own),
            split_heads(keys_all),
            split_heads(values_all),
            split_heads(grad_attn),
        ),
    )
    return tuple((join_heads(item) for item in results))


def on_device(query_rows, key_rows, value_rows, grad_out, out_weight, fetch_list, read_mask):
    query_own = query_rows[0, 0]
    keys_own = key_rows[0, 0]
    values_own = value_rows[0, 0]
    grad_rows = grad_out[0, 0]
    fetch_scene = fetch_list[0]
    reads_own = read_mask[0, 0]
    view_count = lax.axis_size("view")
    own_view = lax.axis_index("view")
    tok_rows = query_own.shape[0]
    inner_width = query_own.shape[1]
    block_count = tok_rows // BLK
    view_ids = jnp.arange(view_count, dtype=jnp.int32)
    block_ids = jnp.arange(block_count, dtype=jnp.int32)
    wanted = lax.dynamic_index_in_dim(fetch_scene, own_view, 0, keepdims=False)
    given = lax.dynamic_index_in_dim(fetch_scene, own_view, 1, keepdims=False)
    grad_attn = jnp.dot(grad_rows, out_weight.T, preferred_element_type=jnp.float32).astype(
        jnp.bfloat16
    )
    paired = jnp.concatenate([keys_own, values_own], axis=1)
    all_views = lax.all_gather(paired, "view", axis=0, tiled=True)
    all_views = all_views.reshape(view_count, block_count, BLK, 2 * inner_width)
    select = (wanted[:, None] == block_ids[None, :]).astype(jnp.bfloat16)
    remote = jnp.einsum(
        "wn,wnbc->wbc", select, all_views, preferred_element_type=jnp.float32
    ).astype(jnp.bfloat16)
    remote_keys = remote[:, :, :inner_width].reshape(view_count * BLK, inner_width)
    remote_values = remote[:, :, inner_width:].reshape(view_count * BLK, inner_width)
    keys_all = jnp.concatenate([keys_own, remote_keys], axis=0)
    values_all = jnp.concatenate([values_own, remote_values], axis=0)
    others = (reads_own == 1) & (view_ids != own_view)[None, :]
    remote_seen = jnp.repeat(jnp.repeat(others, BLK, axis=0), BLK, axis=1)
    visible = jnp.concatenate([jnp.ones((tok_rows, tok_rows), dtype=bool), remote_seen], axis=1)
    attn_full, grad_q, grad_kall, grad_vall = view_pass(
        query_own, keys_all, values_all, grad_attn, visible
    )
    attn_low = attn_full.astype(jnp.bfloat16)
    layer_rows = jnp.dot(attn_low, out_weight, preferred_element_type=jnp.float32).astype(
        jnp.bfloat16
    )
    remote_grads = jnp.concatenate([grad_kall[tok_rows:], grad_vall[tok_rows:]], axis=1).astype(
        jnp.bfloat16
    )
    remote_grads = remote_grads.reshape(view_count, BLK, 2 * inner_width)
    returned = lax.all_to_all(remote_grads, "view", split_axis=0, concat_axis=0, tiled=True)
    landing = ((given[:, None] == block_ids[None, :]) & (view_ids != own_view)[:, None]).astype(
        jnp.bfloat16
    )
    added = jnp.einsum("vn,vbc->nbc", landing, returned, preferred_element_type=jnp.float32)
    own_grads = jnp.concatenate([grad_kall[:tok_rows], grad_vall[:tok_rows]], axis=1)
    summed = (own_grads + added.reshape(tok_rows, 2 * inner_width)).astype(jnp.bfloat16)
    weight_term = jnp.dot(attn_low.T, grad_rows, preferred_element_type=jnp.float32)
    grad_share = lax.psum_scatter(
        weight_term.astype(jnp.bfloat16), "scene", scatter_dimension=0, tiled=True
    ).astype(jnp.float32)
    grad_share = lax.psum_scatter(
        grad_share.astype(jnp.bfloat16), "view", scatter_dimension=1, tiled=True
    ).astype(jnp.float32)
    grad_scale = float(lax.axis_size("scene") * view_count * tok_rows) ** (-0.5)
    grad_share = grad_share * grad_scale
    return (
        layer_rows[None, None],
        grad_q.astype(jnp.bfloat16)[None, None],
        summed[:, :inner_width][None, None],
        summed[:, inner_width:][None, None],
        grad_share,
    )


def solution(mesh):
    placed = (
        P("scene", "view", None, None),
        P("scene", "view", None, None),
        P("scene", "view", None, None),
        P("scene", "view", None, None),
        P(),
        P("scene", None, None),
        P("scene", "view", None, None),
    )
    return jax.shard_map(
        on_device,
        mesh=mesh,
        in_specs=placed,
        out_specs=(
            P("scene", "view", None, None),
            P("scene", "view", None, None),
            P("scene", "view", None, None),
            P("scene", "view", None, None),
            P("scene", "view"),
        ),
        check_vma=False,
    )
```

profile of v0, /device:TPU:6, one launch (start us, length us, event | category | flops | bytes accessed | tf_op | source)
XLA Modules:
  0.0 529.9 jit_solution(8183941287087574747)
XLA Ops:
  14.3 108.4 %all-gather.2.cloned.1.call-done = bf16[4096,1024]{1,0:T(8,128)(2,1)} async-done(((bf16[256,1024]{1,0:T(8,128)(2,1)}), bf16[4096,1024]{1,0:T(8,128)(2,1)}) %all-gather.2.cloned.1.call-update) | async-done | bytes 8388624 | tf_op jit(solution)/shard_map/all_gather | solution.py:76
  122.7 31.7 %fusion.34 = bf16[16,1,128,1024]{3,1,2,0:T(2,128)(2,1)} fusion(bf16[16,2,128,1024]{3,2,1,0:T(8,128)(2,1)} %bitcast.182, pred[16,2,1,1]{1,0,2,3:T(8,128)(4,1)S(1)} %fusion.43), kind=kOutput, calls=%fused_computation.41 | convolution fusion | flops 8388608 | bytes 12582944 | tf_op jit(solution)/shard_map/wn,wnbc->wbc/dot_general | solution.py:79
  154.5 12.6 %copy.48 = bf16[16,1,128,1024]{2,0,3,1:T(8,128)(2,1)} copy(bf16[16,1,128,1024]{3,1,2,0:T(2,128)(2,1)} %fusion.34) | data formatting | bytes 8388608 | tf_op jit(solution)/shard_map/wn,wnbc->wbc/dot_general | solution.py:79
  167.1 5.0 fusion.51
  172.0 4.2 concatenate.40
  176.2 4.2 concatenate.36
  180.4 3.9 maximum_bitcast_fusion
  184.3 86.6 %while.16 = (s32[]{:T(128)}, bf16[8,256,64]{1,2,0:T(8,128)(2,1)S(1)}, bf16[8,256,64]{1,2,0:T(8,128)(2,1)}, f32[8,2304,64]{1,2,0:T(8,128)}, f32[8,2304,64]{1,2,0:...) while((s32[]{:T(128)}, ...), condition=%wide.region_4.5_spmd, body=%wide.region_0.4_spmd.sunk | while | flops 465370368 | bytes 25644148 | solution.py:44
  190.4 2.1 fusion.83
  201.3 2.1 fusion.83
  212.1 2.1 fusion.83
  222.9 2.1 fusion.83
  233.7 2.1 fusion.83
  244.5 2.1 fusion.83
  255.3 2.1 fusion.83
  266.2 2.1 fusion.83
  270.9 2.5 slice.56
  274.0 2.5 slice.57
  277.2 2.3 pad_maximum_fusion
  279.5 6.7 %copy.39 = bf16[16,128,1024]{2,1,0:T(8,128)(2,1)} copy(bf16[16,128,1024]{1,0,2:T(8,128)(2,1)} %pad_maximum_fusion) | data formatting | bytes 8388608 | tf_op jit(solution)/shard_map/concatenate | solution.py:96
  286.2 4.6 all-to-all-start
  292.6 131.3 %reduce-scatter.5.cloned.1.call-done = bf16[16,1024]{1,0:T(8,128)(2,1)} async-done(((bf16[512,1024]{1,0:T(8,128)(2,1)}), bf16[16,1024]{1,0:T(8,128)(2,1)}) %reduce-scatter.5.cloned.1.call-update) | async-done | bytes 32784 | tf_op jit(solution)/shard_map/reduce_scatter | solution.py:108
  429.7 82.8 %reduce-scatter.7.cloned.1.call-done = bf16[64,16]{1,0:T(8,128)(2,1)} async-done(((bf16[1024,16]{1,0:T(8,128)(2,1)}), bf16[64,16]{1,0:T(8,128)(2,1)}) %reduce-scatter.7.cloned.1.call-update) | async-done | bytes 2064
  513.9 4.7 fusion.36
  (111 shorter events, 91.8 us)
Async XLA Ops:
  7.2 4.5 copy-start
  7.2 4.3 copy-start.2
  7.2 4.5 copy-start.1
  7.2 115.5 %all-gather.2.cloned.1.call-start = ((), (), s32[]{:S(2)}) async-start(), calls=%async_computation.3 | async-start | bytes 8912896 | tf_op jit(solution)/shard_map/all_gather | solution.py:76
  9.2 3.1 copy-start.5
  12.2 2.1 copy-start.4
  286.2 227.7 %all-to-all-start = ((bf16[16,128,1024]{2,1,0:T(8,128)(2,1)}), bf16[16,128,1024]{2,1,0:T(8,128)(2,1)}, u32[]{:S(2)}, u32[]{:S(2)}) async-start(bf16[16,128,1024]{2,1,0:T(8,128)(2,1)} %copy.39), calls=%async_computation | async-start | bytes 8388608 | tf_op jit(solution)/shard_map/all_to_all | solution.py:100
  290.8 133.1 %reduce-scatter.5.cloned.1.call-start = ((), (), s32[]{:S(2)}) async-start(), calls=%async_computation.4 | async-start | bytes 1081344 | tf_op jit(solution)/shard_map/reduce_scatter | solution.py:108
  292.3 136.6 %copy-start.3 = (bf16[8,256,64]{1,2,0:T(8,128)(2,1)S(1)}, bf16[8,256,64]{1,2,0:T(8,128)(2,1)}, u32[]{:S(2)}) copy-start(bf16[8,256,64]{1,2,0:T(8,128)(2,1)} %get-tuple-element.61) | copy-start | bytes 786436
  292.3 220.2 %reduce-scatter.7.cloned.1.call-start = ((), (), s32[]{:S(2)}) async-start(), calls=%async_computation.5 | async-start | bytes 278528
Sparse Core Ops, SparseCore 0:
  10.7 112.0 all-gather.1
  296.0 127.8 reduce-scatter.4
  427.4 85.0 reduce-scatter.6
where the time goes:
time: 532 us; the launch traced here: 530 us
  waiting for transfers between devices  322 us (61%)
  matrix products  116 us (22%)
  local copies, waits for them, and re-layouts  53.4 us (10%)
  other arithmetic  18.8 us (4%)
  between operations  14.1 us (3%)
    reduce_scatter x1, waiting for transfers between devices, on_device(): lax.psum_scatter(weight_term.astype(jnp.bfloat16), 'scene', scatter_dimen...  131 us
    all_gather x1, waiting for transfers between devices, on_device(): all_views = lax.all_gather(paired, 'view', axis=0, tiled=True)  108 us
    unnamed x4, waiting for transfers between devices  82.8 us
    dot_general x1, matrix products, on_device(): jnp.einsum('wn,wnbc->wbc', select, all_views, preferred_element_type=jnp....  31.7 us
    dot_general x8, matrix products, head_pass(): jnp.dot(grad_score, key_head, preferred_element_type=jnp.float32)  16.7 us
    dot_general x8, matrix products, head_pass(): jnp.dot(grad_head, value_head.T, preferred_element_type=jnp.float32)  13.8 us
    dot_general x8, matrix products, head_pass(): jnp.dot(query_head, key_head.T, preferred_element_type=jnp.float32)  12.9 us
    dot_general x8, matrix products, head_pass(): head_out = jnp.dot(prob_low, value_head, preferred_element_type=jnp.float32)  12.6 us
  transfers between devices with their start and end apart: 4, of which 3 were waited for; matrix products, arithmetic and copies ran while one was open for 3% of the time, Pallas kernels for 0%

commit v1 on v0

v1 whole, which is shorter than its diff:
```python
import jax
import jax.numpy as jnp
from jax import lax
from jax.experimental import pallas as pl
from jax.experimental.pallas import tpu as pltpu
from jax.sharding import PartitionSpec as P

HEADS = 8
HEAD_DIM = 64
BLK = 128
TOK = 256
VIEWS = 16
INNER = 512
D = 1024
KEYS = TOK + VIEWS * BLK
BF = jnp.bfloat16
F32 = jnp.float32
SCALE = HEAD_DIM ** (-0.5)
PACK_ROWS = TOK + BLK + 16
BACK_ROWS = TOK + BLK
VMEM = pl.BlockSpec(memory_space=pltpu.VMEM)
SMEM = pl.BlockSpec(memory_space=pltpu.SMEM)


def pack_kernel(q_ref, k_ref, v_ref, go_ref, w_ref, mask_ref, out_ref):
    ga = lax.dot_general(
        go_ref[...], w_ref[...], (((1,), (1,)), ((), ())), preferred_element_type=F32
    ).astype(BF)
    q = q_ref[...] * jnp.asarray(SCALE, BF)
    for h in range(HEADS):
        c = slice(h * HEAD_DIM, (h + 1) * HEAD_DIM)
        kv = jnp.concatenate([k_ref[:, c], v_ref[:, c]], axis=1)
        qg = jnp.concatenate([q[:, c], ga[:, c]], axis=1)
        for p in range(2):
            j = 2 * h + p
            out_ref[j, 0:TOK, :] = kv
            out_ref[j, TOK : TOK + BLK, :] = qg[p * BLK : (p + 1) * BLK, :]
            out_ref[j, TOK + BLK : PACK_ROWS, 0:VIEWS] = jnp.broadcast_to(
                mask_ref[p : p + 1, :], (16, VIEWS)
            ).astype(BF)


def attn_kernel(fetch_ref, mask_ref, in_ref, out_ref, kvt, ksel, ktsel, s_ref, d_ref, x_ref, acc):
    lane = lax.broadcasted_iota(jnp.int32, (BLK, 2 * HEAD_DIM), 1)
    for w in range(VIEWS):
        kvt[:, w * TOK : (w + 1) * TOK] = in_ref[w, 0:TOK, :].T
        acc[w] = jnp.zeros((TOK, 2 * HEAD_DIM), F32)

    def one_view(v, carry):
        qg = in_ref[v, TOK : TOK + BLK, :]
        zero = jnp.zeros_like(qg)
        qg2 = jnp.concatenate(
            [jnp.where(lane < HEAD_DIM, qg, zero), jnp.where(lane >= HEAD_DIM, qg, zero)], axis=0
        )
        ksel[0:TOK, :] = in_ref[v, 0:TOK, :]
        ktsel[:, 0:TOK] = kvt[:, pl.ds(pl.multiple_of(v * TOK, TOK), TOK)]
        for w in range(VIEWS):
            at = pl.multiple_of(fetch_ref[v, w] * BLK, BLK)
            to = slice(TOK + w * BLK, TOK + (w + 1) * BLK)
            ksel[to, :] = in_ref[w, pl.ds(at, BLK), :]
            ktsel[:, to] = kvt[:, pl.ds(pl.multiple_of(w * TOK + at, BLK), BLK)]
        top = None
        for c in range(KEYS // TOK):
            rows = slice(c * TOK, (c + 1) * TOK)
            r = lax.dot_general(
                ksel[rows, :], qg2, (((1,), (1,)), ((), ())), preferred_element_type=F32
            )
            d_ref[rows, :] = r[:, BLK:]
            for half in range(2):
                s = r[half * BLK : (half + 1) * BLK, 0:BLK]
                if c > 0:
                    w = 2 * (c - 1) + half
                    seen = jnp.logical_and(mask_ref[v, w] == 1, w != v)
                    s = s + jnp.where(seen, 0.0, -jnp.inf)
                s_ref[c * TOK + half * BLK : c * TOK + (half + 1) * BLK, :] = s
                best = jnp.max(s.reshape(BLK // 8, 8, BLK), axis=0)
                top = best if top is None else jnp.maximum(top, best)
        top = jnp.max(top, axis=0, keepdims=True)
        total = jnp.zeros((8, BLK), F32)
        delta = jnp.zeros((8, BLK), F32)
        for c in range(KEYS // BLK):
            rows = slice(c * BLK, (c + 1) * BLK)
            e = jnp.exp(s_ref[rows, :] - top)
            s_ref[rows, :] = e
            total = total + jnp.sum(e.reshape(BLK // 8, 8, BLK), axis=0)
            delta = delta + jnp.sum((e * d_ref[rows, :]).reshape(BLK // 8, 8, BLK), axis=0)
        total = jnp.sum(total, axis=0, keepdims=True)
        share = 1.0 / total
        delta = jnp.sum(delta, axis=0, keepdims=True) * share
        for c in range(KEYS // TOK):
            rows = slice(c * TOK, (c + 1) * TOK)
            prob = s_ref[rows, :] * share
            x_ref[rows, 0:BLK] = (prob * (d_ref[rows, :] - delta)).astype(BF)
            x_ref[rows, BLK:] = prob.astype(BF)
            g = jnp.dot(x_ref[rows, :], qg2, preferred_element_type=F32)
            if c == 0:
                acc[v] += g
            else:
                for half in range(2):
                    w = 2 * (c - 1) + half
                    at = pl.multiple_of(fetch_ref[v, w] * BLK, BLK)
                    acc[w, pl.ds(at, BLK), :] += g[half * BLK : (half + 1) * BLK, :]
        o = jnp.dot(ktsel[...], x_ref[...], preferred_element_type=F32)
        both = jnp.concatenate([o[:HEAD_DIM, :BLK] * SCALE, o[HEAD_DIM:, BLK:]], axis=0)
        out_ref[v, TOK:BACK_ROWS, :] = both.T.astype(BF)
        return carry

    lax.fori_loop(0, VIEWS, one_view, 0)
    for w in range(VIEWS):
        out_ref[w, 0:TOK, :] = acc[w].astype(BF)


def finish_kernel(in_ref, go_ref, w_ref, layer_ref, gq_ref, gk_ref, gv_ref, wt_ref, attn):
    for h in range(HEADS):
        c = slice(h * HEAD_DIM, (h + 1) * HEAD_DIM)
        kv = in_ref[2 * h, 0:TOK, :].astype(F32) + in_ref[2 * h + 1, 0:TOK, :].astype(F32)
        kv = kv.astype(BF)
        gk_ref[:, c] = kv[:, :HEAD_DIM]
        gv_ref[:, c] = kv[:, HEAD_DIM:]
        for p in range(2):
            rows = slice(p * BLK, (p + 1) * BLK)
            both = in_ref[2 * h + p, TOK:BACK_ROWS, :]
            gq_ref[rows, c] = both[:, :HEAD_DIM]
            attn[rows, c] = both[:, HEAD_DIM:]
    layer_ref[...] = jnp.dot(attn[...], w_ref[...], preferred_element_type=F32).astype(BF)
    term = lax.dot_general(
        attn[...], go_ref[...], (((0,), (0,)), ((), ())), preferred_element_type=F32
    ).astype(BF)
    wide = D // VIEWS
    for j in range(VIEWS):
        c = slice(j * wide, (j + 1) * wide)
        wt_ref[j, :, 0:wide] = term[: INNER // 2, c]
        wt_ref[j, :, wide:] = term[INNER // 2 :, c]


def params(mib):
    return pltpu.CompilerParams(vmem_limit_bytes=mib * 1024 * 1024)


def on_device(query_rows, key_rows, value_rows, grad_out, out_weight, fetch_list, read_mask):
    go = grad_out[0, 0]
    sent = pl.pallas_call(
        pack_kernel,
        out_shape=jax.ShapeDtypeStruct((VIEWS, PACK_ROWS, 2 * HEAD_DIM), BF),
        in_specs=[VMEM] * 6,
        out_specs=VMEM,
        compiler_params=params(24),
    )(query_rows[0, 0], key_rows[0, 0], value_rows[0, 0], go, out_weight, read_mask[0, 0])
    here = lax.all_to_all(sent, "view", split_axis=0, concat_axis=0, tiled=True)
    reads = here[:, TOK + BLK, :VIEWS].astype(jnp.int32)
    back = pl.pallas_call(
        attn_kernel,
        out_shape=jax.ShapeDtypeStruct((VIEWS, BACK_ROWS, 2 * HEAD_DIM), BF),
        in_specs=[SMEM, SMEM, VMEM],
        out_specs=VMEM,
        scratch_shapes=[
            pltpu.VMEM((2 * HEAD_DIM, VIEWS * TOK), BF),
            pltpu.VMEM((KEYS, 2 * HEAD_DIM), BF),
            pltpu.VMEM((2 * HEAD_DIM, KEYS), BF),
            pltpu.VMEM((KEYS, BLK), F32),
            pltpu.VMEM((KEYS, BLK), F32),
            pltpu.VMEM((KEYS, 2 * BLK), BF),
            pltpu.VMEM((VIEWS, TOK, 2 * HEAD_DIM), F32),
        ],
        compiler_params=params(32),
    )(fetch_list[0], reads, here)
    home = lax.all_to_all(back, "view", split_axis=0, concat_axis=0, tiled=True)
    layer, gq, gk, gv, terms = pl.pallas_call(
        finish_kernel,
        out_shape=(
            jax.ShapeDtypeStruct((TOK, D), BF),
            jax.ShapeDtypeStruct((TOK, INNER), BF),
            jax.ShapeDtypeStruct((TOK, INNER), BF),
            jax.ShapeDtypeStruct((TOK, INNER), BF),
            jax.ShapeDtypeStruct((VIEWS, INNER // 2, 2 * D // VIEWS), BF),
        ),
        in_specs=[VMEM] * 3,
        out_specs=(VMEM,) * 5,
        scratch_shapes=[pltpu.VMEM((TOK, INNER), BF)],
        compiler_params=params(32),
    )(home, go, out_weight)
    scenes = lax.axis_size("scene")
    wide = D // VIEWS
    terms = lax.all_to_all(terms, "view", split_axis=0, concat_axis=0, tiled=True)
    part = jnp.sum(terms.astype(F32), axis=0).astype(BF)
    part = jnp.concatenate([part[:, :wide], part[:, wide:]], axis=0)
    part = part.reshape(scenes, INNER // scenes, wide)
    part = lax.all_to_all(part, "scene", split_axis=0, concat_axis=0, tiled=True)
    share = jnp.sum(part.astype(F32), axis=0) * float(scenes * VIEWS * TOK) ** (-0.5)
    return (layer[None, None], gq[None, None], gk[None, None], gv[None, None], share)


def solution(mesh):
    rows = P("scene", "view", None, None)
    return jax.shard_map(
        on_device,
        mesh=mesh,
        in_specs=(rows, rows, rows, rows, P(), P("scene", None, None), rows),
        out_specs=(rows, rows, rows, rows, P("scene", "view")),
        check_vma=False,
    )
```

time: 532 us -> 197 us (0.37)
  waiting for transfers between devices: 322 us -> 0 us
  blocking collectives: 0 us -> 149 us
  matrix products: 116 us -> 0 us
  local copies, waits for them, and re-layouts: 53.4 us -> 6.17 us
  Pallas kernels: 0 us -> 37 us
  other arithmetic: 18.8 us -> 0.83 us
  between operations: 14.1 us -> 0.72 us
    all_to_all x0 -> x4, blocking collectives: none -> 149 us  [the longest x1 48.8 us: on_device(): here = lax.all_to_all(sent, 'view', split_axis=0, concat_axis=0, tiled=True)]
    reduce_scatter x1 -> x0, waiting for transfers between devices: 131 us -> none  [on_device(): lax.psum_scatter(weight_term.astype(jnp.bfloat16), 'scene', scatter_dimen...]
    dot_general x53 -> x0, matrix products: 116 us -> none  [the longest x1 31.7 us: on_device(): jnp.einsum('wn,wnbc->wbc', select, all_views, preferred_element_type=jnp....]
    all_gather x1 -> x0, waiting for transfers between devices: 108 us -> none  [on_device(): all_views = lax.all_gather(paired, 'view', axis=0, tiled=True)]
    unnamed x4 -> x0, waiting for transfers between devices: 82.8 us -> none
    pallas_call x0 -> x3, Pallas kernels: none -> 37 us  [the longest x1 34 us: on_device(): pl.pallas_call(attn_kernel, out_shape=jax.ShapeDtypeStruct((VIEWS, BACK_R...]
    concatenate x4 -> x0, local copies, waits for them, and re-layouts: 15.1 us -> none  [the longest x1 6.69 us: on_device(): jnp.concatenate([grad_kall[tok_rows:], grad_vall[tok_rows:]], axis=1)]
    dot_general x2 -> x0, local copies, waits for them, and re-layouts: 13.9 us -> none  [the longest x1 12.6 us: on_device(): jnp.einsum('wn,wnbc->wbc', select, all_views, preferred_element_type=jnp....]
  transfers between devices with their start and end apart: 4 -> 0, of which waited for: 3 -> 0; matrix products, arithmetic and copies ran while one was open for 3% -> 0% of each run, Pallas kernels for 0% -> 0%
where the time goes in v1:
time: 197 us; the launch traced here: 193 us
  blocking collectives  149 us (76%)
  Pallas kernels  37 us (19%)
  local copies, waits for them, and re-layouts  6.17 us (3%)
    all_to_all x1, blocking collectives, on_device(): here = lax.all_to_all(sent, 'view', split_axis=0, concat_axis=0, tiled=True)  48.8 us
    all_to_all x1, blocking collectives, on_device(): home = lax.all_to_all(back, 'view', split_axis=0, concat_axis=0, tiled=True)  41.3 us
    pallas_call x1, Pallas kernels, on_device(): pl.pallas_call(attn_kernel, out_shape=jax.ShapeDtypeStruct((VIEWS, BACK_R...  34 us
    all_to_all x1, blocking collectives, on_device(): lax.all_to_all(terms, 'view', split_axis=0, concat_axis=0, tiled=True)  30.1 us
    all_to_all x1, blocking collectives, on_device(): lax.all_to_all(part, 'scene', split_axis=0, concat_axis=0, tiled=True)  28.3 us
    unnamed x20, local copies, waits for them, and re-layouts  6.08 us

profile of v1, /device:TPU:6, one launch (start us, length us, event | category | flops | bytes accessed | tf_op | source)
XLA Modules:
  0.0 193.2 jit_solution(15198655969543626226)
XLA Ops:
  0.6 0.0 copy-start
  0.6 1.2 copy-done
  1.9 1.0 copy-done.2
  2.9 0.9 copy-done.4
  3.9 0.9 copy-done.5
  4.8 0.9 copy-done.6
  5.8 0.7 copy-done.8
  6.4 0.5 shard_map.110
  7.0 0.0 copy-start.7
  7.0 48.8 %all_to_all.20.in_ref = bf16[16,400,128]{2,1,0:T(8,128)(2,1)S(1)} all-to-all(bf16[16,400,128]{2,1,0:T(8,128)(2,1)S(1)} %shard_map.110), channel_id=1, replica_groups=mesh['scene'=32,'view'=16] {'view'}, dimensions={0} | all-to-all | bytes 3276800 | tf_op jit(solution)/shard_map/all_to_all | solution.py:149
  55.8 0.0 copy-done.7
  55.8 34.0 %shard_map.111 = bf16[16,384,128]{2,1,0:T(8,128)(2,1)S(1)} custom-call(s32[16,16]{1,0:T(8,128)S(1)} %bitcast.18, s32[16,16]{1,0:T(8,128)S(1)} %bitcast.17, bf16[16,400,128]{2,1,0:T(8,128)(2,1)S(1)} %all_to_all.20.in_ref), custom_call_target="tpu_custom_call" | custom-call | tf_op jit(solution)/shard_map/pallas_call | solution.py:151
  89.8 0.0 copy-start.1
  89.8 0.0 copy-start.3
  89.8 41.3 %all_to_all.21.in_ref = bf16[16,384,128]{2,1,0:T(8,128)(2,1)S(1)} all-to-all(bf16[16,384,128]{2,1,0:T(8,128)(2,1)S(1)} %shard_map.111), channel_id=1, replica_groups=mesh['scene'=32,'view'=16] {'view'}, dimensions={0} | all-to-all | bytes 3145728 | tf_op jit(solution)/shard_map/all_to_all | solution.py:167
  131.1 0.0 copy-done.1
  131.1 2.4 %shard_map.112 = (bf16[256,1024]{1,0:T(8,128)(2,1)}, bf16[256,512]{1,0:T(8,128)(2,1)}, bf16[256,512]{1,0:T(8,128)(2,1)}, bf16[256,512]{1,0:T(8,128)(2,1)}, bf16[16,256,128]{2,1,0:T(8,128)(2,1)S(1)}) custom-call(bf16[16,384,128]{2,1,0:T(8,128)(2,1)S(1)} %all_to_all.21.in_ref, bf16[256,1024]{1,0:T(8,128)(2,1)S(1)} %bitcast.13, bf16[512,1024]{1,0:T(8,128)(2,1)S(1)} %copy-done.1), custom_call_target="tpu_custom_call" | custom-call | tf_op jit(solution)/shard_map/pallas_call | solution.py:168
  133.6 30.1 %all_to_all.22 = bf16[16,256,128]{2,1,0:T(8,128)(2,1)S(1)} all-to-all(bf16[16,256,128]{2,1,0:T(8,128)(2,1)S(1)} %get-tuple-element.14), channel_id=1, replica_groups=mesh['scene'=32,'view'=16] {'view'}, dimensions={0} | all-to-all | bytes 2097152 | tf_op jit(solution)/shard_map/all_to_all | solution.py:184
  163.6 0.1 reduce_sum.21
  163.8 0.1 fusion
  163.9 0.1 reshape.17
  164.0 28.3 %all_to_all.23 = bf16[32,2,512]{2,1,0:T(2,128)(2,1)S(1)} all-to-all(bf16[32,2,512]{2,1,0:T(2,128)(2,1)S(1)} %reshape.17), channel_id=1, replica_groups=mesh['scene'=32,'view'=16] {'scene'}, dimensions={0} | all-to-all | bytes 131072 | tf_op jit(solution)/shard_map/all_to_all | solution.py:188
  192.4 0.1 reshape.18
  192.6 0.6 broadcast_multiply_fusion
  (9 shorter events, 0.1 us)
Async XLA Ops:
  0.6 1.2 copy-start
  1.9 1.0 copy-start.2
  2.9 0.9 copy-start.4
  3.9 0.9 copy-start.5
  4.8 0.9 copy-start.6
  5.8 0.7 copy-start.8
  7.0 48.8 %copy-start.7 = (s32[1,16,16]{2,1,0:T(8,128)S(1)}, s32[1,16,16]{2,1,0:T(8,128)}, u32[]{:S(2)}) copy-start(s32[1,16,16]{2,1,0:T(8,128)} %param.12) | copy-start | bytes 3076
  89.8 41.3 %copy-start.1 = (bf16[512,1024]{1,0:T(8,128)(2,1)S(1)}, bf16[512,1024]{1,0:T(8,128)(2,1)}, u32[]{:S(2)}) copy-start(bf16[512,1024]{1,0:T(8,128)(2,1)} %w_ref.3) | copy-start | bytes 3145732
  89.8 41.3 %copy-start.3 = (bf16[1,1,256,1024]{3,2,1,0:T(8,128)(2,1)S(1)}, bf16[1,1,256,1024]{3,2,1,0:T(8,128)(2,1)}, u32[]{:S(2)}) copy-start(bf16[1,1,256,1024]{3,2,1,0:T(8,128)(2,1)} %param.10) | copy-start | bytes 1572868

commit v2 on v1

v2 whole, which is shorter than its diff:
```python
import jax
import jax.numpy as jnp
from jax import lax
from jax.experimental import pallas as pl
from jax.experimental.pallas import tpu as pltpu
from jax.sharding import PartitionSpec as P

HEADS = 8
HEAD_DIM = 64
BLK = 128
TOK = 256
VIEWS = 16
INNER = 512
D = 1024
KEYS = TOK + VIEWS * BLK
WIDE = 2 * HEAD_DIM
COLS = D // VIEWS
BF = jnp.bfloat16
F32 = jnp.float32
SCALE = HEAD_DIM ** (-0.5)
ROWS = TOK + BLK
PACK_ROWS = ROWS + 16
BACK_ROWS = TOK + BLK // 2
X, ZHI, CORES = 4, 4, 2
NT = (((1,), (1,)), ((), ()))
VMEM = pl.BlockSpec(memory_space=pltpu.VMEM)
SMEM = pl.BlockSpec(memory_space=pltpu.SMEM)


def pack_kernel(q_ref, k_ref, v_ref, go_ref, w_ref, mask_ref, out_ref):
    ga = lax.dot_general(go_ref[...], w_ref[...], NT, preferred_element_type=F32).astype(BF)
    q = q_ref[...] * jnp.asarray(SCALE, BF)
    for h in range(HEADS):
        c = slice(h * HEAD_DIM, (h + 1) * HEAD_DIM)
        kv = jnp.concatenate([k_ref[:, c], v_ref[:, c]], axis=1)
        qg = jnp.concatenate([q[:, c], ga[:, c]], axis=1)
        for p in range(2):
            j = 2 * h + p
            out_ref[j, 0:TOK, :] = kv
            out_ref[j, TOK:ROWS, :] = qg[p * BLK : (p + 1) * BLK, :]
            out_ref[j, ROWS:PACK_ROWS, 0:VIEWS] = jnp.broadcast_to(
                mask_ref[p : p + 1, :], (16, VIEWS)
            ).astype(BF)


def rows_of(v, w, fetch_ref):
    return pl.ds(pl.multiple_of(fetch_ref[v * VIEWS + w] * BLK, BLK), BLK)


def bias_of(v, w, mask_ref):
    seen = jnp.logical_and(mask_ref[v * VIEWS + w] == 1, w != v)
    return jnp.where(seen, 0.0, -jnp.inf)


def gather_cols(v, src, dst, fetch_ref):
    dst[:, 0:TOK] = src[:, pl.ds(pl.multiple_of(v * TOK, TOK), TOK)]
    for w in range(VIEWS):
        at = pl.multiple_of(w * TOK + fetch_ref[v * VIEWS + w] * BLK, BLK)
        dst[:, TOK + w * BLK : TOK + (w + 1) * BLK] = src[:, pl.ds(at, BLK)]


def side_by_side(t):
    half = BLK // 2
    return jnp.concatenate([t[:, :half], t[:, half:]], axis=0).T


def forward_kernel(
    fetch_ref, mask_ref, in_ref, attn_ref, stat_ref, vt, vsel, s_ref, e_ref
):
    lane = lax.broadcasted_iota(jnp.int32, (BLK, WIDE), 1)
    row = lax.broadcasted_iota(jnp.int32, (WIDE, TOK), 0)
    for w in range(VIEWS):
        t = in_ref[w, 0:TOK, :].T
        vt[:, w * TOK : (w + 1) * TOK] = jnp.where(row < HEAD_DIM, jnp.ones_like(t), t)

    def one_view(v, carry):
        qg = in_ref[v, TOK:ROWS, :]
        qs = jnp.where(lane < HEAD_DIM, qg, jnp.zeros_like(qg))
        gather_cols(v, vt, vsel, fetch_ref)
        top = None
        for c in range(KEYS // BLK):
            rows = slice(c * BLK, (c + 1) * BLK)
            if c < 2:
                keys = in_ref[v, rows, :]
            else:
                keys = in_ref[c - 2, rows_of(v, c - 2, fetch_ref), :]
            s = lax.dot_general(keys, qs, NT, preferred_element_type=F32)
            if c >= 2:
                s = s + bias_of(v, c - 2, mask_ref)
            s_ref[rows, :] = s
            best = jnp.max(s.reshape(BLK // 8, 8, BLK), axis=0)
            top = best if top is None else jnp.maximum(top, best)
        top = jnp.max(top, axis=0, keepdims=True)
        for c in range(KEYS // BLK):
            rows = slice(c * BLK, (c + 1) * BLK)
            e_ref[rows, :] = jnp.exp(s_ref[rows, :] - top).astype(BF)
        o = jnp.dot(vsel[...], e_ref[...], preferred_element_type=F32)
        share = 1.0 / o[0:1, :]
        attn = o[HEAD_DIM:, :] * share
        attn_ref[v, :, :] = side_by_side(attn).astype(BF)
        delta = jnp.sum(attn * qg.T[HEAD_DIM:, :].astype(F32), axis=0, keepdims=True)
        stat_ref[v, 0:1, :] = top
        stat_ref[v, 1:2, :] = share
        stat_ref[v, 2:3, :] = delta
        return carry

    lax.fori_loop(0, VIEWS, one_view, 0)


def backward_kernel(
    fetch_ref, mask_ref, in_ref, stat_ref, out_ref, kt, ksel, x_ref, acc
):
    lane = lax.broadcasted_iota(jnp.int32, (BLK, WIDE), 1)
    for w in range(VIEWS):
        kt[:, w * TOK : (w + 1) * TOK] = in_ref[w, 0:TOK, :].T[:HEAD_DIM, :]
        acc[w] = jnp.zeros((TOK, WIDE), F32)

    def one_view(v, carry):
        qg = in_ref[v, TOK:ROWS, :]
        zero = jnp.zeros_like(qg)
        qg2 = jnp.concatenate(
            [jnp.where(lane < HEAD_DIM, qg, zero), jnp.where(lane >= HEAD_DIM, qg, zero)], axis=0
        )
        gather_cols(v, kt, ksel, fetch_ref)
        top = stat_ref[v, 0:1, :]
        share = stat_ref[v, 1:2, :]
        delta = stat_ref[v, 2:3, :]
        for c in range(KEYS // BLK):
            rows = slice(c * BLK, (c + 1) * BLK)
            if c < 2:
                at = (v, rows)
            else:
                at = (c - 2, rows_of(v, c - 2, fetch_ref))
            r = lax.dot_general(in_ref[at[0], at[1], :], qg2, NT, preferred_element_type=F32)
            s = r[:, 0:BLK]
            if c >= 2:
                s = s + bias_of(v, c - 2, mask_ref)
            prob = jnp.exp(s - top) * share
            x = jnp.concatenate([prob * (r[:, BLK:] - delta), prob], axis=1).astype(BF)
            x_ref[rows, :] = x[:, 0:BLK]
            acc[at[0], at[1], :] += jnp.dot(x, qg2, preferred_element_type=F32)
        o = jnp.dot(ksel[...], x_ref[...], preferred_element_type=F32) * SCALE
        out_ref[v, TOK:BACK_ROWS, :] = side_by_side(o).astype(BF)
        return carry

    lax.fori_loop(0, VIEWS, one_view, 0)
    for w in range(VIEWS):
        out_ref[w, 0:TOK, :] = acc[w].astype(BF)


def project_kernel(core_ref, in_ref, go_ref, w_ref, layer_ref, mine_ref, other_ref, attn, term):
    half = BLK // 2
    for h in range(HEADS):
        c = slice(h * HEAD_DIM, (h + 1) * HEAD_DIM)
        for p in range(2):
            both = in_ref[2 * h + p]
            attn[p * BLK : p * BLK + half, c] = both[:, :HEAD_DIM]
            attn[p * BLK + half : (p + 1) * BLK, c] = both[:, HEAD_DIM:]
    layer_ref[...] = jnp.dot(attn[...], w_ref[...], preferred_element_type=F32).astype(BF)
    term[...] = lax.dot_general(
        attn[...], go_ref[...], (((0,), (0,)), ((), ())), preferred_element_type=F32
    ).astype(BF)
    core = core_ref[0]
    own = INNER // (X * ZHI * CORES)
    for x in range(X):
        for side, ref in ((core, mine_ref), (1 - core, other_ref)):
            for z in range(ZHI):
                at = pl.multiple_of((x * ZHI + z) * CORES * own + side * own, own)
                ref[x, z, :, :] = term[pl.ds(at, own), :]


def unpack_kernel(in_ref, gq_ref, gk_ref, gv_ref):
    half = BLK // 2
    for h in range(HEADS):
        c = slice(h * HEAD_DIM, (h + 1) * HEAD_DIM)
        kv = in_ref[2 * h, 0:TOK, :].astype(F32) + in_ref[2 * h + 1, 0:TOK, :].astype(F32)
        kv = kv.astype(BF)
        gk_ref[:, c] = kv[:, :HEAD_DIM]
        gv_ref[:, c] = kv[:, HEAD_DIM:]
        for p in range(2):
            both = in_ref[2 * h + p, TOK:BACK_ROWS, :]
            gq_ref[p * BLK : p * BLK + half, c] = both[:, :HEAD_DIM]
            gq_ref[p * BLK + half : (p + 1) * BLK, c] = both[:, HEAD_DIM:]


def shape(*dims, dtype=BF):
    return jax.ShapeDtypeStruct(dims, dtype)


def call(kernel, outs, args, smem=0, scratch=(), mib=32, flops=0):
    return pl.pallas_call(
        kernel,
        out_shape=outs,
        in_specs=[SMEM] * smem + [VMEM] * (len(args) - smem),
        out_specs=jax.tree.map(lambda _: VMEM, outs),
        scratch_shapes=[pltpu.VMEM(dims, dtype) for dims, dtype in scratch],
        compiler_params=pltpu.CompilerParams(vmem_limit_bytes=mib * 1024 * 1024),
        cost_estimate=pl.CostEstimate(flops=flops, bytes_accessed=4 << 20, transcendentals=0),
    )(*args)


def forward(fetch, reads, here):
    return call(
        forward_kernel,
        (shape(VIEWS, BLK // 2, WIDE), shape(VIEWS, 8, BLK, dtype=F32)),
        (fetch, reads, here),
        smem=2,
        scratch=[
            ((WIDE, VIEWS * TOK), BF),
            ((WIDE, KEYS), BF),
            ((KEYS, BLK), F32),
            ((KEYS, BLK), BF),
        ],
        flops=10**10,
    )


def backward(fetch, reads, here, stat):
    return call(
        backward_kernel,
        shape(VIEWS, BACK_ROWS, WIDE),
        (fetch, reads, here, stat),
        smem=2,
        scratch=[
            ((HEAD_DIM, VIEWS * TOK), BF),
            ((HEAD_DIM, KEYS), BF),
            ((KEYS, BLK), BF),
            ((VIEWS, TOK, WIDE), F32),
        ],
        flops=2 * 10**10,
    )


def swap(rows, axis):
    return lax.all_to_all(rows, axis, split_axis=0, concat_axis=0, tiled=True)


def ring_sum(pieces, scene, size, step):
    here = (scene // step) % size
    total = lax.dynamic_index_in_dim(pieces, here, 0, keepdims=False).astype(F32)
    scenes = X * ZHI * CORES
    for d in range(1, size):
        pairs = []
        for i in range(scenes):
            at = (i // step) % size
            pairs.append((i, i + ((at + d) % size - at) * step))
        send = lax.dynamic_index_in_dim(pieces, (here + d) % size, 0, keepdims=False)
        total = total + lax.ppermute(send, "scene", pairs).astype(F32)
    return total.astype(BF)


def on_device(query_rows, key_rows, value_rows, grad_out, out_weight, fetch_list, read_mask):
    go = grad_out[0, 0]
    scene = lax.axis_index("scene")
    fetch = fetch_list.reshape(VIEWS * VIEWS)
    sent = call(
        pack_kernel,
        shape(VIEWS, PACK_ROWS, WIDE),
        (query_rows[0, 0], key_rows[0, 0], value_rows[0, 0], go, out_weight, read_mask[0, 0]),
    )
    here = swap(sent, "view")
    reads = here[:, ROWS, :VIEWS].astype(jnp.int32).reshape(VIEWS * VIEWS)
    attn, stat = forward(fetch, reads, here)
    attn_home = swap(attn, "view")
    back = backward(fetch, reads, here, stat)
    attn_home, back = lax.optimization_barrier((attn_home, back))
    core = (scene % CORES).astype(jnp.int32)[None]
    own = INNER // (X * ZHI * CORES)
    piece = shape(X, ZHI, own, D)
    layer, mine, other = call(
        project_kernel,
        (shape(TOK, D), piece, piece),
        (core, attn_home, go, out_weight),
        smem=1,
        scratch=[((TOK, INNER), BF), ((INNER, D), BF)],
        flops=10**9,
    )
    home = swap(back, "view")
    scenes = X * ZHI * CORES
    other = lax.ppermute(other, "scene", [(i, i ^ 1) for i in range(scenes)])
    term = (mine.astype(F32) + other.astype(F32)).astype(BF)
    term = ring_sum(term, scene, X, ZHI * CORES)
    term = ring_sum(term, scene, ZHI, CORES)
    term, home = lax.optimization_barrier((term, home))
    term = swap(term.reshape(own, VIEWS, COLS).transpose(1, 0, 2), "view")
    share = jnp.sum(term.astype(F32), axis=0) * float(scenes * VIEWS * TOK) ** (-0.5)
    gq, gk, gv = call(unpack_kernel, (shape(TOK, INNER),) * 3, (home,))
    return (layer[None, None], gq[None, None], gk[None, None], gv[None, None], share)


def solution(mesh):
    rows = P("scene", "view", None, None)
    return jax.shard_map(
        on_device,
        mesh=mesh,
        in_specs=(rows, rows, rows, rows, P(), P("scene", None, None), rows),
        out_specs=(rows, rows, rows, rows, P("scene", "view")),
        check_vma=False,
    )
```

time: 197 us -> 178 us (0.904); the launches traced: 193 us -> 176 us
  blocking collectives: 149 us -> 0 us
  starting transfers between devices: 0 us -> 67.6 us
  waiting for transfers between devices: 0 us -> 51.7 us
  Pallas kernels: 37 us -> 47 us
    all_to_all x4 -> x0, blocking collectives: 149 us -> none  [the longest x1 48.8 us: on_device(): here = lax.all_to_all(sent, 'view', split_axis=0, concat_axis=0, tiled=True)]
    all_to_all x0 -> x4, waiting for transfers between devices: none -> 41.8 us  [swap(): return lax.all_to_all(rows, axis, split_axis=0, concat_axis=0, tiled=True)]
    ppermute x0 -> x7, starting transfers between devices: none -> 34.4 us  [the longest x6 32.5 us: ring_sum(): total = total + lax.ppermute(send, 'scene', pairs).astype(F32)]
    all_to_all x0 -> x4, starting transfers between devices: none -> 33.2 us  [swap(): return lax.all_to_all(rows, axis, split_axis=0, concat_axis=0, tiled=True)]
    pallas_call x3 -> x5, Pallas kernels: 37 us -> 47 us  [call(): pl.pallas_call(kernel, out_shape=outs, in_specs=[SMEM] * smem + [VMEM] *...]
    ppermute x0 -> x7, waiting for transfers between devices: none -> 9.93 us  [the longest x6 7.92 us: ring_sum(): total = total + lax.ppermute(send, 'scene', pairs).astype(F32)]
    unnamed x20 -> x24, local copies, waits for them, and re-layouts: 6.08 us -> 7.57 us
  transfers between devices with their start and end apart: 0 -> 11, of which waited for: 0 -> 7; matrix products, arithmetic and copies ran while one was open for 0% -> 0% of each run, Pallas kernels for 0% -> 14%
where the time goes in v2:
time: 178 us; the launch traced here: 176 us
  starting transfers between devices  67.6 us (38%)
  waiting for transfers between devices  51.7 us (29%)
  Pallas kernels  47 us (26%)
  local copies, waits for them, and re-layouts  7.91 us (4%)
    pallas_call x5, Pallas kernels, call(): pl.pallas_call(kernel, out_shape=outs, in_specs=[SMEM] * smem + [VMEM] *...  47 us
    all_to_all x4, waiting for transfers between devices, swap(): return lax.all_to_all(rows, axis, split_axis=0, concat_axis=0, tiled=True)  41.8 us
    all_to_all x4, starting transfers between devices, swap(): return lax.all_to_all(rows, axis, split_axis=0, concat_axis=0, tiled=True)  33.2 us
    ppermute x6, starting transfers between devices, ring_sum(): total = total + lax.ppermute(send, 'scene', pairs).astype(F32)  32.5 us
    ppermute x6, waiting for transfers between devices, ring_sum(): total = total + lax.ppermute(send, 'scene', pairs).astype(F32)  7.92 us
    unnamed x24, local copies, waits for them, and re-layouts  7.57 us
  transfers between devices with their start and end apart: 11, of which 7 were waited for; matrix products, arithmetic and copies ran while one was open for 0% of the time, Pallas kernels for 14%

profile of v2, /device:TPU:6, one launch (start us, length us, event | category | flops | bytes accessed | tf_op | source)
XLA Modules:
  0.0 176.3 jit_solution(7205190597181654730)
XLA Ops:
  0.6 1.2 copy-done
  6.4 1.8 shard_map.110
  8.2 8.8 %all-to-all-start = ((bf16[16,400,128]{2,1,0:T(8,128)(2,1)}), bf16[16,400,128]{2,1,0:T(8,128)(2,1)S(1)}, u32[]{:S(2)}, u32[]{:S(2)}) async-start(bf16[16,400,128]{2,1,0:T(8,128)(2,1)} %shard_map.110), calls=%async_computation | async-start | bytes 3276800 | tf_op jit(solution)/shard_map/all_to_all | solution.py:235
  17.1 34.9 %all-to-all-done.in_ref = bf16[16,400,128]{2,1,0:T(8,128)(2,1)S(1)} async-done(((bf16[16,400,128]{2,1,0:T(8,128)(2,1)}), bf16[16,400,128]{2,1,0:T(8,128)(2,1)S(1)}, u32[]{:S(2)}, u32[]{:S(2)}) %all-to-all-start) | async-done | bytes 1638432 | tf_op jit(solution)/shard_map/all_to_all | solution.py:235
  52.1 20.3 %shard_map.111 = (bf16[16,64,128]{2,1,0:T(8,128)(2,1)}, f32[16,8,128]{2,1,0:T(8,128)S(1)}) custom-call(s32[256]{0:T(256)S(1)} %reshape.24.fetch_ref, s32[256]{0:T(256)S(1)} %reshape.26.mask_ref, bf16[16,400,128]{2,1,0:T(8,128)(2,1)S(1)} %all-to-all-done.in_ref), custom_call_target="tpu_custom_call" | custom-call | flops 10000000000 | bytes 4194304 | tf_op jit(solution)/shard_map/pallas_call | solution.py:191
  72.5 8.5 %all-to-all-start.1 = ((bf16[16,64,128]{2,1,0:T(8,128)(2,1)}), bf16[16,64,128]{2,1,0:T(8,128)(2,1)S(1)}, u32[]{:S(2)}, u32[]{:S(2)}) async-start(bf16[16,64,128]{2,1,0:T(8,128)(2,1)} %get-tuple-element.17), calls=%async_computation.1 | async-start | bytes 524288 | tf_op jit(solution)/shard_map/all_to_all | solution.py:235
  81.0 21.9 %shard_map.112 = bf16[16,320,128]{2,1,0:T(8,128)(2,1)} custom-call(s32[256]{0:T(256)S(1)} %reshape.24.fetch_ref, s32[256]{0:T(256)S(1)} %reshape.26.mask_ref, bf16[16,400,128]{2,1,0:T(8,128)(2,1)S(1)} %all-to-all-done.in_ref, f32[16,8,128]{2,1,0:T(8,128)S(1)} %get-tuple-element.18.stat_ref), custom_call_target="tpu_custom_call" | custom-call | flops 20000000000 | bytes 4194304 | tf_op jit(solution)/shard_map/pallas_call | solution.py:191
  103.0 7.7 %all-to-all-start.2 = ((bf16[16,320,128]{2,1,0:T(8,128)(2,1)}), bf16[16,320,128]{2,1,0:T(8,128)(2,1)S(1)}, u32[]{:S(2)}, u32[]{:S(2)}) async-start(bf16[16,320,128]{2,1,0:T(8,128)(2,1)} %shard_map.112), calls=%async_computation.2 | async-start | bytes 2621440 | tf_op jit(solution)/shard_map/all_to_all | solution.py:235
  111.6 1.7 shard_map.113
  113.3 1.9 %collective-permute-start = (bf16[4,4,16,1024]{3,2,1,0:T(8,128)(2,1)}, bf16[4,4,16,1024]{3,2,1,0:T(8,128)(2,1)S(1)}, u32[]{:S(2)}, u32[]{:S(2)}) collective-permute-start(bf16[4,4,16,1024]{3,2,1,0:T(8,128)(2,1)} %get-tuple-element.22), channel_id=1, source_target_pairs={{0,16},{16,0},{32,48},{48,32},{64,80},{80,64},{96,112},{112,96},{1... | collective-permute-start | bytes 1572872 | tf_op jit(solution)/shard_map/ppermute | solution.py:280
  115.3 2.0 %collective-permute-done = bf16[4,4,16,1024]{3,2,1,0:T(8,128)(2,1)S(1)} collective-permute-done((bf16[4,4,16,1024]{3,2,1,0:T(8,128)(2,1)}, bf16[4,4,16,1024]{3,2,1,0:T(8,128)(2,1)S(1)}, u32[]{:S(2)}, u32[]{:S(2)}) %collective-permute-start) | collective-permute-done | bytes 524320 | tf_op jit(solution)/shard_map/ppermute | solution.py:280
  117.5 2.7 %collective-permute-start.3 = (bf16[4,16,1024]{2,1,0:T(8,128)(2,1)S(1)}, bf16[4,16,1024]{2,1,0:T(8,128)(2,1)S(1)}, u32[]{:S(2)}, u32[]{:S(2)}) collective-permute-start(bf16[4,16,1024]{2,1,0:T(8,128)(2,1)S(1)} %get-tuple-element.30), channel_id=1, source_target_pairs={{0,384},{16,400},{32,416},{48,432},{64,448},{80,464},{96,480},{112... | collective-permute-start | bytes 393224 | tf_op jit(solution)/shard_map/ppermute | solution.py:248
  120.3 3.0 %collective-permute-start.2 = (bf16[4,16,1024]{2,1,0:T(8,128)(2,1)S(1)}, bf16[4,16,1024]{2,1,0:T(8,128)(2,1)S(1)}, u32[]{:S(2)}, u32[]{:S(2)}) collective-permute-start(bf16[4,16,1024]{2,1,0:T(8,128)(2,1)S(1)} %get-tuple-element.31), channel_id=1, source_target_pairs={{0,256},{16,272},{32,288},{48,304},{64,320},{80,336},{96,352},{112... | collective-permute-start | bytes 393224 | tf_op jit(solution)/shard_map/ppermute | solution.py:248
  123.3 4.0 %collective-permute-start.1 = (bf16[4,16,1024]{2,1,0:T(8,128)(2,1)S(1)}, bf16[4,16,1024]{2,1,0:T(8,128)(2,1)S(1)}, u32[]{:S(2)}, u32[]{:S(2)}) collective-permute-start(bf16[4,16,1024]{2,1,0:T(8,128)(2,1)S(1)} %get-tuple-element.29), channel_id=1, source_target_pairs={{0,128},{16,144},{32,160},{48,176},{64,192},{80,208},{96,224},{112... | collective-permute-start | bytes 393224 | tf_op jit(solution)/shard_map/ppermute | solution.py:248
  127.4 1.6 collective-permute-done.2
  129.0 2.5 %collective-permute-done.1 = bf16[4,16,1024]{2,1,0:T(8,128)(2,1)S(1)} collective-permute-done((bf16[4,16,1024]{2,1,0:T(8,128)(2,1)S(1)}, bf16[4,16,1024]{2,1,0:T(8,128)(2,1)S(1)}, u32[]{:S(2)}, u32[]{:S(2)}) %collective-permute-start.1) | collective-permute-done | bytes 131104 | tf_op jit(solution)/shard_map/ppermute | solution.py:248
  131.6 10.1 %collective-permute-start.6 = (bf16[16,1024]{1,0:T(8,128)(2,1)S(1)}, bf16[16,1024]{1,0:T(8,128)(2,1)S(1)}, u32[]{:S(2)}, u32[]{:S(2)}) collective-permute-start(bf16[16,1024]{1,0:T(8,128)(2,1)S(1)} %get-tuple-element.33), channel_id=1, source_target_pairs={{0,96},{16,112},{32,0},{48,16},{64,32},{80,48},{96,64},{112,80},{1... | collective-permute-start | bytes 98312 | tf_op jit(solution)/shard_map/ppermute | solution.py:248
  141.7 6.3 %collective-permute-start.5 = (bf16[16,1024]{1,0:T(8,128)(2,1)S(1)}, bf16[16,1024]{1,0:T(8,128)(2,1)S(1)}, u32[]{:S(2)}, u32[]{:S(2)}) collective-permute-start(bf16[16,1024]{1,0:T(8,128)(2,1)S(1)} %get-tuple-element.34), channel_id=1, source_target_pairs={{0,64},{16,80},{32,96},{48,112},{64,0},{80,16},{96,32},{112,48},{1... | collective-permute-start | bytes 98312 | tf_op jit(solution)/shard_map/ppermute | solution.py:248
  148.0 6.4 %collective-permute-start.4 = (bf16[16,1024]{1,0:T(8,128)(2,1)S(1)}, bf16[16,1024]{1,0:T(8,128)(2,1)S(1)}, u32[]{:S(2)}, u32[]{:S(2)}) collective-permute-start(bf16[16,1024]{1,0:T(8,128)(2,1)S(1)} %get-tuple-element.32), channel_id=1, source_target_pairs={{0,32},{16,48},{32,64},{48,80},{64,96},{80,112},{96,0},{112,16},{1... | collective-permute-start | bytes 98312 | tf_op jit(solution)/shard_map/ppermute | solution.py:248
  154.4 2.2 %collective-permute-done.5 = bf16[16,1024]{1,0:T(8,128)(2,1)S(1)} collective-permute-done((bf16[16,1024]{1,0:T(8,128)(2,1)S(1)}, bf16[16,1024]{1,0:T(8,128)(2,1)S(1)}, u32[]{:S(2)}, u32[]{:S(2)}) %collective-permute-start.5) | collective-permute-done | bytes 32800 | tf_op jit(solution)/shard_map/ppermute | solution.py:248
  156.6 1.7 collective-permute-done.4
  159.1 8.2 %all-to-all-start.3 = ((bf16[16,2,512]{2,1,0:T(2,128)(2,1)}), bf16[16,2,512]{2,1,0:T(2,128)(2,1)S(1)}, u32[]{:S(2)}, u32[]{:S(2)}) async-start(bf16[16,2,512]{2,1,0:T(2,128)(2,1)} %reshape.36), calls=%async_computation.3 | async-start | bytes 65536 | tf_op jit(solution)/shard_map/all_to_all | solution.py:235
  167.4 1.3 shard_map.114
  168.7 6.8 %all-to-all-done.3 = bf16[16,2,512]{2,1,0:T(2,128)(2,1)S(1)} async-done(((bf16[16,2,512]{2,1,0:T(2,128)(2,1)}), bf16[16,2,512]{2,1,0:T(2,128)(2,1)S(1)}, u32[]{:S(2)}, u32[]{:S(2)}) %all-to-all-start.3) | async-done | bytes 32800 | tf_op jit(solution)/shard_map/all_to_all | solution.py:235
  (39 shorter events, 7.6 us)
Async XLA Ops:
  0.6 1.2 copy-start
  1.9 1.0 copy-start.2
  2.9 0.9 copy-start.4
  3.9 0.9 copy-start.5
  4.8 0.9 copy-start.6
  5.8 0.7 copy-start.9
  8.2 8.8 %copy-start.10 = (s32[1,16,16]{2,1,0:T(8,128)S(1)}, s32[1,16,16]{2,1,0:T(8,128)}, u32[]{:S(2)}) copy-start(s32[1,16,16]{2,1,0:T(8,128)} %param.12) | copy-start | bytes 3076
  8.2 43.8 %all-to-all-start = ((bf16[16,400,128]{2,1,0:T(8,128)(2,1)}), bf16[16,400,128]{2,1,0:T(8,128)(2,1)S(1)}, u32[]{:S(2)}, u32[]{:S(2)}) async-start(bf16[16,400,128]{2,1,0:T(8,128)(2,1)} %shard_map.110), calls=%async_computation | async-start | bytes 3276800 | tf_op jit(solution)/shard_map/all_to_all | solution.py:235
  72.5 30.5 %all-to-all-start.1 = ((bf16[16,64,128]{2,1,0:T(8,128)(2,1)}), bf16[16,64,128]{2,1,0:T(8,128)(2,1)S(1)}, u32[]{:S(2)}, u32[]{:S(2)}) async-start(bf16[16,64,128]{2,1,0:T(8,128)(2,1)} %get-tuple-element.17), calls=%async_computation.1 | async-start | bytes 524288 | tf_op jit(solution)/shard_map/all_to_all | solution.py:235
  102.9 7.7 %copy-start.1 = (bf16[512,1024]{1,0:T(8,128)(2,1)S(1)}, bf16[512,1024]{1,0:T(8,128)(2,1)}, u32[]{:S(2)}) copy-start(bf16[512,1024]{1,0:T(8,128)(2,1)} %w_ref.3) | copy-start | bytes 3145732
  102.9 7.7 %copy-start.3 = (bf16[1,1,256,1024]{3,2,1,0:T(8,128)(2,1)S(1)}, bf16[1,1,256,1024]{3,2,1,0:T(8,128)(2,1)}, u32[]{:S(2)}) copy-start(bf16[1,1,256,1024]{3,2,1,0:T(8,128)(2,1)} %param.10) | copy-start | bytes 1572868
  103.0 7.7 %copy-start.7 = (bf16[16,64,128]{2,1,0:T(8,128)(2,1)}, bf16[16,64,128]{2,1,0:T(8,128)(2,1)S(1)}, u32[]{:S(2)}) copy-start(bf16[16,64,128]{2,1,0:T(8,128)(2,1)S(1)} %all-to-all-done.1.in_ref) | copy-start | bytes 786436
  103.0 55.3 %all-to-all-start.2 = ((bf16[16,320,128]{2,1,0:T(8,128)(2,1)}), bf16[16,320,128]{2,1,0:T(8,128)(2,1)S(1)}, u32[]{:S(2)}, u32[]{:S(2)}) async-start(bf16[16,320,128]{2,1,0:T(8,128)(2,1)} %shard_map.112), calls=%async_computation.2 | async-start | bytes 2621440 | tf_op jit(solution)/shard_map/all_to_all | solution.py:235
  110.7 1.0 copy-start.8
  113.3 4.0 %collective-permute-start = (bf16[4,4,16,1024]{3,2,1,0:T(8,128)(2,1)}, bf16[4,4,16,1024]{3,2,1,0:T(8,128)(2,1)S(1)}, u32[]{:S(2)}, u32[]{:S(2)}) collective-permute-start(bf16[4,4,16,1024]{3,2,1,0:T(8,128)(2,1)} %get-tuple-element.22), channel_id=1, source_target_pairs={{0,16},{16,0},{32,48},{48,32},{64,80},{80,64},{96,112},{112,96},{1... | collective-permute-start | bytes 1572872 | tf_op jit(solution)/shard_map/ppermute | solution.py:280
  117.5 9.9 %collective-permute-start.3 = (bf16[4,16,1024]{2,1,0:T(8,128)(2,1)S(1)}, bf16[4,16,1024]{2,1,0:T(8,128)(2,1)S(1)}, u32[]{:S(2)}, u32[]{:S(2)}) collective-permute-start(bf16[4,16,1024]{2,1,0:T(8,128)(2,1)S(1)} %get-tuple-element.30), channel_id=1, source_target_pairs={{0,384},{16,400},{32,416},{48,432},{64,448},{80,464},{96,480},{112... | collective-permute-start | bytes 393224 | tf_op jit(solution)/shard_map/ppermute | solution.py:248
  120.3 8.7 %collective-permute-start.2 = (bf16[4,16,1024]{2,1,0:T(8,128)(2,1)S(1)}, bf16[4,16,1024]{2,1,0:T(8,128)(2,1)S(1)}, u32[]{:S(2)}, u32[]{:S(2)}) collective-permute-start(bf16[4,16,1024]{2,1,0:T(8,128)(2,1)S(1)} %get-tuple-element.31), channel_id=1, source_target_pairs={{0,256},{16,272},{32,288},{48,304},{64,320},{80,336},{96,352},{112... | collective-permute-start | bytes 393224 | tf_op jit(solution)/shard_map/ppermute | solution.py:248
  123.3 8.2 %collective-permute-start.1 = (bf16[4,16,1024]{2,1,0:T(8,128)(2,1)S(1)}, bf16[4,16,1024]{2,1,0:T(8,128)(2,1)S(1)}, u32[]{:S(2)}, u32[]{:S(2)}) collective-permute-start(bf16[4,16,1024]{2,1,0:T(8,128)(2,1)S(1)} %get-tuple-element.29), channel_id=1, source_target_pairs={{0,128},{16,144},{32,160},{48,176},{64,192},{80,208},{96,224},{112... | collective-permute-start | bytes 393224 | tf_op jit(solution)/shard_map/ppermute | solution.py:248
  131.6 22.8 %collective-permute-start.6 = (bf16[16,1024]{1,0:T(8,128)(2,1)S(1)}, bf16[16,1024]{1,0:T(8,128)(2,1)S(1)}, u32[]{:S(2)}, u32[]{:S(2)}) collective-permute-start(bf16[16,1024]{1,0:T(8,128)(2,1)S(1)} %get-tuple-element.33), channel_id=1, source_target_pairs={{0,96},{16,112},{32,0},{48,16},{64,32},{80,48},{96,64},{112,80},{1... | collective-permute-start | bytes 98312 | tf_op jit(solution)/shard_map/ppermute | solution.py:248
  141.7 14.9 %collective-permute-start.5 = (bf16[16,1024]{1,0:T(8,128)(2,1)S(1)}, bf16[16,1024]{1,0:T(8,128)(2,1)S(1)}, u32[]{:S(2)}, u32[]{:S(2)}) collective-permute-start(bf16[16,1024]{1,0:T(8,128)(2,1)S(1)} %get-tuple-element.34), channel_id=1, source_target_pairs={{0,64},{16,80},{32,96},{48,112},{64,0},{80,16},{96,32},{112,48},{1... | collective-permute-start | bytes 98312 | tf_op jit(solution)/shard_map/ppermute | solution.py:248
  148.0 10.3 %collective-permute-start.4 = (bf16[16,1024]{1,0:T(8,128)(2,1)S(1)}, bf16[16,1024]{1,0:T(8,128)(2,1)S(1)}, u32[]{:S(2)}, u32[]{:S(2)}) collective-permute-start(bf16[16,1024]{1,0:T(8,128)(2,1)S(1)} %get-tuple-element.32), channel_id=1, source_target_pairs={{0,32},{16,48},{32,64},{48,80},{64,96},{80,112},{96,0},{112,16},{1... | collective-permute-start | bytes 98312 | tf_op jit(solution)/shard_map/ppermute | solution.py:248
  159.1 16.4 %all-to-all-start.3 = ((bf16[16,2,512]{2,1,0:T(2,128)(2,1)}), bf16[16,2,512]{2,1,0:T(2,128)(2,1)S(1)}, u32[]{:S(2)}, u32[]{:S(2)}) async-start(bf16[16,2,512]{2,1,0:T(2,128)(2,1)} %reshape.36), calls=%async_computation.3 | async-start | bytes 65536 | tf_op jit(solution)/shard_map/all_to_all | solution.py:235

commit v3 on v2

v3 whole, which is shorter than its diff:
```python
import jax
import jax.numpy as jnp
from jax import lax
from jax.experimental import pallas as pl
from jax.experimental.pallas import tpu as pltpu
from jax.sharding import PartitionSpec as P

HEADS = 8
HEAD_DIM = 64
BLK = 128
TOK = 256
VIEWS = 16
INNER = 512
D = 1024
KEYS = TOK + VIEWS * BLK
WIDE = 2 * HEAD_DIM
COLS = D // VIEWS
BF = jnp.bfloat16
F32 = jnp.float32
SCALE = HEAD_DIM ** (-0.5)
ROWS = TOK + BLK
PACK_ROWS = ROWS + 16
CHUNK = 768
BACK_ROWS = TOK + BLK // 2
X, ZHI, CORES = 4, 4, 2
ZLO, Y = 4, 4
NT = (((1,), (1,)), ((), ()))
VMEM = pl.BlockSpec(memory_space=pltpu.VMEM)
SMEM = pl.BlockSpec(memory_space=pltpu.SMEM)


def pack_kernel(q_ref, k_ref, v_ref, go_ref, w_ref, mask_ref, out_ref):
    ga = lax.dot_general(go_ref[...], w_ref[...], NT, preferred_element_type=F32).astype(BF)
    q = q_ref[...] * jnp.asarray(SCALE, BF)
    for h in range(HEADS):
        c = slice(h * HEAD_DIM, (h + 1) * HEAD_DIM)
        kv = jnp.concatenate([k_ref[:, c], v_ref[:, c]], axis=1)
        qg = jnp.concatenate([q[:, c], ga[:, c]], axis=1)
        for p in range(2):
            j = 2 * h + p
            out_ref[j, 0:TOK, :] = kv
            out_ref[j, TOK:ROWS, :] = qg[p * BLK : (p + 1) * BLK, :]
            out_ref[j, ROWS:PACK_ROWS, 0:VIEWS] = jnp.broadcast_to(
                mask_ref[p : p + 1, :], (16, VIEWS)
            ).astype(BF)


def rows_of(v, w, fetch_ref):
    return pl.ds(pl.multiple_of(fetch_ref[v * VIEWS + w] * BLK, BLK), BLK)


def bias_of(v, w, mask_ref):
    seen = jnp.logical_and(mask_ref[v * VIEWS + w] == 1, w != v)
    return jnp.where(seen, 0.0, -jnp.inf)


def gather_cols(v, src, dst, dims, fetch_ref):
    dst[dims, 0:TOK] = src[:, pl.ds(pl.multiple_of(v * TOK, TOK), TOK)]
    for w in range(VIEWS):
        at = pl.multiple_of(w * TOK + fetch_ref[v * VIEWS + w] * BLK, BLK)
        dst[dims, TOK + w * BLK : TOK + (w + 1) * BLK] = src[:, pl.ds(at, BLK)]


def gather_rows(v, in_ref, dst, fetch_ref):
    dst[0:TOK, :] = in_ref[v, 0:TOK, :]
    for w in range(VIEWS):
        dst[TOK + w * BLK : TOK + (w + 1) * BLK, :] = in_ref[w, rows_of(v, w, fetch_ref), :]


def side_by_side(t):
    half = BLK // 2
    return jnp.concatenate([t[:, :half], t[:, half:]], axis=0).T


def forward_kernel(fetch_ref, mask_ref, in_ref, attn_ref, stat_ref, vt, vsel, s_ref, e_ref, top_ref, kall):
    lane = lax.broadcasted_iota(jnp.int32, (BLK, WIDE), 1)
    for w in range(VIEWS):
        vt[:, w * TOK : (w + 1) * TOK] = in_ref[w, 0:TOK, :].T[HEAD_DIM:, :]
    vsel[0:HEAD_DIM, :] = jnp.ones((HEAD_DIM, KEYS), BF)

    def scores(v, slot):
        qg = in_ref[v, TOK:ROWS, :]
        qs = jnp.where(lane < HEAD_DIM, qg, jnp.zeros_like(qg))
        gather_rows(v, in_ref, kall.at[slot], fetch_ref)
        top = None
        for c in range(0, KEYS, CHUNK):
            r = lax.dot_general(
                kall[slot, c : c + CHUNK, :], qs, NT, preferred_element_type=F32
            )
            for b in range(0, CHUNK, BLK):
                s = r[b : b + BLK, :]
                w = (c + b - TOK) // BLK
                if w >= 0:
                    s = s + bias_of(v, w, mask_ref)
                s_ref[slot, c + b : c + b + BLK, :] = s
                best = jnp.max(s.reshape(BLK // 8, 8, BLK), axis=0)
                top = best if top is None else jnp.maximum(top, best)
        top_ref[slot, 0:1, :] = jnp.max(top, axis=0, keepdims=True)

    def output(v, slot):
        qg = in_ref[v, TOK:ROWS, :]
        gather_cols(v, vt, vsel, slice(HEAD_DIM, WIDE), fetch_ref)
        top = top_ref[slot, 0:1, :]
        for c in range(KEYS // BLK):
            rows = slice(c * BLK, (c + 1) * BLK)
            e_ref[slot, rows, :] = jnp.exp(s_ref[slot, rows, :] - top).astype(BF)
        o = jnp.dot(vsel[...], e_ref[slot], preferred_element_type=F32)
        share = 1.0 / o[0:1, :]
        attn = o[HEAD_DIM:, :] * share
        attn_ref[v, :, :] = side_by_side(attn).astype(BF)
        delta = jnp.sum(attn * qg.T[HEAD_DIM:, :].astype(F32), axis=0, keepdims=True)
        stat_ref[v, 0:1, :] = top
        stat_ref[v, 1:2, :] = share
        stat_ref[v, 2:3, :] = delta

    def two_views(i, carry):
        v = 2 * i
        scores(v + 1, 1)
        output(v, 0)
        scores(jnp.minimum(v + 2, VIEWS - 1), 0)
        output(v + 1, 1)
        return carry

    scores(0, 0)
    lax.fori_loop(0, VIEWS // 2, two_views, 0)


def backward_kernel(
    fetch_ref, mask_ref, in_ref, stat_ref, out_ref, kt, ksel, x_ref, acc, kall, qg2_ref
):
    lane = lax.broadcasted_iota(jnp.int32, (BLK, WIDE), 1)
    for w in range(VIEWS):
        kt[:, w * TOK : (w + 1) * TOK] = in_ref[w, 0:TOK, :].T[:HEAD_DIM, :]
        acc[w] = jnp.zeros((TOK, WIDE), F32)

    def weights(v, slot):
        qg = in_ref[v, TOK:ROWS, :]
        zero = jnp.zeros_like(qg)
        qg2_ref[slot, 0:BLK, :] = jnp.where(lane < HEAD_DIM, qg, zero)
        qg2_ref[slot, BLK:, :] = jnp.where(lane >= HEAD_DIM, qg, zero)
        qg2 = qg2_ref[slot]
        top = stat_ref[v, 0:1, :]
        share = stat_ref[v, 1:2, :]
        delta = stat_ref[v, 2:3, :]
        gather_rows(v, in_ref, kall.at[slot], fetch_ref)
        for c in range(0, KEYS, 768):
            r = lax.dot_general(
                kall[slot, c : c + 768, :], qg2, NT, preferred_element_type=F32
            )
            for b in range(0, 768, BLK):
                rows = slice(c + b, c + b + BLK)
                s = r[b : b + BLK, 0:BLK]
                w = (c + b - TOK) // BLK
                if w >= 0:
                    s = s + bias_of(v, w, mask_ref)
                prob = jnp.exp(s - top) * share
                x_ref[slot, rows, 0:BLK] = (prob * (r[b : b + BLK, BLK:] - delta)).astype(BF)
                x_ref[slot, rows, BLK:] = prob.astype(BF)

    def sums(v, slot):
        for c in range(0, KEYS, 768):
            g = jnp.dot(x_ref[slot, c : c + 768, :], qg2_ref[slot], preferred_element_type=F32)
            for b in range(0, 768, BLK):
                w = (c + b - TOK) // BLK
                if w >= 0:
                    acc[w, rows_of(v, w, fetch_ref), :] += g[b : b + BLK, :]
                else:
                    acc[v, c + b : c + b + BLK, :] += g[b : b + BLK, :]
        gather_cols(v, kt, ksel, slice(0, HEAD_DIM), fetch_ref)
        o = jnp.dot(ksel[...], x_ref[slot, :, 0:BLK], preferred_element_type=F32) * SCALE
        out_ref[v, TOK:BACK_ROWS, :] = side_by_side(o).astype(BF)

    def two_views(i, carry):
        v = 2 * i
        weights(v + 1, 1)
        sums(v, 0)
        weights(jnp.minimum(v + 2, VIEWS - 1), 0)
        sums(v + 1, 1)
        return carry

    weights(0, 0)
    lax.fori_loop(0, VIEWS // 2, two_views, 0)
    for w in range(VIEWS):
        out_ref[w, 0:TOK, :] = acc[w].astype(BF)


def project_kernel(core_ref, in_ref, go_ref, w_ref, layer_ref, mine_ref, other_ref, attn, term):
    half = BLK // 2
    for h in range(HEADS):
        c = slice(h * HEAD_DIM, (h + 1) * HEAD_DIM)
        for p in range(2):
            both = in_ref[2 * h + p]
            attn[p * BLK : p * BLK + half, c] = both[:, :HEAD_DIM]
            attn[p * BLK + half : (p + 1) * BLK, c] = both[:, HEAD_DIM:]
    layer_ref[...] = jnp.dot(attn[...], w_ref[...], preferred_element_type=F32).astype(BF)
    cols = [(z * Y + y) * COLS for y in range(Y) for z in range(ZLO)]
    go = jnp.concatenate([go_ref[:, c : c + COLS] for c in cols], axis=1)
    term[...] = lax.dot_general(
        attn[...], go, (((0,), (0,)), ((), ())), preferred_element_type=F32
    ).astype(BF)
    core = core_ref[0]
    own = INNER // (X * ZHI * CORES)
    wide = ZLO * COLS
    for x in range(X):
        for side, ref in ((core, mine_ref), (1 - core, other_ref)):
            for z in range(ZHI):
                at = pl.multiple_of((x * ZHI + z) * CORES * own + side * own, own)
                rows = term[pl.ds(at, own), :]
                for y in range(Y):
                    ref[x, y, z, :, :] = rows[:, y * wide : (y + 1) * wide]


def unpack_kernel(in_ref, gq_ref, gk_ref, gv_ref):
    half = BLK // 2
    for h in range(HEADS):
        c = slice(h * HEAD_DIM, (h + 1) * HEAD_DIM)
        kv = in_ref[2 * h, 0:TOK, :].astype(F32) + in_ref[2 * h + 1, 0:TOK, :].astype(F32)
        kv = kv.astype(BF)
        gk_ref[:, c] = kv[:, :HEAD_DIM]
        gv_ref[:, c] = kv[:, HEAD_DIM:]
        for p in range(2):
            both = in_ref[2 * h + p, TOK:BACK_ROWS, :]
            gq_ref[p * BLK : p * BLK + half, c] = both[:, :HEAD_DIM]
            gq_ref[p * BLK + half : (p + 1) * BLK, c] = both[:, HEAD_DIM:]


def shape(*dims, dtype=BF):
    return jax.ShapeDtypeStruct(dims, dtype)


def call(kernel, outs, args, smem=0, scratch=(), mib=32, flops=0):
    return pl.pallas_call(
        kernel,
        out_shape=outs,
        in_specs=[SMEM] * smem + [VMEM] * (len(args) - smem),
        out_specs=jax.tree.map(lambda _: VMEM, outs),
        scratch_shapes=[pltpu.VMEM(dims, dtype) for dims, dtype in scratch],
        compiler_params=pltpu.CompilerParams(vmem_limit_bytes=mib * 1024 * 1024),
        cost_estimate=pl.CostEstimate(flops=flops, bytes_accessed=4 << 20, transcendentals=0),
    )(*args)


def forward(fetch, reads, here):
    return call(
        forward_kernel,
        (shape(VIEWS, BLK // 2, WIDE), shape(VIEWS, 8, BLK, dtype=F32)),
        (fetch, reads, here),
        smem=2,
        scratch=[
            ((HEAD_DIM, VIEWS * TOK), BF),
            ((WIDE, KEYS), BF),
            ((2, KEYS, BLK), F32),
            ((2, KEYS, BLK), BF),
            ((2, 8, BLK), F32),
            ((2, KEYS, WIDE), BF),
        ],
        flops=10**10,
    )


def backward(fetch, reads, here, stat):
    return call(
        backward_kernel,
        shape(VIEWS, BACK_ROWS, WIDE),
        (fetch, reads, here, stat),
        smem=2,
        scratch=[
            ((HEAD_DIM, VIEWS * TOK), BF),
            ((HEAD_DIM, KEYS), BF),
            ((2, KEYS, 2 * BLK), BF),
            ((VIEWS, TOK, WIDE), F32),
            ((2, KEYS, WIDE), BF),
            ((2, 2 * BLK, WIDE), BF),
        ],
        flops=2 * 10**10,
    )


def swap(rows, axis):
    return lax.all_to_all(rows, axis, split_axis=0, concat_axis=0, tiled=True)


def ring_sum(pieces, axis, count, size, step):
    here = (lax.axis_index(axis) // step) % size
    total = lax.dynamic_index_in_dim(pieces, here, 0, keepdims=False).astype(F32)
    for d in range(1, size):
        pairs = []
        for i in range(count):
            at = (i // step) % size
            pairs.append((i, i + ((at + d) % size - at) * step))
        send = lax.dynamic_index_in_dim(pieces, (here + d) % size, 0, keepdims=False)
        total = total + lax.ppermute(send, axis, pairs).astype(F32)
    return total


def on_device(query_rows, key_rows, value_rows, grad_out, out_weight, fetch_list, read_mask):
    go = grad_out[0, 0]
    fetch = fetch_list.reshape(VIEWS * VIEWS)
    sent = call(
        pack_kernel,
        shape(VIEWS, PACK_ROWS, WIDE),
        (query_rows[0, 0], key_rows[0, 0], value_rows[0, 0], go, out_weight, read_mask[0, 0]),
        mib=60,
    )
    here = swap(sent, "view")
    reads = here[:, ROWS, :VIEWS].astype(jnp.int32).reshape(VIEWS * VIEWS)
    attn, stat = forward(fetch, reads, here)
    attn_home = swap(attn, "view")
    back = backward(fetch, reads, here, stat)
    attn_home, back = lax.optimization_barrier((attn_home, back))
    core = (lax.axis_index("scene") % CORES).astype(jnp.int32)[None]
    own = INNER // (X * ZHI * CORES)
    piece = shape(X, Y, ZHI, own, ZLO * COLS)
    layer, mine, other = call(
        project_kernel,
        (shape(TOK, D), piece, piece),
        (core, attn_home, go, out_weight),
        smem=1,
        scratch=[((TOK, INNER), BF), ((INNER, D), BF)],
        flops=10**9,
    )
    home = swap(back, "view")
    scenes = X * ZHI * CORES
    other = lax.ppermute(other, "scene", [(i, i ^ 1) for i in range(scenes)])
    term = (mine.astype(F32) + other.astype(F32)).astype(BF)
    term = ring_sum(term, "scene", scenes, X, ZHI * CORES).astype(BF)
    term = ring_sum(term, "view", VIEWS, Y, 1).astype(BF)
    term = ring_sum(term, "scene", scenes, ZHI, CORES).astype(BF)
    term = term.reshape(own, ZLO, COLS).transpose(1, 0, 2)
    share = ring_sum(term, "view", VIEWS, ZLO, Y) * float(scenes * VIEWS * TOK) ** (-0.5)
    gq, gk, gv = call(unpack_kernel, (shape(TOK, INNER),) * 3, (home,))
    return (layer[None, None], gq[None, None], gk[None, None], gv[None, None], share)


def solution(mesh):
    rows = P("scene", "view", None, None)
    return jax.shard_map(
        on_device,
        mesh=mesh,
        in_specs=(rows, rows, rows, rows, P(), P("scene", None, None), rows),
        out_specs=(rows, rows, rows, rows, P("scene", "view")),
        check_vma=False,
    )
```

time: 178 us -> 174 us (0.978)
  starting transfers between devices: 67.6 us -> 80.4 us
  Pallas kernels: 47 us -> 36.4 us
  local copies, waits for them, and re-layouts: 7.91 us -> 1.33 us
    ppermute x6 -> x12, starting transfers between devices: 32.5 us -> 53.6 us  [ring_sum(): total = total + lax.ppermute(send, axis, pairs).astype(F32)]
    pallas_call x5, Pallas kernels: 47 us -> 36.4 us  [call(): pl.pallas_call(kernel, out_shape=outs, in_specs=[SMEM] * smem + [VMEM] *...]
    all_to_all x4 -> x3, starting transfers between devices: 33.2 us -> 24.9 us  [swap(): return lax.all_to_all(rows, axis, split_axis=0, concat_axis=0, tiled=True)]
    ppermute x6 -> x12, waiting for transfers between devices: 7.92 us -> 14.8 us  [ring_sum(): total = total + lax.ppermute(send, axis, pairs).astype(F32)]
    all_to_all x4 -> x3, waiting for transfers between devices: 41.8 us -> 34.9 us  [swap(): return lax.all_to_all(rows, axis, split_axis=0, concat_axis=0, tiled=True)]
    unnamed x24 -> x13, local copies, waits for them, and re-layouts: 7.57 us -> 0.97 us
  transfers between devices with their start and end apart: 11 -> 16, of which waited for: 7 -> 8; matrix products, arithmetic and copies ran while one was open for 0% -> 1% of each run, Pallas kernels for 14% -> 11%
where the time goes in v3:
time: 174 us; the launch traced here: 172 us
  starting transfers between devices  80.4 us (46%)
  waiting for transfers between devices  51.7 us (30%)
  Pallas kernels  36.4 us (21%)
    ppermute x12, starting transfers between devices, ring_sum(): total = total + lax.ppermute(send, axis, pairs).astype(F32)  53.6 us
    pallas_call x5, Pallas kernels, call(): pl.pallas_call(kernel, out_shape=outs, in_specs=[SMEM] * smem + [VMEM] *...  36.4 us
    all_to_all x3, waiting for transfers between devices, swap(): return lax.all_to_all(rows, axis, split_axis=0, concat_axis=0, tiled=True)  34.9 us
    all_to_all x3, starting transfers between devices, swap(): return lax.all_to_all(rows, axis, split_axis=0, concat_axis=0, tiled=True)  24.9 us
    ppermute x12, waiting for transfers between devices, ring_sum(): total = total + lax.ppermute(send, axis, pairs).astype(F32)  14.8 us
  transfers between devices with their start and end apart: 16, of which 8 were waited for; matrix products, arithmetic and copies ran while one was open for 1% of the time, Pallas kernels for 11%

profile of v3, /device:TPU:6, one launch (start us, length us, event | category | flops | bytes accessed | tf_op | source)
XLA Modules:
  0.0 172.1 jit_solution(1375522430669314189)
XLA Ops:
  0.6 3.4 %shard_map.110 = bf16[16,400,128]{2,1,0:T(8,128)(2,1)} custom-call(bf16[256,512]{1,0:T(8,128)(2,1)} %bitcast.53, bf16[256,512]{1,0:T(8,128)(2,1)} %bitcast.54, bf16[256,512]{1,0:T(8,128)(2,1)} %bitcast.55, bf16[256,1024]{1,0:T(8,128)(2,1)} %bitcast.51, bf16[512,1024]{1,0:T(8,128)(2,1)} %w_ref.3, s32[2,16]{1,0:T(2,128)} %bitcast.59), custom_call_target="tpu_custom_call" | custom-call | bytes 4194304 | tf_op jit(solution)/shard_map/pallas_call | solution.py:232
  4.0 8.8 %all-to-all-start = ((bf16[16,400,128]{2,1,0:T(8,128)(2,1)}), bf16[16,400,128]{2,1,0:T(8,128)(2,1)S(1)}, u32[]{:S(2)}, u32[]{:S(2)}) async-start(bf16[16,400,128]{2,1,0:T(8,128)(2,1)} %shard_map.110), calls=%async_computation | async-start | bytes 3276800 | tf_op jit(solution)/shard_map/all_to_all | solution.py:280
  12.9 34.9 %all-to-all-done.in_ref = bf16[16,400,128]{2,1,0:T(8,128)(2,1)S(1)} async-done(((bf16[16,400,128]{2,1,0:T(8,128)(2,1)}), bf16[16,400,128]{2,1,0:T(8,128)(2,1)S(1)}, u32[]{:S(2)}, u32[]{:S(2)}) %all-to-all-start) | async-done | bytes 1638432 | tf_op jit(solution)/shard_map/all_to_all | solution.py:280
  47.9 12.3 %shard_map.111 = (bf16[16,64,128]{2,1,0:T(8,128)(2,1)}, f32[16,8,128]{2,1,0:T(8,128)S(1)}) custom-call(s32[256]{0:T(256)S(1)} %reshape.36.fetch_ref, s32[256]{0:T(256)S(1)} %reshape.38.mask_ref, bf16[16,400,128]{2,1,0:T(8,128)(2,1)S(1)} %all-to-all-done.in_ref), custom_call_target="tpu_custom_call" | custom-call | flops 10000000000 | bytes 4194304 | tf_op jit(solution)/shard_map/pallas_call | solution.py:232
  60.3 8.5 %all-to-all-start.1 = ((bf16[16,64,128]{2,1,0:T(8,128)(2,1)}), bf16[16,64,128]{2,1,0:T(8,128)(2,1)S(1)}, u32[]{:S(2)}, u32[]{:S(2)}) async-start(bf16[16,64,128]{2,1,0:T(8,128)(2,1)} %get-tuple-element.15), calls=%async_computation.1 | async-start | bytes 524288 | tf_op jit(solution)/shard_map/all_to_all | solution.py:280
  68.8 17.7 %shard_map.112 = bf16[16,320,128]{2,1,0:T(8,128)(2,1)} custom-call(s32[256]{0:T(256)S(1)} %reshape.36.fetch_ref, s32[256]{0:T(256)S(1)} %reshape.38.mask_ref, bf16[16,400,128]{2,1,0:T(8,128)(2,1)S(1)} %all-to-all-done.in_ref, f32[16,8,128]{2,1,0:T(8,128)S(1)} %get-tuple-element.16.stat_ref), custom_call_target="tpu_custom_call" | custom-call | flops 20000000000 | bytes 4194304 | tf_op jit(solution)/shard_map/pallas_call | solution.py:232
  86.5 7.7 %all-to-all-start.2 = ((bf16[16,320,128]{2,1,0:T(8,128)(2,1)}), bf16[16,320,128]{2,1,0:T(8,128)(2,1)S(1)}, u32[]{:S(2)}, u32[]{:S(2)}) async-start(bf16[16,320,128]{2,1,0:T(8,128)(2,1)} %shard_map.112), calls=%async_computation.2 | async-start | bytes 2621440 | tf_op jit(solution)/shard_map/all_to_all | solution.py:280
  98.8 2.0 %collective-permute-done = bf16[4,4,4,16,256]{4,3,2,1,0:T(8,128)(2,1)S(1)} collective-permute-done((bf16[4,4,4,16,256]{4,3,2,1,0:T(8,128)(2,1)}, bf16[4,4,4,16,256]{4,3,2,1,0:T(8,128)(2,1)S(1)}, u32[]{:S(2)}, u32[]{:S(2)}) %collective-permute-start) | collective-permute-done | bytes 524320 | tf_op jit(solution)/shard_map/ppermute | solution.py:324
  101.1 2.3 %collective-permute-start.1 = (bf16[4,4,16,256]{3,2,1,0:T(8,128)(2,1)S(1)}, bf16[4,4,16,256]{3,2,1,0:T(8,128)(2,1)S(1)}, u32[]{:S(2)}, u32[]{:S(2)}) collective-permute-start(bf16[4,4,16,256]{3,2,1,0:T(8,128)(2,1)S(1)} %get-tuple-element.25), channel_id=1, source_target_pairs={{0,128},{16,144},{32,160},{48,176},{64,192},{80,208},{96,224},{112... | collective-permute-start | bytes 393224 | tf_op jit(solution)/shard_map/ppermute | solution.py:292
  103.4 3.5 %collective-permute-start.3 = (bf16[4,4,16,256]{3,2,1,0:T(8,128)(2,1)S(1)}, bf16[4,4,16,256]{3,2,1,0:T(8,128)(2,1)S(1)}, u32[]{:S(2)}, u32[]{:S(2)}) collective-permute-start(bf16[4,4,16,256]{3,2,1,0:T(8,128)(2,1)S(1)} %get-tuple-element.26), channel_id=1, source_target_pairs={{0,384},{16,400},{32,416},{48,432},{64,448},{80,464},{96,480},{112... | collective-permute-start | bytes 393224 | tf_op jit(solution)/shard_map/ppermute | solution.py:292
  106.9 3.3 %collective-permute-start.2 = (bf16[4,4,16,256]{3,2,1,0:T(8,128)(2,1)S(1)}, bf16[4,4,16,256]{3,2,1,0:T(8,128)(2,1)S(1)}, u32[]{:S(2)}, u32[]{:S(2)}) collective-permute-start(bf16[4,4,16,256]{3,2,1,0:T(8,128)(2,1)S(1)} %get-tuple-element.27), channel_id=1, source_target_pairs={{0,256},{16,272},{32,288},{48,304},{64,320},{80,336},{96,352},{112... | collective-permute-start | bytes 393224 | tf_op jit(solution)/shard_map/ppermute | solution.py:292
  111.8 3.5 %collective-permute-done.2 = bf16[4,4,16,256]{3,2,1,0:T(8,128)(2,1)S(1)} collective-permute-done((bf16[4,4,16,256]{3,2,1,0:T(8,128)(2,1)S(1)}, bf16[4,4,16,256]{3,2,1,0:T(8,128)(2,1)S(1)}, u32[]{:S(2)}, u32[]{:S(2)}) %collective-permute-start.2) | collective-permute-done | bytes 131104 | tf_op jit(solution)/shard_map/ppermute | solution.py:292
  115.4 3.8 %collective-permute-start.4 = (bf16[4,16,256]{2,1,0:T(8,128)(2,1)S(1)}, bf16[4,16,256]{2,1,0:T(8,128)(2,1)S(1)}, u32[]{:S(2)}, u32[]{:S(2)}) collective-permute-start(bf16[4,16,256]{2,1,0:T(8,128)(2,1)S(1)} %get-tuple-element.28), channel_id=1, source_target_pairs={{0,1},{1,2},{2,3},{3,0},{4,5},{5,6},{6,7},{7,4},{8,9},{9,10},{10,1... | collective-permute-start | bytes 98312 | tf_op jit(solution)/shard_map/ppermute | solution.py:292
  119.2 3.2 %collective-permute-start.6 = (bf16[4,16,256]{2,1,0:T(8,128)(2,1)S(1)}, bf16[4,16,256]{2,1,0:T(8,128)(2,1)S(1)}, u32[]{:S(2)}, u32[]{:S(2)}) collective-permute-start(bf16[4,16,256]{2,1,0:T(8,128)(2,1)S(1)} %get-tuple-element.29), channel_id=1, source_target_pairs={{0,3},{1,0},{2,1},{3,2},{4,7},{5,4},{6,5},{7,6},{8,11},{9,8},{10,9... | collective-permute-start | bytes 98312 | tf_op jit(solution)/shard_map/ppermute | solution.py:292
  122.5 4.1 %collective-permute-start.5 = (bf16[4,16,256]{2,1,0:T(8,128)(2,1)S(1)}, bf16[4,16,256]{2,1,0:T(8,128)(2,1)S(1)}, u32[]{:S(2)}, u32[]{:S(2)}) collective-permute-start(bf16[4,16,256]{2,1,0:T(8,128)(2,1)S(1)} %get-tuple-element.30), channel_id=1, source_target_pairs={{0,2},{1,3},{2,0},{3,1},{4,6},{5,7},{6,4},{7,5},{8,10},{9,11},{10,... | collective-permute-start | bytes 98312 | tf_op jit(solution)/shard_map/ppermute | solution.py:292
  126.7 3.1 %collective-permute-done.5 = bf16[4,16,256]{2,1,0:T(8,128)(2,1)S(1)} collective-permute-done((bf16[4,16,256]{2,1,0:T(8,128)(2,1)S(1)}, bf16[4,16,256]{2,1,0:T(8,128)(2,1)S(1)}, u32[]{:S(2)}, u32[]{:S(2)}) %collective-permute-start.5) | collective-permute-done | bytes 32800 | tf_op jit(solution)/shard_map/ppermute | solution.py:292
  129.8 9.1 %collective-permute-start.7 = (bf16[16,256]{1,0:T(8,128)(2,1)S(1)}, bf16[16,256]{1,0:T(8,128)(2,1)S(1)}, u32[]{:S(2)}, u32[]{:S(2)}) collective-permute-start(bf16[16,256]{1,0:T(8,128)(2,1)S(1)} %get-tuple-element.31), channel_id=1, source_target_pairs={{0,32},{16,48},{32,64},{48,80},{64,96},{80,112},{96,0},{112,16},{1... | collective-permute-start | bytes 24584 | tf_op jit(solution)/shard_map/ppermute | solution.py:292
  138.9 2.9 %collective-permute-start.9 = (bf16[16,256]{1,0:T(8,128)(2,1)S(1)}, bf16[16,256]{1,0:T(8,128)(2,1)S(1)}, u32[]{:S(2)}, u32[]{:S(2)}) collective-permute-start(bf16[16,256]{1,0:T(8,128)(2,1)S(1)} %get-tuple-element.32), channel_id=1, source_target_pairs={{0,96},{16,112},{32,0},{48,16},{64,32},{80,48},{96,64},{112,80},{1... | collective-permute-start | bytes 24584 | tf_op jit(solution)/shard_map/ppermute | solution.py:292
  141.8 10.8 %collective-permute-start.8 = (bf16[16,256]{1,0:T(8,128)(2,1)S(1)}, bf16[16,256]{1,0:T(8,128)(2,1)S(1)}, u32[]{:S(2)}, u32[]{:S(2)}) collective-permute-start(bf16[16,256]{1,0:T(8,128)(2,1)S(1)} %get-tuple-element.33), channel_id=1, source_target_pairs={{0,64},{16,80},{32,96},{48,112},{64,0},{80,16},{96,32},{112,48},{1... | collective-permute-start | bytes 24584 | tf_op jit(solution)/shard_map/ppermute | solution.py:292
  152.7 3.3 %collective-permute-done.8 = bf16[16,256]{1,0:T(8,128)(2,1)S(1)} collective-permute-done((bf16[16,256]{1,0:T(8,128)(2,1)S(1)}, bf16[16,256]{1,0:T(8,128)(2,1)S(1)}, u32[]{:S(2)}, u32[]{:S(2)}) %collective-permute-start.8) | collective-permute-done | bytes 8224 | tf_op jit(solution)/shard_map/ppermute | solution.py:292
  156.2 5.6 %collective-permute-start.12 = (bf16[16,64]{1,0:T(8,128)(2,1)S(1)}, bf16[16,64]{1,0:T(8,128)(2,1)S(1)}, u32[]{:S(2)}, u32[]{:S(2)}) collective-permute-start(bf16[16,64]{1,0:T(8,128)(2,1)S(1)} %bitcast.58), channel_id=1, source_target_pairs={{0,12},{1,13},{2,14},{3,15},{4,0},{5,1},{6,2},{7,3},{8,4},{9,5},{1... | collective-permute-start | bytes 6152 | tf_op jit(solution)/shard_map/ppermute | solution.py:292
  161.8 1.9 %collective-permute-start.10 = (bf16[16,64]{1,0:T(8,128)(2,1)S(1)}, bf16[16,64]{1,0:T(8,128)(2,1)S(1)}, u32[]{:S(2)}, u32[]{:S(2)}) collective-permute-start(bf16[16,64]{1,0:T(8,128)(2,1)S(1)} %bitcast.57), channel_id=1, source_target_pairs={{0,4},{1,5},{2,6},{3,7},{4,8},{5,9},{6,10},{7,11},{8,12},{9,13},{1... | collective-permute-start | bytes 6152 | tf_op jit(solution)/shard_map/ppermute | solution.py:292
  163.8 3.0 %collective-permute-start.11 = (bf16[16,64]{1,0:T(8,128)(2,1)S(1)}, bf16[16,64]{1,0:T(8,128)(2,1)S(1)}, u32[]{:S(2)}, u32[]{:S(2)}) collective-permute-start(bf16[16,64]{1,0:T(8,128)(2,1)S(1)} %bitcast.56), channel_id=1, source_target_pairs={{0,8},{1,9},{2,10},{3,11},{4,12},{5,13},{6,14},{7,15},{8,0},{9,1},... | collective-permute-start | bytes 6152 | tf_op jit(solution)/shard_map/ppermute | solution.py:292
  166.8 2.3 %collective-permute-done.10 = bf16[16,64]{1,0:T(8,128)(2,1)S(1)} collective-permute-done((bf16[16,64]{1,0:T(8,128)(2,1)S(1)}, bf16[16,64]{1,0:T(8,128)(2,1)S(1)}, u32[]{:S(2)}, u32[]{:S(2)}) %collective-permute-start.10) | collective-permute-done | bytes 2080 | tf_op jit(solution)/shard_map/ppermute | solution.py:292
  (39 shorter events, 9.7 us)
Async XLA Ops:
  4.0 8.8 %copy-start.4 = (s32[1,16,16]{2,1,0:T(8,128)S(1)}, s32[1,16,16]{2,1,0:T(8,128)}, u32[]{:S(2)}) copy-start(s32[1,16,16]{2,1,0:T(8,128)} %param.12) | copy-start | bytes 3076
  4.0 43.8 %all-to-all-start = ((bf16[16,400,128]{2,1,0:T(8,128)(2,1)}), bf16[16,400,128]{2,1,0:T(8,128)(2,1)S(1)}, u32[]{:S(2)}, u32[]{:S(2)}) async-start(bf16[16,400,128]{2,1,0:T(8,128)(2,1)} %shard_map.110), calls=%async_computation | async-start | bytes 3276800 | tf_op jit(solution)/shard_map/all_to_all | solution.py:280
  60.3 26.2 %all-to-all-start.1 = ((bf16[16,64,128]{2,1,0:T(8,128)(2,1)}), bf16[16,64,128]{2,1,0:T(8,128)(2,1)S(1)}, u32[]{:S(2)}, u32[]{:S(2)}) async-start(bf16[16,64,128]{2,1,0:T(8,128)(2,1)} %get-tuple-element.15), calls=%async_computation.1 | async-start | bytes 524288 | tf_op jit(solution)/shard_map/all_to_all | solution.py:280
  86.5 7.7 %copy-start = (bf16[512,1024]{1,0:T(8,128)(2,1)S(1)}, bf16[512,1024]{1,0:T(8,128)(2,1)}, u32[]{:S(2)}) copy-start(bf16[512,1024]{1,0:T(8,128)(2,1)} %w_ref.3) | copy-start | bytes 3145732
  86.5 7.7 %copy-start.1 = (bf16[1,1,256,1024]{3,2,1,0:T(8,128)(2,1)S(1)}, bf16[1,1,256,1024]{3,2,1,0:T(8,128)(2,1)}, u32[]{:S(2)}) copy-start(bf16[1,1,256,1024]{3,2,1,0:T(8,128)(2,1)} %param.10) | copy-start | bytes 1572868
  86.5 7.7 %copy-start.2 = (bf16[16,64,128]{2,1,0:T(8,128)(2,1)}, bf16[16,64,128]{2,1,0:T(8,128)(2,1)S(1)}, u32[]{:S(2)}) copy-start(bf16[16,64,128]{2,1,0:T(8,128)(2,1)S(1)} %all-to-all-done.1.in_ref) | copy-start | bytes 786436
  86.5 84.3 %all-to-all-start.2 = ((bf16[16,320,128]{2,1,0:T(8,128)(2,1)}), bf16[16,320,128]{2,1,0:T(8,128)(2,1)S(1)}, u32[]{:S(2)}, u32[]{:S(2)}) async-start(bf16[16,320,128]{2,1,0:T(8,128)(2,1)} %shard_map.112), calls=%async_computation.2 | async-start | bytes 2621440 | tf_op jit(solution)/shard_map/all_to_all | solution.py:280
  94.2 1.0 copy-start.3
  96.8 4.0 %collective-permute-start = (bf16[4,4,4,16,256]{4,3,2,1,0:T(8,128)(2,1)}, bf16[4,4,4,16,256]{4,3,2,1,0:T(8,128)(2,1)S(1)}, u32[]{:S(2)}, u32[]{:S(2)}) collective-permute-start(bf16[4,4,4,16,256]{4,3,2,1,0:T(8,128)(2,1)} %get-tuple-element.24), channel_id=1, source_target_pairs={{0,16},{16,0},{32,48},{48,32},{64,80},{80,64},{96,112},{112,96},{1... | collective-permute-start | bytes 1572872 | tf_op jit(solution)/shard_map/ppermute | solution.py:324
  101.1 9.2 %collective-permute-start.1 = (bf16[4,4,16,256]{3,2,1,0:T(8,128)(2,1)S(1)}, bf16[4,4,16,256]{3,2,1,0:T(8,128)(2,1)S(1)}, u32[]{:S(2)}, u32[]{:S(2)}) collective-permute-start(bf16[4,4,16,256]{3,2,1,0:T(8,128)(2,1)S(1)} %get-tuple-element.25), channel_id=1, source_target_pairs={{0,128},{16,144},{32,160},{48,176},{64,192},{80,208},{96,224},{112... | collective-permute-start | bytes 393224 | tf_op jit(solution)/shard_map/ppermute | solution.py:292
  103.4 8.4 %collective-permute-start.3 = (bf16[4,4,16,256]{3,2,1,0:T(8,128)(2,1)S(1)}, bf16[4,4,16,256]{3,2,1,0:T(8,128)(2,1)S(1)}, u32[]{:S(2)}, u32[]{:S(2)}) collective-permute-start(bf16[4,4,16,256]{3,2,1,0:T(8,128)(2,1)S(1)} %get-tuple-element.26), channel_id=1, source_target_pairs={{0,384},{16,400},{32,416},{48,432},{64,448},{80,464},{96,480},{112... | collective-permute-start | bytes 393224 | tf_op jit(solution)/shard_map/ppermute | solution.py:292
  106.9 8.4 %collective-permute-start.2 = (bf16[4,4,16,256]{3,2,1,0:T(8,128)(2,1)S(1)}, bf16[4,4,16,256]{3,2,1,0:T(8,128)(2,1)S(1)}, u32[]{:S(2)}, u32[]{:S(2)}) collective-permute-start(bf16[4,4,16,256]{3,2,1,0:T(8,128)(2,1)S(1)} %get-tuple-element.27), channel_id=1, source_target_pairs={{0,256},{16,272},{32,288},{48,304},{64,320},{80,336},{96,352},{112... | collective-permute-start | bytes 393224 | tf_op jit(solution)/shard_map/ppermute | solution.py:292
  115.4 11.3 %collective-permute-start.4 = (bf16[4,16,256]{2,1,0:T(8,128)(2,1)S(1)}, bf16[4,16,256]{2,1,0:T(8,128)(2,1)S(1)}, u32[]{:S(2)}, u32[]{:S(2)}) collective-permute-start(bf16[4,16,256]{2,1,0:T(8,128)(2,1)S(1)} %get-tuple-element.28), channel_id=1, source_target_pairs={{0,1},{1,2},{2,3},{3,0},{4,5},{5,6},{6,7},{7,4},{8,9},{9,10},{10,1... | collective-permute-start | bytes 98312 | tf_op jit(solution)/shard_map/ppermute | solution.py:292
  119.2 7.5 %collective-permute-start.6 = (bf16[4,16,256]{2,1,0:T(8,128)(2,1)S(1)}, bf16[4,16,256]{2,1,0:T(8,128)(2,1)S(1)}, u32[]{:S(2)}, u32[]{:S(2)}) collective-permute-start(bf16[4,16,256]{2,1,0:T(8,128)(2,1)S(1)} %get-tuple-element.29), channel_id=1, source_target_pairs={{0,3},{1,0},{2,1},{3,2},{4,7},{5,4},{6,5},{7,6},{8,11},{9,8},{10,9... | collective-permute-start | bytes 98312 | tf_op jit(solution)/shard_map/ppermute | solution.py:292
  122.5 7.3 %collective-permute-start.5 = (bf16[4,16,256]{2,1,0:T(8,128)(2,1)S(1)}, bf16[4,16,256]{2,1,0:T(8,128)(2,1)S(1)}, u32[]{:S(2)}, u32[]{:S(2)}) collective-permute-start(bf16[4,16,256]{2,1,0:T(8,128)(2,1)S(1)} %get-tuple-element.30), channel_id=1, source_target_pairs={{0,2},{1,3},{2,0},{3,1},{4,6},{5,7},{6,4},{7,5},{8,10},{9,11},{10,... | collective-permute-start | bytes 98312 | tf_op jit(solution)/shard_map/ppermute | solution.py:292
  129.8 22.9 %collective-permute-start.7 = (bf16[16,256]{1,0:T(8,128)(2,1)S(1)}, bf16[16,256]{1,0:T(8,128)(2,1)S(1)}, u32[]{:S(2)}, u32[]{:S(2)}) collective-permute-start(bf16[16,256]{1,0:T(8,128)(2,1)S(1)} %get-tuple-element.31), channel_id=1, source_target_pairs={{0,32},{16,48},{32,64},{48,80},{64,96},{80,112},{96,0},{112,16},{1... | collective-permute-start | bytes 24584 | tf_op jit(solution)/shard_map/ppermute | solution.py:292
  138.9 13.8 %collective-permute-start.9 = (bf16[16,256]{1,0:T(8,128)(2,1)S(1)}, bf16[16,256]{1,0:T(8,128)(2,1)S(1)}, u32[]{:S(2)}, u32[]{:S(2)}) collective-permute-start(bf16[16,256]{1,0:T(8,128)(2,1)S(1)} %get-tuple-element.32), channel_id=1, source_target_pairs={{0,96},{16,112},{32,0},{48,16},{64,32},{80,48},{96,64},{112,80},{1... | collective-permute-start | bytes 24584 | tf_op jit(solution)/shard_map/ppermute | solution.py:292
  141.8 14.3 %collective-permute-start.8 = (bf16[16,256]{1,0:T(8,128)(2,1)S(1)}, bf16[16,256]{1,0:T(8,128)(2,1)S(1)}, u32[]{:S(2)}, u32[]{:S(2)}) collective-permute-start(bf16[16,256]{1,0:T(8,128)(2,1)S(1)} %get-tuple-element.33), channel_id=1, source_target_pairs={{0,64},{16,80},{32,96},{48,112},{64,0},{80,16},{96,32},{112,48},{1... | collective-permute-start | bytes 24584 | tf_op jit(solution)/shard_map/ppermute | solution.py:292
  156.2 10.6 %collective-permute-start.12 = (bf16[16,64]{1,0:T(8,128)(2,1)S(1)}, bf16[16,64]{1,0:T(8,128)(2,1)S(1)}, u32[]{:S(2)}, u32[]{:S(2)}) collective-permute-start(bf16[16,64]{1,0:T(8,128)(2,1)S(1)} %bitcast.58), channel_id=1, source_target_pairs={{0,12},{1,13},{2,14},{3,15},{4,0},{5,1},{6,2},{7,3},{8,4},{9,5},{1... | collective-permute-start | bytes 6152 | tf_op jit(solution)/shard_map/ppermute | solution.py:292
  161.8 7.3 %collective-permute-start.10 = (bf16[16,64]{1,0:T(8,128)(2,1)S(1)}, bf16[16,64]{1,0:T(8,128)(2,1)S(1)}, u32[]{:S(2)}, u32[]{:S(2)}) collective-permute-start(bf16[16,64]{1,0:T(8,128)(2,1)S(1)} %bitcast.57), channel_id=1, source_target_pairs={{0,4},{1,5},{2,6},{3,7},{4,8},{5,9},{6,10},{7,11},{8,12},{9,13},{1... | collective-permute-start | bytes 6152 | tf_op jit(solution)/shard_map/ppermute | solution.py:292
  163.8 6.4 %collective-permute-start.11 = (bf16[16,64]{1,0:T(8,128)(2,1)S(1)}, bf16[16,64]{1,0:T(8,128)(2,1)S(1)}, u32[]{:S(2)}, u32[]{:S(2)}) collective-permute-start(bf16[16,64]{1,0:T(8,128)(2,1)S(1)} %bitcast.56), channel_id=1, source_target_pairs={{0,8},{1,9},{2,10},{3,11},{4,12},{5,13},{6,14},{7,15},{8,0},{9,1},... | collective-permute-start | bytes 6152 | tf_op jit(solution)/shard_map/ppermute | solution.py:292

commit v4 on v3

--- a/solution.py
+++ b/solution.py
@@ -325,9 +325,18 @@
     term = (mine.astype(F32) + other.astype(F32)).astype(BF)
     term = ring_sum(term, "scene", scenes, X, ZHI * CORES).astype(BF)
     term = ring_sum(term, "view", VIEWS, Y, 1).astype(BF)
-    term = ring_sum(term, "scene", scenes, ZHI, CORES).astype(BF)
-    term = term.reshape(own, ZLO, COLS).transpose(1, 0, 2)
-    share = ring_sum(term, "view", VIEWS, ZLO, Y) * float(scenes * VIEWS * TOK) ** (-0.5)
+    term, home = lax.optimization_barrier((term, home))
+    term = term.reshape(ZHI, own, ZLO, COLS).transpose(0, 2, 1, 3).reshape(ZHI * ZLO, own, COLS)
+    along_z = [
+        [((x * ZHI + zh) * CORES + k) * VIEWS + zl * Y + y for zh in range(ZHI) for zl in range(ZLO)]
+        for x in range(X)
+        for k in range(CORES)
+        for y in range(Y)
+    ]
+    term = lax.all_to_all(
+        term, ("scene", "view"), 0, 0, tiled=True, axis_index_groups=along_z
+    )
+    share = jnp.sum(term.astype(F32), axis=0) * float(scenes * VIEWS * TOK) ** (-0.5)
     gq, gk, gv = call(unpack_kernel, (shape(TOK, INNER),) * 3, (home,))
     return (layer[None, None], gq[None, None], gk[None, None], gv[None, None], share)
 

time: 174 us -> 158 us (0.908)
  starting transfers between devices: 80.4 us -> 59.6 us
  waiting for transfers between devices: 51.7 us -> 56.5 us
    ppermute x12 -> x6, starting transfers between devices: 53.6 us -> 20.3 us  [ring_sum(): total = total + lax.ppermute(send, axis, pairs).astype(F32)]
    all_to_all x0 -> x1, starting transfers between devices: none -> 12.5 us  [on_device(): lax.all_to_all(term, ('scene', 'view'), 0, 0, tiled=True, axis_index_grou...]
    all_to_all x0 -> x1, waiting for transfers between devices: none -> 11.3 us  [on_device(): lax.all_to_all(term, ('scene', 'view'), 0, 0, tiled=True, axis_index_grou...]
    ppermute x12 -> x6, waiting for transfers between devices: 14.8 us -> 8.32 us  [ring_sum(): total = total + lax.ppermute(send, axis, pairs).astype(F32)]
  transfers between devices with their start and end apart: 16 -> 11, of which waited for: 8 -> 7; matrix products, arithmetic and copies ran while one was open for 1% -> 0% of each run, Pallas kernels for 11% -> 13%
where the time goes in v4:
time: 158 us; the launch traced here: 157 us
  starting transfers between devices  59.6 us (38%)
  waiting for transfers between devices  56.5 us (36%)
  Pallas kernels  36.4 us (23%)
  local copies, waits for them, and re-layouts  2.08 us (1%)
    pallas_call x5, Pallas kernels, call(): pl.pallas_call(kernel, out_shape=outs, in_specs=[SMEM] * smem + [VMEM] *...  36.4 us
    all_to_all x3, waiting for transfers between devices, swap(): return lax.all_to_all(rows, axis, split_axis=0, concat_axis=0, tiled=True)  34.9 us
    all_to_all x3, starting transfers between devices, swap(): return lax.all_to_all(rows, axis, split_axis=0, concat_axis=0, tiled=True)  24.9 us
    ppermute x6, starting transfers between devices, ring_sum(): total = total + lax.ppermute(send, axis, pairs).astype(F32)  20.3 us
    all_to_all x1, starting transfers between devices, on_device(): lax.all_to_all(term, ('scene', 'view'), 0, 0, tiled=True, axis_index_grou...  12.5 us
    all_to_all x1, waiting for transfers between devices, on_device(): lax.all_to_all(term, ('scene', 'view'), 0, 0, tiled=True, axis_index_grou...  11.3 us
    ppermute x6, waiting for transfers between devices, ring_sum(): total = total + lax.ppermute(send, axis, pairs).astype(F32)  8.32 us
  transfers between devices with their start and end apart: 11, of which 7 were waited for; matrix products, arithmetic and copies ran while one was open for 0% of the time, Pallas kernels for 13%

profile of v4, /device:TPU:6, one launch (start us, length us, event | category | flops | bytes accessed | tf_op | source)
XLA Modules:
  0.0 156.6 jit_solution(7511606321867251882)
XLA Ops:
  0.6 3.4 %shard_map.110 = bf16[16,400,128]{2,1,0:T(8,128)(2,1)} custom-call(bf16[256,512]{1,0:T(8,128)(2,1)} %bitcast.31, bf16[256,512]{1,0:T(8,128)(2,1)} %bitcast.32, bf16[256,512]{1,0:T(8,128)(2,1)} %bitcast.33, bf16[256,1024]{1,0:T(8,128)(2,1)} %bitcast.29, bf16[512,1024]{1,0:T(8,128)(2,1)} %w_ref.3, s32[2,16]{1,0:T(2,128)} %bitcast.35), custom_call_target="tpu_custom_call" | custom-call | bytes 4194304 | tf_op jit(solution)/shard_map/pallas_call | solution.py:232
  4.0 8.8 %all-to-all-start = ((bf16[16,400,128]{2,1,0:T(8,128)(2,1)}), bf16[16,400,128]{2,1,0:T(8,128)(2,1)S(1)}, u32[]{:S(2)}, u32[]{:S(2)}) async-start(bf16[16,400,128]{2,1,0:T(8,128)(2,1)} %shard_map.110), calls=%async_computation | async-start | bytes 3276800 | tf_op jit(solution)/shard_map/all_to_all | solution.py:280
  12.9 34.9 %all-to-all-done.in_ref = bf16[16,400,128]{2,1,0:T(8,128)(2,1)S(1)} async-done(((bf16[16,400,128]{2,1,0:T(8,128)(2,1)}), bf16[16,400,128]{2,1,0:T(8,128)(2,1)S(1)}, u32[]{:S(2)}, u32[]{:S(2)}) %all-to-all-start) | async-done | bytes 1638432 | tf_op jit(solution)/shard_map/all_to_all | solution.py:280
  47.9 12.4 %shard_map.111 = (bf16[16,64,128]{2,1,0:T(8,128)(2,1)}, f32[16,8,128]{2,1,0:T(8,128)S(1)}) custom-call(s32[256]{0:T(256)S(1)} %reshape.25.fetch_ref, s32[256]{0:T(256)S(1)} %reshape.27.mask_ref, bf16[16,400,128]{2,1,0:T(8,128)(2,1)S(1)} %all-to-all-done.in_ref), custom_call_target="tpu_custom_call" | custom-call | flops 10000000000 | bytes 4194304 | tf_op jit(solution)/shard_map/pallas_call | solution.py:232
  60.3 8.5 %all-to-all-start.1 = ((bf16[16,64,128]{2,1,0:T(8,128)(2,1)}), bf16[16,64,128]{2,1,0:T(8,128)(2,1)S(1)}, u32[]{:S(2)}, u32[]{:S(2)}) async-start(bf16[16,64,128]{2,1,0:T(8,128)(2,1)} %get-tuple-element.17), calls=%async_computation.1 | async-start | bytes 524288 | tf_op jit(solution)/shard_map/all_to_all | solution.py:280
  68.8 17.7 %shard_map.112 = bf16[16,320,128]{2,1,0:T(8,128)(2,1)} custom-call(s32[256]{0:T(256)S(1)} %reshape.25.fetch_ref, s32[256]{0:T(256)S(1)} %reshape.27.mask_ref, bf16[16,400,128]{2,1,0:T(8,128)(2,1)S(1)} %all-to-all-done.in_ref, f32[16,8,128]{2,1,0:T(8,128)S(1)} %get-tuple-element.18.stat_ref), custom_call_target="tpu_custom_call" | custom-call | flops 20000000000 | bytes 4194304 | tf_op jit(solution)/shard_map/pallas_call | solution.py:232
  86.5 7.7 %all-to-all-start.2 = ((bf16[16,320,128]{2,1,0:T(8,128)(2,1)}), bf16[16,320,128]{2,1,0:T(8,128)(2,1)S(1)}, u32[]{:S(2)}, u32[]{:S(2)}) async-start(bf16[16,320,128]{2,1,0:T(8,128)(2,1)} %shard_map.112), calls=%async_computation.2 | async-start | bytes 2621440 | tf_op jit(solution)/shard_map/all_to_all | solution.py:280
  94.2 0.9 copy-done.3
  95.1 1.7 %shard_map.113 = (bf16[256,1024]{1,0:T(8,128)(2,1)}, bf16[4,4,4,16,256]{4,3,2,1,0:T(8,128)(2,1)S(1)}, bf16[4,4,4,16,256]{4,3,2,1,0:T(8,128)(2,1)}) custom-call(s32[1]{0:T(128)} %bitcast.core_ref, bf16[16,64,128]{2,1,0:T(8,128)(2,1)S(1)} %copy-done.3, bf16[256,1024]{1,0:T(8,128)(2,1)S(1)} %bitcast.30, bf16[512,1024]{1,0:T(8,128)(2,1)S(1)} %copy-done), custom_call_target="tpu_custom_call" | custom-call | flops 1000000000 | bytes 4194304 | tf_op jit(solution)/shard_map/pallas_call | solution.py:232
  96.8 1.9 %collective-permute-start = (bf16[4,4,4,16,256]{4,3,2,1,0:T(8,128)(2,1)}, bf16[4,4,4,16,256]{4,3,2,1,0:T(8,128)(2,1)S(1)}, u32[]{:S(2)}, u32[]{:S(2)}) collective-permute-start(bf16[4,4,4,16,256]{4,3,2,1,0:T(8,128)(2,1)} %get-tuple-element.22), channel_id=1, source_target_pairs={{0,16},{16,0},{32,48},{48,32},{64,80},{80,64},{96,112},{112,96},{1... | collective-permute-start | bytes 1572872 | tf_op jit(solution)/shard_map/ppermute | solution.py:324
  98.8 2.0 %collective-permute-done = bf16[4,4,4,16,256]{4,3,2,1,0:T(8,128)(2,1)S(1)} collective-permute-done((bf16[4,4,4,16,256]{4,3,2,1,0:T(8,128)(2,1)}, bf16[4,4,4,16,256]{4,3,2,1,0:T(8,128)(2,1)S(1)}, u32[]{:S(2)}, u32[]{:S(2)}) %collective-permute-start) | collective-permute-done | bytes 524320 | tf_op jit(solution)/shard_map/ppermute | solution.py:324
  101.0 2.7 %collective-permute-start.3 = (bf16[4,4,16,256]{3,2,1,0:T(8,128)(2,1)S(1)}, bf16[4,4,16,256]{3,2,1,0:T(8,128)(2,1)S(1)}, u32[]{:S(2)}, u32[]{:S(2)}) collective-permute-start(bf16[4,4,16,256]{3,2,1,0:T(8,128)(2,1)S(1)} %get-tuple-element.30), channel_id=1, source_target_pairs={{0,384},{16,400},{32,416},{48,432},{64,448},{80,464},{96,480},{112... | collective-permute-start | bytes 393224 | tf_op jit(solution)/shard_map/ppermute | solution.py:292
  103.7 3.0 %collective-permute-start.2 = (bf16[4,4,16,256]{3,2,1,0:T(8,128)(2,1)S(1)}, bf16[4,4,16,256]{3,2,1,0:T(8,128)(2,1)S(1)}, u32[]{:S(2)}, u32[]{:S(2)}) collective-permute-start(bf16[4,4,16,256]{3,2,1,0:T(8,128)(2,1)S(1)} %get-tuple-element.31), channel_id=1, source_target_pairs={{0,256},{16,272},{32,288},{48,304},{64,320},{80,336},{96,352},{112... | collective-permute-start | bytes 393224 | tf_op jit(solution)/shard_map/ppermute | solution.py:292
  106.7 4.0 %collective-permute-start.1 = (bf16[4,4,16,256]{3,2,1,0:T(8,128)(2,1)S(1)}, bf16[4,4,16,256]{3,2,1,0:T(8,128)(2,1)S(1)}, u32[]{:S(2)}, u32[]{:S(2)}) collective-permute-start(bf16[4,4,16,256]{3,2,1,0:T(8,128)(2,1)S(1)} %get-tuple-element.29), channel_id=1, source_target_pairs={{0,128},{16,144},{32,160},{48,176},{64,192},{80,208},{96,224},{112... | collective-permute-start | bytes 393224 | tf_op jit(solution)/shard_map/ppermute | solution.py:292
  110.8 1.6 %collective-permute-done.2 = bf16[4,4,16,256]{3,2,1,0:T(8,128)(2,1)S(1)} collective-permute-done((bf16[4,4,16,256]{3,2,1,0:T(8,128)(2,1)S(1)}, bf16[4,4,16,256]{3,2,1,0:T(8,128)(2,1)S(1)}, u32[]{:S(2)}, u32[]{:S(2)}) %collective-permute-start.2) | collective-permute-done | bytes 131104 | tf_op jit(solution)/shard_map/ppermute | solution.py:292
  112.4 2.5 %collective-permute-done.1 = bf16[4,4,16,256]{3,2,1,0:T(8,128)(2,1)S(1)} collective-permute-done((bf16[4,4,16,256]{3,2,1,0:T(8,128)(2,1)S(1)}, bf16[4,4,16,256]{3,2,1,0:T(8,128)(2,1)S(1)}, u32[]{:S(2)}, u32[]{:S(2)}) %collective-permute-start.1) | collective-permute-done | bytes 131104 | tf_op jit(solution)/shard_map/ppermute | solution.py:292
  115.0 5.0 %collective-permute-start.6 = (bf16[4,16,256]{2,1,0:T(8,128)(2,1)S(1)}, bf16[4,16,256]{2,1,0:T(8,128)(2,1)S(1)}, u32[]{:S(2)}, u32[]{:S(2)}) collective-permute-start(bf16[4,16,256]{2,1,0:T(8,128)(2,1)S(1)} %get-tuple-element.33), channel_id=1, source_target_pairs={{0,3},{1,0},{2,1},{3,2},{4,7},{5,4},{6,5},{7,6},{8,11},{9,8},{10,9... | collective-permute-start | bytes 98312 | tf_op jit(solution)/shard_map/ppermute | solution.py:292
  120.1 2.8 %collective-permute-start.5 = (bf16[4,16,256]{2,1,0:T(8,128)(2,1)S(1)}, bf16[4,16,256]{2,1,0:T(8,128)(2,1)S(1)}, u32[]{:S(2)}, u32[]{:S(2)}) collective-permute-start(bf16[4,16,256]{2,1,0:T(8,128)(2,1)S(1)} %get-tuple-element.34), channel_id=1, source_target_pairs={{0,2},{1,3},{2,0},{3,1},{4,6},{5,7},{6,4},{7,5},{8,10},{9,11},{10,... | collective-permute-start | bytes 98312 | tf_op jit(solution)/shard_map/ppermute | solution.py:292
  122.8 2.8 %collective-permute-start.4 = (bf16[4,16,256]{2,1,0:T(8,128)(2,1)S(1)}, bf16[4,16,256]{2,1,0:T(8,128)(2,1)S(1)}, u32[]{:S(2)}, u32[]{:S(2)}) collective-permute-start(bf16[4,16,256]{2,1,0:T(8,128)(2,1)S(1)} %get-tuple-element.32), channel_id=1, source_target_pairs={{0,1},{1,2},{2,3},{3,0},{4,5},{5,6},{6,7},{7,4},{8,9},{9,10},{10,1... | collective-permute-start | bytes 98312 | tf_op jit(solution)/shard_map/ppermute | solution.py:292
  125.6 2.1 %collective-permute-done.5 = bf16[4,16,256]{2,1,0:T(8,128)(2,1)S(1)} collective-permute-done((bf16[4,16,256]{2,1,0:T(8,128)(2,1)S(1)}, bf16[4,16,256]{2,1,0:T(8,128)(2,1)S(1)}, u32[]{:S(2)}, u32[]{:S(2)}) %collective-permute-start.5) | collective-permute-done | bytes 32800 | tf_op jit(solution)/shard_map/ppermute | solution.py:292
  127.7 2.1 %collective-permute-done.4 = bf16[4,16,256]{2,1,0:T(8,128)(2,1)S(1)} collective-permute-done((bf16[4,16,256]{2,1,0:T(8,128)(2,1)S(1)}, bf16[4,16,256]{2,1,0:T(8,128)(2,1)S(1)}, u32[]{:S(2)}, u32[]{:S(2)}) %collective-permute-start.4) | collective-permute-done | bytes 32800 | tf_op jit(solution)/shard_map/ppermute | solution.py:292
  130.7 12.5 %all-to-all-start.3 = ((bf16[16,2,512]{2,1,0:T(2,128)(2,1)}), bf16[16,2,512]{2,1,0:T(2,128)(2,1)S(1)}, u32[]{:S(2)}, u32[]{:S(2)}) async-start(bf16[16,2,512]{2,1,0:T(2,128)(2,1)} %reshape.37), calls=%async_computation.3 | async-start | bytes 65536 | tf_op jit(solution)/shard_map/all_to_all | solution.py:336
  143.2 1.3 shard_map.114
  144.6 11.3 %all-to-all-done.3 = bf16[16,2,512]{2,1,0:T(2,128)(2,1)S(1)} async-done(((bf16[16,2,512]{2,1,0:T(2,128)(2,1)}), bf16[16,2,512]{2,1,0:T(2,128)(2,1)S(1)}, u32[]{:S(2)}, u32[]{:S(2)}) %all-to-all-start.3) | async-done | bytes 32800 | tf_op jit(solution)/shard_map/all_to_all | solution.py:336
  (27 shorter events, 2.1 us)
Async XLA Ops:
  4.0 8.8 %copy-start.4 = (s32[1,16,16]{2,1,0:T(8,128)S(1)}, s32[1,16,16]{2,1,0:T(8,128)}, u32[]{:S(2)}) copy-start(s32[1,16,16]{2,1,0:T(8,128)} %param.12) | copy-start | bytes 3076
  4.0 43.8 %all-to-all-start = ((bf16[16,400,128]{2,1,0:T(8,128)(2,1)}), bf16[16,400,128]{2,1,0:T(8,128)(2,1)S(1)}, u32[]{:S(2)}, u32[]{:S(2)}) async-start(bf16[16,400,128]{2,1,0:T(8,128)(2,1)} %shard_map.110), calls=%async_computation | async-start | bytes 3276800 | tf_op jit(solution)/shard_map/all_to_all | solution.py:280
  60.3 26.2 %all-to-all-start.1 = ((bf16[16,64,128]{2,1,0:T(8,128)(2,1)}), bf16[16,64,128]{2,1,0:T(8,128)(2,1)S(1)}, u32[]{:S(2)}, u32[]{:S(2)}) async-start(bf16[16,64,128]{2,1,0:T(8,128)(2,1)} %get-tuple-element.17), calls=%async_computation.1 | async-start | bytes 524288 | tf_op jit(solution)/shard_map/all_to_all | solution.py:280
  86.4 7.7 %copy-start = (bf16[512,1024]{1,0:T(8,128)(2,1)S(1)}, bf16[512,1024]{1,0:T(8,128)(2,1)}, u32[]{:S(2)}) copy-start(bf16[512,1024]{1,0:T(8,128)(2,1)} %w_ref.3) | copy-start | bytes 3145732
  86.4 7.7 %copy-start.1 = (bf16[1,1,256,1024]{3,2,1,0:T(8,128)(2,1)S(1)}, bf16[1,1,256,1024]{3,2,1,0:T(8,128)(2,1)}, u32[]{:S(2)}) copy-start(bf16[1,1,256,1024]{3,2,1,0:T(8,128)(2,1)} %param.10) | copy-start | bytes 1572868
  86.4 7.7 %copy-start.2 = (bf16[16,64,128]{2,1,0:T(8,128)(2,1)}, bf16[16,64,128]{2,1,0:T(8,128)(2,1)S(1)}, u32[]{:S(2)}) copy-start(bf16[16,64,128]{2,1,0:T(8,128)(2,1)S(1)} %all-to-all-done.1.in_ref) | copy-start | bytes 786436
  86.5 43.4 %all-to-all-start.2 = ((bf16[16,320,128]{2,1,0:T(8,128)(2,1)}), bf16[16,320,128]{2,1,0:T(8,128)(2,1)S(1)}, u32[]{:S(2)}, u32[]{:S(2)}) async-start(bf16[16,320,128]{2,1,0:T(8,128)(2,1)} %shard_map.112), calls=%async_computation.2 | async-start | bytes 2621440 | tf_op jit(solution)/shard_map/all_to_all | solution.py:280
  94.2 1.0 copy-start.3
  96.8 4.0 %collective-permute-start = (bf16[4,4,4,16,256]{4,3,2,1,0:T(8,128)(2,1)}, bf16[4,4,4,16,256]{4,3,2,1,0:T(8,128)(2,1)S(1)}, u32[]{:S(2)}, u32[]{:S(2)}) collective-permute-start(bf16[4,4,4,16,256]{4,3,2,1,0:T(8,128)(2,1)} %get-tuple-element.22), channel_id=1, source_target_pairs={{0,16},{16,0},{32,48},{48,32},{64,80},{80,64},{96,112},{112,96},{1... | collective-permute-start | bytes 1572872 | tf_op jit(solution)/shard_map/ppermute | solution.py:324
  101.0 9.8 %collective-permute-start.3 = (bf16[4,4,16,256]{3,2,1,0:T(8,128)(2,1)S(1)}, bf16[4,4,16,256]{3,2,1,0:T(8,128)(2,1)S(1)}, u32[]{:S(2)}, u32[]{:S(2)}) collective-permute-start(bf16[4,4,16,256]{3,2,1,0:T(8,128)(2,1)S(1)} %get-tuple-element.30), channel_id=1, source_target_pairs={{0,384},{16,400},{32,416},{48,432},{64,448},{80,464},{96,480},{112... | collective-permute-start | bytes 393224 | tf_op jit(solution)/shard_map/ppermute | solution.py:292
  103.7 8.7 %collective-permute-start.2 = (bf16[4,4,16,256]{3,2,1,0:T(8,128)(2,1)S(1)}, bf16[4,4,16,256]{3,2,1,0:T(8,128)(2,1)S(1)}, u32[]{:S(2)}, u32[]{:S(2)}) collective-permute-start(bf16[4,4,16,256]{3,2,1,0:T(8,128)(2,1)S(1)} %get-tuple-element.31), channel_id=1, source_target_pairs={{0,256},{16,272},{32,288},{48,304},{64,320},{80,336},{96,352},{112... | collective-permute-start | bytes 393224 | tf_op jit(solution)/shard_map/ppermute | solution.py:292
  106.7 8.2 %collective-permute-start.1 = (bf16[4,4,16,256]{3,2,1,0:T(8,128)(2,1)S(1)}, bf16[4,4,16,256]{3,2,1,0:T(8,128)(2,1)S(1)}, u32[]{:S(2)}, u32[]{:S(2)}) collective-permute-start(bf16[4,4,16,256]{3,2,1,0:T(8,128)(2,1)S(1)} %get-tuple-element.29), channel_id=1, source_target_pairs={{0,128},{16,144},{32,160},{48,176},{64,192},{80,208},{96,224},{112... | collective-permute-start | bytes 393224 | tf_op jit(solution)/shard_map/ppermute | solution.py:292
  115.0 10.6 %collective-permute-start.6 = (bf16[4,16,256]{2,1,0:T(8,128)(2,1)S(1)}, bf16[4,16,256]{2,1,0:T(8,128)(2,1)S(1)}, u32[]{:S(2)}, u32[]{:S(2)}) collective-permute-start(bf16[4,16,256]{2,1,0:T(8,128)(2,1)S(1)} %get-tuple-element.33), channel_id=1, source_target_pairs={{0,3},{1,0},{2,1},{3,2},{4,7},{5,4},{6,5},{7,6},{8,11},{9,8},{10,9... | collective-permute-start | bytes 98312 | tf_op jit(solution)/shard_map/ppermute | solution.py:292
  120.1 7.7 %collective-permute-start.5 = (bf16[4,16,256]{2,1,0:T(8,128)(2,1)S(1)}, bf16[4,16,256]{2,1,0:T(8,128)(2,1)S(1)}, u32[]{:S(2)}, u32[]{:S(2)}) collective-permute-start(bf16[4,16,256]{2,1,0:T(8,128)(2,1)S(1)} %get-tuple-element.34), channel_id=1, source_target_pairs={{0,2},{1,3},{2,0},{3,1},{4,6},{5,7},{6,4},{7,5},{8,10},{9,11},{10,... | collective-permute-start | bytes 98312 | tf_op jit(solution)/shard_map/ppermute | solution.py:292
  122.8 7.0 %collective-permute-start.4 = (bf16[4,16,256]{2,1,0:T(8,128)(2,1)S(1)}, bf16[4,16,256]{2,1,0:T(8,128)(2,1)S(1)}, u32[]{:S(2)}, u32[]{:S(2)}) collective-permute-start(bf16[4,16,256]{2,1,0:T(8,128)(2,1)S(1)} %get-tuple-element.32), channel_id=1, source_target_pairs={{0,1},{1,2},{2,3},{3,0},{4,5},{5,6},{6,7},{7,4},{8,9},{9,10},{10,1... | collective-permute-start | bytes 98312 | tf_op jit(solution)/shard_map/ppermute | solution.py:292
  130.7 25.1 %all-to-all-start.3 = ((bf16[16,2,512]{2,1,0:T(2,128)(2,1)}), bf16[16,2,512]{2,1,0:T(2,128)(2,1)S(1)}, u32[]{:S(2)}, u32[]{:S(2)}) async-start(bf16[16,2,512]{2,1,0:T(2,128)(2,1)} %reshape.37), calls=%async_computation.3 | async-start | bytes 65536 | tf_op jit(solution)/shard_map/all_to_all | solution.py:336

commit v5 on v4

--- a/solution.py
+++ b/solution.py
@@ -24,6 +24,7 @@
 BACK_ROWS = TOK + BLK // 2
 X, ZHI, CORES = 4, 4, 2
 ZLO, Y = 4, 4
+RING = (0, 2, 3, 1)
 NT = (((1,), (1,)), ((), ()))
 VMEM = pl.BlockSpec(memory_space=pltpu.VMEM)
 SMEM = pl.BlockSpec(memory_space=pltpu.SMEM)
@@ -207,7 +208,7 @@
                 at = pl.multiple_of((x * ZHI + z) * CORES * own + side * own, own)
                 rows = term[pl.ds(at, own), :]
                 for y in range(Y):
-                    ref[x, y, z, :, :] = rows[:, y * wide : (y + 1) * wide]
+                    ref[RING[x], RING[y], z, :, :] = rows[:, y * wide : (y + 1) * wide]
 
 
 def unpack_kernel(in_ref, gq_ref, gk_ref, gv_ref):
@@ -228,7 +229,7 @@
     return jax.ShapeDtypeStruct(dims, dtype)
 
 
-def call(kernel, outs, args, smem=0, scratch=(), mib=32, flops=0):
+def call(kernel, outs, args, smem=0, scratch=(), mib=20, flops=0):
     return pl.pallas_call(
         kernel,
         out_shape=outs,
@@ -280,17 +281,19 @@
     return lax.all_to_all(rows, axis, split_axis=0, concat_axis=0, tiled=True)
 
 
-def ring_sum(pieces, axis, count, size, step):
-    here = (lax.axis_index(axis) // step) % size
-    total = lax.dynamic_index_in_dim(pieces, here, 0, keepdims=False).astype(F32)
-    for d in range(1, size):
+def pair_sums(pieces, axis, count, step):
+    here = (lax.axis_index(axis) // step) % 4
+    pieces = pieces.reshape((2, 2) + pieces.shape[1:])
+    for side, partner in ((((here + 1) // 2) % 2, (1, 0, 3, 2)), (here // 2, (3, 2, 1, 0))):
         pairs = []
         for i in range(count):
-            at = (i // step) % size
-            pairs.append((i, i + ((at + d) % size - at) * step))
-        send = lax.dynamic_index_in_dim(pieces, (here + d) % size, 0, keepdims=False)
-        total = total + lax.ppermute(send, axis, pairs).astype(F32)
-    return total
+            at = (i // step) % 4
+            pairs.append((i, i + (partner[at] - at) * step))
+        keep = lax.dynamic_index_in_dim(pieces, side, 0, keepdims=False)
+        send = lax.dynamic_index_in_dim(pieces, 1 - side, 0, keepdims=False)
+        got = lax.ppermute(send, axis, pairs)
+        pieces = (keep.astype(F32) + got.astype(F32)).astype(BF)
+    return pieces
 
 
 def on_device(query_rows, key_rows, value_rows, grad_out, out_weight, fetch_list, read_mask):
@@ -323,8 +326,8 @@
     scenes = X * ZHI * CORES
     other = lax.ppermute(other, "scene", [(i, i ^ 1) for i in range(scenes)])
     term = (mine.astype(F32) + other.astype(F32)).astype(BF)
-    term = ring_sum(term, "scene", scenes, X, ZHI * CORES).astype(BF)
-    term = ring_sum(term, "view", VIEWS, Y, 1).astype(BF)
+    term = pair_sums(term, "scene", scenes, ZHI * CORES)
+    term = pair_sums(term, "view", VIEWS, 1)
     term, home = lax.optimization_barrier((term, home))
     term = term.reshape(ZHI, own, ZLO, COLS).transpose(0, 2, 1, 3).reshape(ZHI * ZLO, own, COLS)
     along_z = [

time: 158 us -> 161 us (1.019)
  waiting for transfers between devices: 56.5 us -> 65.6 us
  starting transfers between devices: 59.6 us -> 53.8 us
    ppermute x6 -> x4, waiting for transfers between devices: 8.32 us -> 17.4 us  [pair_sums(): got = lax.ppermute(send, axis, pairs)]
    ppermute x6 -> x4, starting transfers between devices: 20.3 us -> 13.9 us  [pair_sums(): got = lax.ppermute(send, axis, pairs)]
  transfers between devices with their start and end apart: 11 -> 9, of which waited for: 7 -> 7; matrix products, arithmetic and copies ran while one was open for 0% -> 0% of each run, Pallas kernels for 13% -> 13%
where the time goes in v5:
time: 161 us; the launch traced here: 160 us
  waiting for transfers between devices  65.6 us (41%)
  starting transfers between devices  53.8 us (33%)
  Pallas kernels  36.4 us (23%)
  local copies, waits for them, and re-layouts  2.1 us (1%)
    pallas_call x5, Pallas kernels, call(): pl.pallas_call(kernel, out_shape=outs, in_specs=[SMEM] * smem + [VMEM] *...  36.4 us
    all_to_all x3, waiting for transfers between devices, swap(): return lax.all_to_all(rows, axis, split_axis=0, concat_axis=0, tiled=True)  34.9 us
    all_to_all x3, starting transfers between devices, swap(): return lax.all_to_all(rows, axis, split_axis=0, concat_axis=0, tiled=True)  25 us
    ppermute x4, waiting for transfers between devices, pair_sums(): got = lax.ppermute(send, axis, pairs)  17.4 us
    ppermute x4, starting transfers between devices, pair_sums(): got = lax.ppermute(send, axis, pairs)  13.9 us
    all_to_all x1, starting transfers between devices, on_device(): lax.all_to_all(term, ('scene', 'view'), 0, 0, tiled=True, axis_index_grou...  13 us
    all_to_all x1, waiting for transfers between devices, on_device(): lax.all_to_all(term, ('scene', 'view'), 0, 0, tiled=True, axis_index_grou...  11.3 us
  transfers between devices with their start and end apart: 9, of which 7 were waited for; matrix products, arithmetic and copies ran while one was open for 0% of the time, Pallas kernels for 13%

profile of v5, /device:TPU:6, one launch (start us, length us, event | category | flops | bytes accessed | tf_op | source)
XLA Modules:
  0.0 159.9 jit_solution(5671139554540850013)
XLA Ops:
  0.6 3.4 %shard_map.110 = bf16[16,400,128]{2,1,0:T(8,128)(2,1)} custom-call(bf16[256,512]{1,0:T(8,128)(2,1)} %bitcast.39, bf16[256,512]{1,0:T(8,128)(2,1)} %bitcast.40, bf16[256,512]{1,0:T(8,128)(2,1)} %bitcast.41, bf16[256,1024]{1,0:T(8,128)(2,1)} %bitcast.33, bf16[512,1024]{1,0:T(8,128)(2,1)} %w_ref.3, s32[2,16]{1,0:T(2,128)} %bitcast.43), custom_call_target="tpu_custom_call" | custom-call | bytes 4194304 | tf_op jit(solution)/shard_map/pallas_call | solution.py:233
  4.0 8.8 %all-to-all-start = ((bf16[16,400,128]{2,1,0:T(8,128)(2,1)}), bf16[16,400,128]{2,1,0:T(8,128)(2,1)S(1)}, u32[]{:S(2)}, u32[]{:S(2)}) async-start(bf16[16,400,128]{2,1,0:T(8,128)(2,1)} %shard_map.110), calls=%async_computation | async-start | bytes 3276800 | tf_op jit(solution)/shard_map/all_to_all | solution.py:281
  12.9 34.9 %all-to-all-done.in_ref = bf16[16,400,128]{2,1,0:T(8,128)(2,1)S(1)} async-done(((bf16[16,400,128]{2,1,0:T(8,128)(2,1)}), bf16[16,400,128]{2,1,0:T(8,128)(2,1)S(1)}, u32[]{:S(2)}, u32[]{:S(2)}) %all-to-all-start) | async-done | bytes 1638432 | tf_op jit(solution)/shard_map/all_to_all | solution.py:281
  47.9 12.3 %shard_map.111 = (bf16[16,64,128]{2,1,0:T(8,128)(2,1)}, f32[16,8,128]{2,1,0:T(8,128)S(1)}) custom-call(s32[256]{0:T(256)S(1)} %reshape.35.fetch_ref, s32[256]{0:T(256)S(1)} %reshape.39.mask_ref, bf16[16,400,128]{2,1,0:T(8,128)(2,1)S(1)} %all-to-all-done.in_ref), custom_call_target="tpu_custom_call" | custom-call | flops 10000000000 | bytes 4194304 | tf_op jit(solution)/shard_map/pallas_call | solution.py:233
  60.3 8.5 %all-to-all-start.1 = ((bf16[16,64,128]{2,1,0:T(8,128)(2,1)}), bf16[16,64,128]{2,1,0:T(8,128)(2,1)S(1)}, u32[]{:S(2)}, u32[]{:S(2)}) async-start(bf16[16,64,128]{2,1,0:T(8,128)(2,1)} %get-tuple-element.17), calls=%async_computation.1 | async-start | bytes 524288 | tf_op jit(solution)/shard_map/all_to_all | solution.py:281
  68.8 17.6 %shard_map.112 = bf16[16,320,128]{2,1,0:T(8,128)(2,1)} custom-call(s32[256]{0:T(256)S(1)} %reshape.35.fetch_ref, s32[256]{0:T(256)S(1)} %reshape.39.mask_ref, bf16[16,400,128]{2,1,0:T(8,128)(2,1)S(1)} %all-to-all-done.in_ref, f32[16,8,128]{2,1,0:T(8,128)S(1)} %get-tuple-element.18.stat_ref), custom_call_target="tpu_custom_call" | custom-call | flops 20000000000 | bytes 4194304 | tf_op jit(solution)/shard_map/pallas_call | solution.py:233
  86.5 7.7 %all-to-all-start.2 = ((bf16[16,320,128]{2,1,0:T(8,128)(2,1)}), bf16[16,320,128]{2,1,0:T(8,128)(2,1)S(1)}, u32[]{:S(2)}, u32[]{:S(2)}) async-start(bf16[16,320,128]{2,1,0:T(8,128)(2,1)} %shard_map.112), calls=%async_computation.2 | async-start | bytes 2621440 | tf_op jit(solution)/shard_map/all_to_all | solution.py:281
  94.2 0.9 copy-done.3
  95.1 1.7 %shard_map.113 = (bf16[256,1024]{1,0:T(8,128)(2,1)}, bf16[4,4,4,16,256]{4,3,2,1,0:T(8,128)(2,1)S(1)}, bf16[4,4,4,16,256]{4,3,2,1,0:T(8,128)(2,1)}) custom-call(s32[1]{0:T(128)} %bitcast.core_ref, bf16[16,64,128]{2,1,0:T(8,128)(2,1)S(1)} %copy-done.3, bf16[256,1024]{1,0:T(8,128)(2,1)S(1)} %bitcast.34, bf16[512,1024]{1,0:T(8,128)(2,1)S(1)} %copy-done), custom_call_target="tpu_custom_call" | custom-call | flops 1000000000 | bytes 4194304 | tf_op jit(solution)/shard_map/pallas_call | solution.py:233
  96.8 1.9 %collective-permute-start = (bf16[4,4,4,16,256]{4,3,2,1,0:T(8,128)(2,1)}, bf16[4,4,4,16,256]{4,3,2,1,0:T(8,128)(2,1)S(1)}, u32[]{:S(2)}, u32[]{:S(2)}) collective-permute-start(bf16[4,4,4,16,256]{4,3,2,1,0:T(8,128)(2,1)} %get-tuple-element.22), channel_id=1, source_target_pairs={{0,16},{16,0},{32,48},{48,32},{64,80},{80,64},{96,112},{112,96},{1... | collective-permute-start | bytes 1572872 | tf_op jit(solution)/shard_map/ppermute | solution.py:327
  98.8 2.0 %collective-permute-done = bf16[4,4,4,16,256]{4,3,2,1,0:T(8,128)(2,1)S(1)} collective-permute-done((bf16[4,4,4,16,256]{4,3,2,1,0:T(8,128)(2,1)}, bf16[4,4,4,16,256]{4,3,2,1,0:T(8,128)(2,1)S(1)}, u32[]{:S(2)}, u32[]{:S(2)}) %collective-permute-start) | collective-permute-done | bytes 524320 | tf_op jit(solution)/shard_map/ppermute | solution.py:327
  101.0 2.7 %collective-permute-start.1 = (bf16[2,4,4,16,256]{4,3,2,1,0:T(8,128)(2,1)S(1)}, bf16[2,4,4,16,256]{4,3,2,1,0:T(8,128)(2,1)S(1)}, u32[]{:S(2)}, u32[]{:S(2)}) collective-permute-start(bf16[2,4,4,16,256]{4,3,2,1,0:T(8,128)(2,1)S(1)} %dynamic-slice_bitcast_fusion), channel_id=1, source_target_pairs={{0,128},{16,144},{32,160},{48,176},{64,192},{80,208},{96,224},{112... | collective-permute-start | bytes 786440 | tf_op jit(solution)/shard_map/ppermute | solution.py:294
  103.8 7.5 %collective-permute-done.1 = bf16[2,4,4,16,256]{4,3,2,1,0:T(8,128)(2,1)S(1)} collective-permute-done((bf16[2,4,4,16,256]{4,3,2,1,0:T(8,128)(2,1)S(1)}, bf16[2,4,4,16,256]{4,3,2,1,0:T(8,128)(2,1)S(1)}, u32[]{:S(2)}, u32[]{:S(2)}) %collective-permute-start.1) | collective-permute-done | bytes 262176 | tf_op jit(solution)/shard_map/ppermute | solution.py:294
  111.4 2.3 %collective-permute-start.2 = (bf16[4,4,16,256]{3,2,1,0:T(8,128)(2,1)S(1)}, bf16[4,4,16,256]{3,2,1,0:T(8,128)(2,1)S(1)}, u32[]{:S(2)}, u32[]{:S(2)}) collective-permute-start(bf16[4,4,16,256]{3,2,1,0:T(8,128)(2,1)S(1)} %dynamic-slice_bitcast_fusion.1), channel_id=1, source_target_pairs={{0,384},{16,400},{32,416},{48,432},{64,448},{80,464},{96,480},{112... | collective-permute-start | bytes 393224 | tf_op jit(solution)/shard_map/ppermute | solution.py:294
  113.8 5.7 %collective-permute-done.2 = bf16[4,4,16,256]{3,2,1,0:T(8,128)(2,1)S(1)} collective-permute-done((bf16[4,4,16,256]{3,2,1,0:T(8,128)(2,1)S(1)}, bf16[4,4,16,256]{3,2,1,0:T(8,128)(2,1)S(1)}, u32[]{:S(2)}, u32[]{:S(2)}) %collective-permute-start.2) | collective-permute-done | bytes 131104 | tf_op jit(solution)/shard_map/ppermute | solution.py:294
  119.5 3.8 %collective-permute-start.3 = (bf16[2,4,16,256]{3,2,1,0:T(8,128)(2,1)S(1)}, bf16[2,4,16,256]{3,2,1,0:T(8,128)(2,1)S(1)}, u32[]{:S(2)}, u32[]{:S(2)}) collective-permute-start(bf16[2,4,16,256]{3,2,1,0:T(8,128)(2,1)S(1)} %dynamic-slice_bitcast_fusion.2), channel_id=1, source_target_pairs={{0,1},{1,0},{2,3},{3,2},{4,5},{5,4},{6,7},{7,6},{8,9},{9,8},{10,11... | collective-permute-start | bytes 196616 | tf_op jit(solution)/shard_map/ppermute | solution.py:294
  123.4 2.3 %collective-permute-done.3 = bf16[2,4,16,256]{3,2,1,0:T(8,128)(2,1)S(1)} collective-permute-done((bf16[2,4,16,256]{3,2,1,0:T(8,128)(2,1)S(1)}, bf16[2,4,16,256]{3,2,1,0:T(8,128)(2,1)S(1)}, u32[]{:S(2)}, u32[]{:S(2)}) %collective-permute-start.3) | collective-permute-done | bytes 65568 | tf_op jit(solution)/shard_map/ppermute | solution.py:294
  125.7 5.0 %collective-permute-start.4 = (bf16[4,16,256]{2,1,0:T(8,128)(2,1)S(1)}, bf16[4,16,256]{2,1,0:T(8,128)(2,1)S(1)}, u32[]{:S(2)}, u32[]{:S(2)}) collective-permute-start(bf16[4,16,256]{2,1,0:T(8,128)(2,1)S(1)} %dynamic-slice_bitcast_fusion.3), channel_id=1, source_target_pairs={{0,3},{1,2},{2,1},{3,0},{4,7},{5,6},{6,5},{7,4},{8,11},{9,10},{10,... | collective-permute-start | bytes 98312 | tf_op jit(solution)/shard_map/ppermute | solution.py:294
  130.7 2.0 %collective-permute-done.4 = bf16[4,16,256]{2,1,0:T(8,128)(2,1)S(1)} collective-permute-done((bf16[4,16,256]{2,1,0:T(8,128)(2,1)S(1)}, bf16[4,16,256]{2,1,0:T(8,128)(2,1)S(1)}, u32[]{:S(2)}, u32[]{:S(2)}) %collective-permute-start.4) | collective-permute-done | bytes 32800 | tf_op jit(solution)/shard_map/ppermute | solution.py:294
  132.9 0.7 reshape.51
  133.6 13.0 %all-to-all-start.3 = ((bf16[16,2,512]{2,1,0:T(2,128)(2,1)}), bf16[16,2,512]{2,1,0:T(2,128)(2,1)S(1)}, u32[]{:S(2)}, u32[]{:S(2)}) async-start(bf16[16,2,512]{2,1,0:T(2,128)(2,1)} %reshape.51), calls=%async_computation.3 | async-start | bytes 65536 | tf_op jit(solution)/shard_map/all_to_all | solution.py:339
  146.5 1.3 shard_map.114
  147.9 11.3 %all-to-all-done.3 = bf16[16,2,512]{2,1,0:T(2,128)(2,1)S(1)} async-done(((bf16[16,2,512]{2,1,0:T(2,128)(2,1)}), bf16[16,2,512]{2,1,0:T(2,128)(2,1)S(1)}, u32[]{:S(2)}, u32[]{:S(2)}) %all-to-all-start.3) | async-done | bytes 32800 | tf_op jit(solution)/shard_map/all_to_all | solution.py:339
  159.3 0.6 broadcast_multiply_fusion
  (27 shorter events, 0.8 us)
Async XLA Ops:
  4.0 8.8 %copy-start.4 = (s32[1,16,16]{2,1,0:T(8,128)S(1)}, s32[1,16,16]{2,1,0:T(8,128)}, u32[]{:S(2)}) copy-start(s32[1,16,16]{2,1,0:T(8,128)} %param.12) | copy-start | bytes 3076
  4.0 43.8 %all-to-all-start = ((bf16[16,400,128]{2,1,0:T(8,128)(2,1)}), bf16[16,400,128]{2,1,0:T(8,128)(2,1)S(1)}, u32[]{:S(2)}, u32[]{:S(2)}) async-start(bf16[16,400,128]{2,1,0:T(8,128)(2,1)} %shard_map.110), calls=%async_computation | async-start | bytes 3276800 | tf_op jit(solution)/shard_map/all_to_all | solution.py:281
  60.3 26.2 %all-to-all-start.1 = ((bf16[16,64,128]{2,1,0:T(8,128)(2,1)}), bf16[16,64,128]{2,1,0:T(8,128)(2,1)S(1)}, u32[]{:S(2)}, u32[]{:S(2)}) async-start(bf16[16,64,128]{2,1,0:T(8,128)(2,1)} %get-tuple-element.17), calls=%async_computation.1 | async-start | bytes 524288 | tf_op jit(solution)/shard_map/all_to_all | solution.py:281
  86.4 7.7 %copy-start = (bf16[512,1024]{1,0:T(8,128)(2,1)S(1)}, bf16[512,1024]{1,0:T(8,128)(2,1)}, u32[]{:S(2)}) copy-start(bf16[512,1024]{1,0:T(8,128)(2,1)} %w_ref.3) | copy-start | bytes 3145732
  86.4 7.7 %copy-start.1 = (bf16[1,1,256,1024]{3,2,1,0:T(8,128)(2,1)S(1)}, bf16[1,1,256,1024]{3,2,1,0:T(8,128)(2,1)}, u32[]{:S(2)}) copy-start(bf16[1,1,256,1024]{3,2,1,0:T(8,128)(2,1)} %param.10) | copy-start | bytes 1572868
  86.4 7.7 %copy-start.2 = (bf16[16,64,128]{2,1,0:T(8,128)(2,1)}, bf16[16,64,128]{2,1,0:T(8,128)(2,1)S(1)}, u32[]{:S(2)}) copy-start(bf16[16,64,128]{2,1,0:T(8,128)(2,1)S(1)} %all-to-all-done.1.in_ref) | copy-start | bytes 786436
  86.5 46.3 %all-to-all-start.2 = ((bf16[16,320,128]{2,1,0:T(8,128)(2,1)}), bf16[16,320,128]{2,1,0:T(8,128)(2,1)S(1)}, u32[]{:S(2)}, u32[]{:S(2)}) async-start(bf16[16,320,128]{2,1,0:T(8,128)(2,1)} %shard_map.112), calls=%async_computation.2 | async-start | bytes 2621440 | tf_op jit(solution)/shard_map/all_to_all | solution.py:281
  94.2 1.0 copy-start.3
  96.8 4.0 %collective-permute-start = (bf16[4,4,4,16,256]{4,3,2,1,0:T(8,128)(2,1)}, bf16[4,4,4,16,256]{4,3,2,1,0:T(8,128)(2,1)S(1)}, u32[]{:S(2)}, u32[]{:S(2)}) collective-permute-start(bf16[4,4,4,16,256]{4,3,2,1,0:T(8,128)(2,1)} %get-tuple-element.22), channel_id=1, source_target_pairs={{0,16},{16,0},{32,48},{48,32},{64,80},{80,64},{96,112},{112,96},{1... | collective-permute-start | bytes 1572872 | tf_op jit(solution)/shard_map/ppermute | solution.py:327
  101.0 10.2 %collective-permute-start.1 = (bf16[2,4,4,16,256]{4,3,2,1,0:T(8,128)(2,1)S(1)}, bf16[2,4,4,16,256]{4,3,2,1,0:T(8,128)(2,1)S(1)}, u32[]{:S(2)}, u32[]{:S(2)}) collective-permute-start(bf16[2,4,4,16,256]{4,3,2,1,0:T(8,128)(2,1)S(1)} %dynamic-slice_bitcast_fusion), channel_id=1, source_target_pairs={{0,128},{16,144},{32,160},{48,176},{64,192},{80,208},{96,224},{112... | collective-permute-start | bytes 786440 | tf_op jit(solution)/shard_map/ppermute | solution.py:294
  111.4 8.1 %collective-permute-start.2 = (bf16[4,4,16,256]{3,2,1,0:T(8,128)(2,1)S(1)}, bf16[4,4,16,256]{3,2,1,0:T(8,128)(2,1)S(1)}, u32[]{:S(2)}, u32[]{:S(2)}) collective-permute-start(bf16[4,4,16,256]{3,2,1,0:T(8,128)(2,1)S(1)} %dynamic-slice_bitcast_fusion.1), channel_id=1, source_target_pairs={{0,384},{16,400},{32,416},{48,432},{64,448},{80,464},{96,480},{112... | collective-permute-start | bytes 393224 | tf_op jit(solution)/shard_map/ppermute | solution.py:294
  119.5 6.2 %collective-permute-start.3 = (bf16[2,4,16,256]{3,2,1,0:T(8,128)(2,1)S(1)}, bf16[2,4,16,256]{3,2,1,0:T(8,128)(2,1)S(1)}, u32[]{:S(2)}, u32[]{:S(2)}) collective-permute-start(bf16[2,4,16,256]{3,2,1,0:T(8,128)(2,1)S(1)} %dynamic-slice_bitcast_fusion.2), channel_id=1, source_target_pairs={{0,1},{1,0},{2,3},{3,2},{4,5},{5,4},{6,7},{7,6},{8,9},{9,8},{10,11... | collective-permute-start | bytes 196616 | tf_op jit(solution)/shard_map/ppermute | solution.py:294
  125.7 7.0 %collective-permute-start.4 = (bf16[4,16,256]{2,1,0:T(8,128)(2,1)S(1)}, bf16[4,16,256]{2,1,0:T(8,128)(2,1)S(1)}, u32[]{:S(2)}, u32[]{:S(2)}) collective-permute-start(bf16[4,16,256]{2,1,0:T(8,128)(2,1)S(1)} %dynamic-slice_bitcast_fusion.3), channel_id=1, source_target_pairs={{0,3},{1,2},{2,1},{3,0},{4,7},{5,6},{6,5},{7,4},{8,11},{9,10},{10,... | collective-permute-start | bytes 98312 | tf_op jit(solution)/shard_map/ppermute | solution.py:294
  133.6 25.6 %all-to-all-start.3 = ((bf16[16,2,512]{2,1,0:T(2,128)(2,1)}), bf16[16,2,512]{2,1,0:T(2,128)(2,1)S(1)}, u32[]{:S(2)}, u32[]{:S(2)}) async-start(bf16[16,2,512]{2,1,0:T(2,128)(2,1)} %reshape.51), calls=%async_computation.3 | async-start | bytes 65536 | tf_op jit(solution)/shard_map/all_to_all | solution.py:339

commit v6 on v3

--- a/solution.py
+++ b/solution.py
@@ -325,9 +325,16 @@
     term = (mine.astype(F32) + other.astype(F32)).astype(BF)
     term = ring_sum(term, "scene", scenes, X, ZHI * CORES).astype(BF)
     term = ring_sum(term, "view", VIEWS, Y, 1).astype(BF)
-    term = ring_sum(term, "scene", scenes, ZHI, CORES).astype(BF)
+    term, home = lax.optimization_barrier((term, home))
+    by_zhi = [
+        [(x * ZHI + z) * CORES + k for z in range(ZHI)] for x in range(X) for k in range(CORES)
+    ]
+    term = lax.all_to_all(term, "scene", 0, 0, tiled=True, axis_index_groups=by_zhi)
+    term = jnp.sum(term.astype(F32), axis=0).astype(BF)
     term = term.reshape(own, ZLO, COLS).transpose(1, 0, 2)
-    share = ring_sum(term, "view", VIEWS, ZLO, Y) * float(scenes * VIEWS * TOK) ** (-0.5)
+    by_zlo = [[z * Y + y for z in range(ZLO)] for y in range(Y)]
+    term = lax.all_to_all(term, "view", 0, 0, tiled=True, axis_index_groups=by_zlo)
+    share = jnp.sum(term.astype(F32), axis=0) * float(scenes * VIEWS * TOK) ** (-0.5)
     gq, gk, gv = call(unpack_kernel, (shape(TOK, INNER),) * 3, (home,))
     return (layer[None, None], gq[None, None], gk[None, None], gv[None, None], share)
 

time: 174 us -> 168 us (0.966)
  starting transfers between devices: 80.4 us -> 51.3 us
  blocking collectives: 0 us -> 25.3 us
  waiting for transfers between devices: 51.7 us -> 49.5 us
    ppermute x12 -> x6, starting transfers between devices: 53.6 us -> 20.3 us  [ring_sum(): total = total + lax.ppermute(send, axis, pairs).astype(F32)]
    all_to_all x0 -> x1, blocking collectives: none -> 25.3 us  [on_device(): lax.all_to_all(term, 'scene', 0, 0, tiled=True, axis_index_groups=by_zhi)]
    ppermute x12 -> x6, waiting for transfers between devices: 14.8 us -> 8.3 us  [ring_sum(): total = total + lax.ppermute(send, axis, pairs).astype(F32)]
    all_to_all x0 -> x1, waiting for transfers between devices: none -> 4.26 us  [on_device(): lax.all_to_all(term, 'view', 0, 0, tiled=True, axis_index_groups=by_zlo)]
    all_to_all x0 -> x1, starting transfers between devices: none -> 4.1 us  [on_device(): lax.all_to_all(term, 'view', 0, 0, tiled=True, axis_index_groups=by_zlo)]
  transfers between devices with their start and end apart: 16 -> 11, of which waited for: 8 -> 7; matrix products, arithmetic and copies ran while one was open for 1% -> 0% of each run, Pallas kernels for 11% -> 12%
where the time goes in v6:
time: 168 us; the launch traced here: 166 us
  starting transfers between devices  51.3 us (31%)
  waiting for transfers between devices  49.5 us (29%)
  Pallas kernels  36.4 us (22%)
  blocking collectives  25.3 us (15%)
  local copies, waits for them, and re-layouts  2.05 us (1%)
    pallas_call x5, Pallas kernels, call(): pl.pallas_call(kernel, out_shape=outs, in_specs=[SMEM] * smem + [VMEM] *...  36.4 us
    all_to_all x3, waiting for transfers between devices, swap(): return lax.all_to_all(rows, axis, split_axis=0, concat_axis=0, tiled=True)  34.9 us
    all_to_all x1, blocking collectives, on_device(): lax.all_to_all(term, 'scene', 0, 0, tiled=True, axis_index_groups=by_zhi)  25.3 us
    all_to_all x3, starting transfers between devices, swap(): return lax.all_to_all(rows, axis, split_axis=0, concat_axis=0, tiled=True)  24.9 us
    ppermute x6, starting transfers between devices, ring_sum(): total = total + lax.ppermute(send, axis, pairs).astype(F32)  20.3 us
    ppermute x6, waiting for transfers between devices, ring_sum(): total = total + lax.ppermute(send, axis, pairs).astype(F32)  8.3 us
    all_to_all x1, waiting for transfers between devices, on_device(): lax.all_to_all(term, 'view', 0, 0, tiled=True, axis_index_groups=by_zlo)  4.26 us
    all_to_all x1, starting transfers between devices, on_device(): lax.all_to_all(term, 'view', 0, 0, tiled=True, axis_index_groups=by_zlo)  4.1 us
  transfers between devices with their start and end apart: 11, of which 7 were waited for; matrix products, arithmetic and copies ran while one was open for 0% of the time, Pallas kernels for 12%

profile of v6, /device:TPU:6, one launch (start us, length us, event | category | flops | bytes accessed | tf_op | source)
XLA Modules:
  0.0 166.4 jit_solution(849626345345408823)
XLA Ops:
  0.6 3.4 %shard_map.110 = bf16[16,400,128]{2,1,0:T(8,128)(2,1)} custom-call(bf16[256,512]{1,0:T(8,128)(2,1)} %bitcast.31, bf16[256,512]{1,0:T(8,128)(2,1)} %bitcast.32, bf16[256,512]{1,0:T(8,128)(2,1)} %bitcast.33, bf16[256,1024]{1,0:T(8,128)(2,1)} %bitcast.29, bf16[512,1024]{1,0:T(8,128)(2,1)} %w_ref.3, s32[2,16]{1,0:T(2,128)} %bitcast.35), custom_call_target="tpu_custom_call" | custom-call | bytes 4194304 | tf_op jit(solution)/shard_map/pallas_call | solution.py:232
  4.0 8.8 %all-to-all-start = ((bf16[16,400,128]{2,1,0:T(8,128)(2,1)}), bf16[16,400,128]{2,1,0:T(8,128)(2,1)S(1)}, u32[]{:S(2)}, u32[]{:S(2)}) async-start(bf16[16,400,128]{2,1,0:T(8,128)(2,1)} %shard_map.110), calls=%async_computation | async-start | bytes 3276800 | tf_op jit(solution)/shard_map/all_to_all | solution.py:280
  12.9 34.9 %all-to-all-done.in_ref = bf16[16,400,128]{2,1,0:T(8,128)(2,1)S(1)} async-done(((bf16[16,400,128]{2,1,0:T(8,128)(2,1)}), bf16[16,400,128]{2,1,0:T(8,128)(2,1)S(1)}, u32[]{:S(2)}, u32[]{:S(2)}) %all-to-all-start) | async-done | bytes 1638432 | tf_op jit(solution)/shard_map/all_to_all | solution.py:280
  47.9 12.3 %shard_map.111 = (bf16[16,64,128]{2,1,0:T(8,128)(2,1)}, f32[16,8,128]{2,1,0:T(8,128)S(1)}) custom-call(s32[256]{0:T(256)S(1)} %reshape.24.fetch_ref, s32[256]{0:T(256)S(1)} %reshape.26.mask_ref, bf16[16,400,128]{2,1,0:T(8,128)(2,1)S(1)} %all-to-all-done.in_ref), custom_call_target="tpu_custom_call" | custom-call | flops 10000000000 | bytes 4194304 | tf_op jit(solution)/shard_map/pallas_call | solution.py:232
  60.3 8.5 %all-to-all-start.1 = ((bf16[16,64,128]{2,1,0:T(8,128)(2,1)}), bf16[16,64,128]{2,1,0:T(8,128)(2,1)S(1)}, u32[]{:S(2)}, u32[]{:S(2)}) async-start(bf16[16,64,128]{2,1,0:T(8,128)(2,1)} %get-tuple-element.17), calls=%async_computation.1 | async-start | bytes 524288 | tf_op jit(solution)/shard_map/all_to_all | solution.py:280
  68.8 17.6 %shard_map.112 = bf16[16,320,128]{2,1,0:T(8,128)(2,1)} custom-call(s32[256]{0:T(256)S(1)} %reshape.24.fetch_ref, s32[256]{0:T(256)S(1)} %reshape.26.mask_ref, bf16[16,400,128]{2,1,0:T(8,128)(2,1)S(1)} %all-to-all-done.in_ref, f32[16,8,128]{2,1,0:T(8,128)S(1)} %get-tuple-element.18.stat_ref), custom_call_target="tpu_custom_call" | custom-call | flops 20000000000 | bytes 4194304 | tf_op jit(solution)/shard_map/pallas_call | solution.py:232
  86.5 7.7 %all-to-all-start.2 = ((bf16[16,320,128]{2,1,0:T(8,128)(2,1)}), bf16[16,320,128]{2,1,0:T(8,128)(2,1)S(1)}, u32[]{:S(2)}, u32[]{:S(2)}) async-start(bf16[16,320,128]{2,1,0:T(8,128)(2,1)} %shard_map.112), calls=%async_computation.2 | async-start | bytes 2621440 | tf_op jit(solution)/shard_map/all_to_all | solution.py:280
  95.1 1.7 %shard_map.113 = (bf16[256,1024]{1,0:T(8,128)(2,1)}, bf16[4,4,4,16,256]{4,3,2,1,0:T(8,128)(2,1)S(1)}, bf16[4,4,4,16,256]{4,3,2,1,0:T(8,128)(2,1)}) custom-call(s32[1]{0:T(128)} %bitcast.core_ref, bf16[16,64,128]{2,1,0:T(8,128)(2,1)S(1)} %copy-done.3, bf16[256,1024]{1,0:T(8,128)(2,1)S(1)} %bitcast.30, bf16[512,1024]{1,0:T(8,128)(2,1)S(1)} %copy-done), custom_call_target="tpu_custom_call" | custom-call | flops 1000000000 | bytes 4194304 | tf_op jit(solution)/shard_map/pallas_call | solution.py:232
  96.8 1.9 %collective-permute-start = (bf16[4,4,4,16,256]{4,3,2,1,0:T(8,128)(2,1)}, bf16[4,4,4,16,256]{4,3,2,1,0:T(8,128)(2,1)S(1)}, u32[]{:S(2)}, u32[]{:S(2)}) collective-permute-start(bf16[4,4,4,16,256]{4,3,2,1,0:T(8,128)(2,1)} %get-tuple-element.22), channel_id=1, source_target_pairs={{0,16},{16,0},{32,48},{48,32},{64,80},{80,64},{96,112},{112,96},{1... | collective-permute-start | bytes 1572872 | tf_op jit(solution)/shard_map/ppermute | solution.py:324
  98.8 2.0 %collective-permute-done = bf16[4,4,4,16,256]{4,3,2,1,0:T(8,128)(2,1)S(1)} collective-permute-done((bf16[4,4,4,16,256]{4,3,2,1,0:T(8,128)(2,1)}, bf16[4,4,4,16,256]{4,3,2,1,0:T(8,128)(2,1)S(1)}, u32[]{:S(2)}, u32[]{:S(2)}) %collective-permute-start) | collective-permute-done | bytes 524320 | tf_op jit(solution)/shard_map/ppermute | solution.py:324
  101.0 2.7 %collective-permute-start.3 = (bf16[4,4,16,256]{3,2,1,0:T(8,128)(2,1)S(1)}, bf16[4,4,16,256]{3,2,1,0:T(8,128)(2,1)S(1)}, u32[]{:S(2)}, u32[]{:S(2)}) collective-permute-start(bf16[4,4,16,256]{3,2,1,0:T(8,128)(2,1)S(1)} %get-tuple-element.30), channel_id=1, source_target_pairs={{0,384},{16,400},{32,416},{48,432},{64,448},{80,464},{96,480},{112... | collective-permute-start | bytes 393224 | tf_op jit(solution)/shard_map/ppermute | solution.py:292
  103.7 3.0 %collective-permute-start.2 = (bf16[4,4,16,256]{3,2,1,0:T(8,128)(2,1)S(1)}, bf16[4,4,16,256]{3,2,1,0:T(8,128)(2,1)S(1)}, u32[]{:S(2)}, u32[]{:S(2)}) collective-permute-start(bf16[4,4,16,256]{3,2,1,0:T(8,128)(2,1)S(1)} %get-tuple-element.31), channel_id=1, source_target_pairs={{0,256},{16,272},{32,288},{48,304},{64,320},{80,336},{96,352},{112... | collective-permute-start | bytes 393224 | tf_op jit(solution)/shard_map/ppermute | solution.py:292
  106.8 4.0 %collective-permute-start.1 = (bf16[4,4,16,256]{3,2,1,0:T(8,128)(2,1)S(1)}, bf16[4,4,16,256]{3,2,1,0:T(8,128)(2,1)S(1)}, u32[]{:S(2)}, u32[]{:S(2)}) collective-permute-start(bf16[4,4,16,256]{3,2,1,0:T(8,128)(2,1)S(1)} %get-tuple-element.29), channel_id=1, source_target_pairs={{0,128},{16,144},{32,160},{48,176},{64,192},{80,208},{96,224},{112... | collective-permute-start | bytes 393224 | tf_op jit(solution)/shard_map/ppermute | solution.py:292
  110.9 1.6 collective-permute-done.2
  112.5 2.5 %collective-permute-done.1 = bf16[4,4,16,256]{3,2,1,0:T(8,128)(2,1)S(1)} collective-permute-done((bf16[4,4,16,256]{3,2,1,0:T(8,128)(2,1)S(1)}, bf16[4,4,16,256]{3,2,1,0:T(8,128)(2,1)S(1)}, u32[]{:S(2)}, u32[]{:S(2)}) %collective-permute-start.1) | collective-permute-done | bytes 131104 | tf_op jit(solution)/shard_map/ppermute | solution.py:292
  115.1 5.0 %collective-permute-start.6 = (bf16[4,16,256]{2,1,0:T(8,128)(2,1)S(1)}, bf16[4,16,256]{2,1,0:T(8,128)(2,1)S(1)}, u32[]{:S(2)}, u32[]{:S(2)}) collective-permute-start(bf16[4,16,256]{2,1,0:T(8,128)(2,1)S(1)} %get-tuple-element.33), channel_id=1, source_target_pairs={{0,3},{1,0},{2,1},{3,2},{4,7},{5,4},{6,5},{7,6},{8,11},{9,8},{10,9... | collective-permute-start | bytes 98312 | tf_op jit(solution)/shard_map/ppermute | solution.py:292
  120.1 2.8 %collective-permute-start.5 = (bf16[4,16,256]{2,1,0:T(8,128)(2,1)S(1)}, bf16[4,16,256]{2,1,0:T(8,128)(2,1)S(1)}, u32[]{:S(2)}, u32[]{:S(2)}) collective-permute-start(bf16[4,16,256]{2,1,0:T(8,128)(2,1)S(1)} %get-tuple-element.34), channel_id=1, source_target_pairs={{0,2},{1,3},{2,0},{3,1},{4,6},{5,7},{6,4},{7,5},{8,10},{9,11},{10,... | collective-permute-start | bytes 98312 | tf_op jit(solution)/shard_map/ppermute | solution.py:292
  122.9 2.8 %collective-permute-start.4 = (bf16[4,16,256]{2,1,0:T(8,128)(2,1)S(1)}, bf16[4,16,256]{2,1,0:T(8,128)(2,1)S(1)}, u32[]{:S(2)}, u32[]{:S(2)}) collective-permute-start(bf16[4,16,256]{2,1,0:T(8,128)(2,1)S(1)} %get-tuple-element.32), channel_id=1, source_target_pairs={{0,1},{1,2},{2,3},{3,0},{4,5},{5,6},{6,7},{7,4},{8,9},{9,10},{10,1... | collective-permute-start | bytes 98312 | tf_op jit(solution)/shard_map/ppermute | solution.py:292
  125.7 2.1 %collective-permute-done.5 = bf16[4,16,256]{2,1,0:T(8,128)(2,1)S(1)} collective-permute-done((bf16[4,16,256]{2,1,0:T(8,128)(2,1)S(1)}, bf16[4,16,256]{2,1,0:T(8,128)(2,1)S(1)}, u32[]{:S(2)}, u32[]{:S(2)}) %collective-permute-start.5) | collective-permute-done | bytes 32800 | tf_op jit(solution)/shard_map/ppermute | solution.py:292
  127.7 2.1 %collective-permute-done.4 = bf16[4,16,256]{2,1,0:T(8,128)(2,1)S(1)} collective-permute-done((bf16[4,16,256]{2,1,0:T(8,128)(2,1)S(1)}, bf16[4,16,256]{2,1,0:T(8,128)(2,1)S(1)}, u32[]{:S(2)}, u32[]{:S(2)}) %collective-permute-start.4) | collective-permute-done | bytes 32800 | tf_op jit(solution)/shard_map/ppermute | solution.py:292
  129.9 25.3 %all_to_all.25 = bf16[4,16,256]{2,1,0:T(8,128)(2,1)S(1)} all-to-all(bf16[4,16,256]{2,1,0:T(8,128)(2,1)S(1)} %fusion.5), channel_id=1, replica_groups={{0,32,64,96},{16,48,80,112},{128,160,192,224},{144,176,208,240},{256,28..., dimensions={0} | all-to-all | bytes 65536 | tf_op jit(solution)/shard_map/all_to_all | solution.py:332
  156.0 4.1 %all-to-all-start.4 = ((bf16[4,2,512]{2,1,0:T(2,128)(2,1)}), bf16[4,2,512]{2,1,0:T(2,128)(2,1)S(1)}, u32[]{:S(2)}, u32[]{:S(2)}) async-start(bf16[4,2,512]{2,1,0:T(2,128)(2,1)} %reshape.36), calls=%async_computation.4 | async-start | bytes 16384 | tf_op jit(solution)/shard_map/all_to_all | solution.py:336
  160.1 1.3 shard_map.114
  161.4 4.3 %all-to-all-done.4 = bf16[4,2,512]{2,1,0:T(2,128)(2,1)S(1)} async-done(((bf16[4,2,512]{2,1,0:T(2,128)(2,1)}), bf16[4,2,512]{2,1,0:T(2,128)(2,1)S(1)}, u32[]{:S(2)}, u32[]{:S(2)}) %all-to-all-start.4) | async-done | bytes 8224 | tf_op jit(solution)/shard_map/all_to_all | solution.py:336
  (29 shorter events, 3.0 us)
Async XLA Ops:
  4.0 8.8 %copy-start.4 = (s32[1,16,16]{2,1,0:T(8,128)S(1)}, s32[1,16,16]{2,1,0:T(8,128)}, u32[]{:S(2)}) copy-start(s32[1,16,16]{2,1,0:T(8,128)} %param.12) | copy-start | bytes 3076
  4.0 43.8 %all-to-all-start = ((bf16[16,400,128]{2,1,0:T(8,128)(2,1)}), bf16[16,400,128]{2,1,0:T(8,128)(2,1)S(1)}, u32[]{:S(2)}, u32[]{:S(2)}) async-start(bf16[16,400,128]{2,1,0:T(8,128)(2,1)} %shard_map.110), calls=%async_computation | async-start | bytes 3276800 | tf_op jit(solution)/shard_map/all_to_all | solution.py:280
  60.3 26.2 %all-to-all-start.1 = ((bf16[16,64,128]{2,1,0:T(8,128)(2,1)}), bf16[16,64,128]{2,1,0:T(8,128)(2,1)S(1)}, u32[]{:S(2)}, u32[]{:S(2)}) async-start(bf16[16,64,128]{2,1,0:T(8,128)(2,1)} %get-tuple-element.17), calls=%async_computation.1 | async-start | bytes 524288 | tf_op jit(solution)/shard_map/all_to_all | solution.py:280
  86.4 7.7 %copy-start = (bf16[512,1024]{1,0:T(8,128)(2,1)S(1)}, bf16[512,1024]{1,0:T(8,128)(2,1)}, u32[]{:S(2)}) copy-start(bf16[512,1024]{1,0:T(8,128)(2,1)} %w_ref.3) | copy-start | bytes 3145732
  86.4 7.7 %copy-start.1 = (bf16[1,1,256,1024]{3,2,1,0:T(8,128)(2,1)S(1)}, bf16[1,1,256,1024]{3,2,1,0:T(8,128)(2,1)}, u32[]{:S(2)}) copy-start(bf16[1,1,256,1024]{3,2,1,0:T(8,128)(2,1)} %param.10) | copy-start | bytes 1572868
  86.4 7.7 %copy-start.2 = (bf16[16,64,128]{2,1,0:T(8,128)(2,1)}, bf16[16,64,128]{2,1,0:T(8,128)(2,1)S(1)}, u32[]{:S(2)}) copy-start(bf16[16,64,128]{2,1,0:T(8,128)(2,1)S(1)} %all-to-all-done.1.in_ref) | copy-start | bytes 786436
  86.5 43.5 %all-to-all-start.2 = ((bf16[16,320,128]{2,1,0:T(8,128)(2,1)}), bf16[16,320,128]{2,1,0:T(8,128)(2,1)S(1)}, u32[]{:S(2)}, u32[]{:S(2)}) async-start(bf16[16,320,128]{2,1,0:T(8,128)(2,1)} %shard_map.112), calls=%async_computation.2 | async-start | bytes 2621440 | tf_op jit(solution)/shard_map/all_to_all | solution.py:280
  94.2 1.0 copy-start.3
  96.8 4.0 %collective-permute-start = (bf16[4,4,4,16,256]{4,3,2,1,0:T(8,128)(2,1)}, bf16[4,4,4,16,256]{4,3,2,1,0:T(8,128)(2,1)S(1)}, u32[]{:S(2)}, u32[]{:S(2)}) collective-permute-start(bf16[4,4,4,16,256]{4,3,2,1,0:T(8,128)(2,1)} %get-tuple-element.22), channel_id=1, source_target_pairs={{0,16},{16,0},{32,48},{48,32},{64,80},{80,64},{96,112},{112,96},{1... | collective-permute-start | bytes 1572872 | tf_op jit(solution)/shard_map/ppermute | solution.py:324
  101.0 9.9 %collective-permute-start.3 = (bf16[4,4,16,256]{3,2,1,0:T(8,128)(2,1)S(1)}, bf16[4,4,16,256]{3,2,1,0:T(8,128)(2,1)S(1)}, u32[]{:S(2)}, u32[]{:S(2)}) collective-permute-start(bf16[4,4,16,256]{3,2,1,0:T(8,128)(2,1)S(1)} %get-tuple-element.30), channel_id=1, source_target_pairs={{0,384},{16,400},{32,416},{48,432},{64,448},{80,464},{96,480},{112... | collective-permute-start | bytes 393224 | tf_op jit(solution)/shard_map/ppermute | solution.py:292
  103.7 8.7 %collective-permute-start.2 = (bf16[4,4,16,256]{3,2,1,0:T(8,128)(2,1)S(1)}, bf16[4,4,16,256]{3,2,1,0:T(8,128)(2,1)S(1)}, u32[]{:S(2)}, u32[]{:S(2)}) collective-permute-start(bf16[4,4,16,256]{3,2,1,0:T(8,128)(2,1)S(1)} %get-tuple-element.31), channel_id=1, source_target_pairs={{0,256},{16,272},{32,288},{48,304},{64,320},{80,336},{96,352},{112... | collective-permute-start | bytes 393224 | tf_op jit(solution)/shard_map/ppermute | solution.py:292
  106.8 8.2 %collective-permute-start.1 = (bf16[4,4,16,256]{3,2,1,0:T(8,128)(2,1)S(1)}, bf16[4,4,16,256]{3,2,1,0:T(8,128)(2,1)S(1)}, u32[]{:S(2)}, u32[]{:S(2)}) collective-permute-start(bf16[4,4,16,256]{3,2,1,0:T(8,128)(2,1)S(1)} %get-tuple-element.29), channel_id=1, source_target_pairs={{0,128},{16,144},{32,160},{48,176},{64,192},{80,208},{96,224},{112... | collective-permute-start | bytes 393224 | tf_op jit(solution)/shard_map/ppermute | solution.py:292
  115.1 10.6 %collective-permute-start.6 = (bf16[4,16,256]{2,1,0:T(8,128)(2,1)S(1)}, bf16[4,16,256]{2,1,0:T(8,128)(2,1)S(1)}, u32[]{:S(2)}, u32[]{:S(2)}) collective-permute-start(bf16[4,16,256]{2,1,0:T(8,128)(2,1)S(1)} %get-tuple-element.33), channel_id=1, source_target_pairs={{0,3},{1,0},{2,1},{3,2},{4,7},{5,4},{6,5},{7,6},{8,11},{9,8},{10,9... | collective-permute-start | bytes 98312 | tf_op jit(solution)/shard_map/ppermute | solution.py:292
  120.1 7.7 %collective-permute-start.5 = (bf16[4,16,256]{2,1,0:T(8,128)(2,1)S(1)}, bf16[4,16,256]{2,1,0:T(8,128)(2,1)S(1)}, u32[]{:S(2)}, u32[]{:S(2)}) collective-permute-start(bf16[4,16,256]{2,1,0:T(8,128)(2,1)S(1)} %get-tuple-element.34), channel_id=1, source_target_pairs={{0,2},{1,3},{2,0},{3,1},{4,6},{5,7},{6,4},{7,5},{8,10},{9,11},{10,... | collective-permute-start | bytes 98312 | tf_op jit(solution)/shard_map/ppermute | solution.py:292
  122.9 7.0 %collective-permute-start.4 = (bf16[4,16,256]{2,1,0:T(8,128)(2,1)S(1)}, bf16[4,16,256]{2,1,0:T(8,128)(2,1)S(1)}, u32[]{:S(2)}, u32[]{:S(2)}) collective-permute-start(bf16[4,16,256]{2,1,0:T(8,128)(2,1)S(1)} %get-tuple-element.32), channel_id=1, source_target_pairs={{0,1},{1,2},{2,3},{3,0},{4,5},{5,6},{6,7},{7,4},{8,9},{9,10},{10,1... | collective-permute-start | bytes 98312 | tf_op jit(solution)/shard_map/ppermute | solution.py:292
  156.0 9.7 %all-to-all-start.4 = ((bf16[4,2,512]{2,1,0:T(2,128)(2,1)}), bf16[4,2,512]{2,1,0:T(2,128)(2,1)S(1)}, u32[]{:S(2)}, u32[]{:S(2)}) async-start(bf16[4,2,512]{2,1,0:T(2,128)(2,1)} %reshape.36), calls=%async_computation.4 | async-start | bytes 16384 | tf_op jit(solution)/shard_map/all_to_all | solution.py:336

commit v7 on v4

v7 whole, which is shorter than its diff:
```python
import jax
import jax.numpy as jnp
from jax import lax
from jax.experimental import pallas as pl
from jax.experimental.pallas import tpu as pltpu
from jax.sharding import PartitionSpec as P

HEADS = 8
HEAD_DIM = 64
BLK = 128
TOK = 256
VIEWS = 16
INNER = 512
D = 1024
KEYS = TOK + VIEWS * BLK
WIDE = 2 * HEAD_DIM
COLS = D // VIEWS
BF = jnp.bfloat16
F32 = jnp.float32
SCALE = HEAD_DIM ** (-0.5)
SIDES = 2
PACK_ROWS = TOK + 16
CHUNK = 768
BACK_CHUNK = 256
BACK_ROWS = TOK + BLK
X, ZHI, CORES = 4, 4, 2
ZLO, Y = 4, 4
NT = (((1,), (1,)), ((), ()))
VMEM = pl.BlockSpec(memory_space=pltpu.VMEM)
SMEM = pl.BlockSpec(memory_space=pltpu.SMEM)


def pack_keys_kernel(k_ref, v_ref, out_ref):
    for h in range(HEADS):
        c = slice(h * HEAD_DIM, (h + 1) * HEAD_DIM)
        kv = jnp.concatenate([k_ref[:, c], v_ref[:, c]], axis=1)
        for u in range(SIDES):
            out_ref[u * HEADS + h, :, :] = kv


def pack_queries_kernel(q_ref, go_ref, w_ref, mask_ref, out_ref):
    ga = lax.dot_general(go_ref[...], w_ref[...], NT, preferred_element_type=F32).astype(BF)
    q = q_ref[...] * jnp.asarray(SCALE, BF)
    reads = jnp.concatenate(
        [jnp.broadcast_to(mask_ref[b : b + 1, :], (8, VIEWS)) for b in range(2)], axis=0
    ).astype(BF)
    for h in range(HEADS):
        c = slice(h * HEAD_DIM, (h + 1) * HEAD_DIM)
        out_ref[h, 0:TOK, :] = jnp.concatenate([q[:, c], ga[:, c]], axis=1)
        out_ref[h, TOK:PACK_ROWS, 0:VIEWS] = reads


def rows_of(v, w, fetch_ref):
    return pl.ds(pl.multiple_of(fetch_ref[v * VIEWS + w] * BLK, BLK), BLK)


def gather_rows(v, in_ref, dst, fetch_ref):
    dst[0:TOK, :] = in_ref[v, :, :]
    for w in range(VIEWS):
        dst[TOK + w * BLK : TOK + (w + 1) * BLK, :] = in_ref[w, rows_of(v, w, fetch_ref), :]


def gather_cols(v, src, dst, dims, fetch_ref):
    dst[dims, 0:TOK] = src[:, pl.ds(pl.multiple_of(v * TOK, TOK), TOK)]
    for w in range(VIEWS):
        at = pl.multiple_of(w * TOK + fetch_ref[v * VIEWS + w] * BLK, BLK)
        dst[dims, TOK + w * BLK : TOK + (w + 1) * BLK] = src[:, pl.ds(at, BLK)]


def masked(s, v, w, source, mask_ref):
    parts = []
    for b in range(2):
        seen = jnp.logical_and(mask_ref[(source * 2 + b) * VIEWS + w] == 1, w != v)
        parts.append(s[:, b * BLK : (b + 1) * BLK] + jnp.where(seen, 0.0, -jnp.inf))
    return jnp.concatenate(parts, axis=1)


def side_by_side(t):
    return jnp.concatenate([t[:, :BLK], t[:, BLK:]], axis=0).T


def halves(qg):
    lane = lax.broadcasted_iota(jnp.int32, (TOK, WIDE), 1)
    zero = jnp.zeros_like(qg)
    return jnp.where(lane < HEAD_DIM, qg, zero), jnp.where(lane >= HEAD_DIM, qg, zero)


def place_queries(place_ref, pieces, qg_ref):
    for d, piece in enumerate(pieces):
        at = lax.rem(place_ref[1] - d + HEADS, HEADS)
        qg_ref[at, :, :] = piece[0:TOK, :]


def forward_kernel(fetch_ref, mask_ref, place_ref, in_ref, *refs):
    attn_ref, stat_ref, qg_ref, vt, vsel, s_ref, e_ref, top_ref, kall = refs[HEADS:]
    place_queries(place_ref, refs[:HEADS], qg_ref)
    for w in range(VIEWS):
        vt[:, w * TOK : (w + 1) * TOK] = in_ref[w, :, :].T[HEAD_DIM:, :]
    vsel[0:HEAD_DIM, :] = jnp.ones((HEAD_DIM, KEYS), BF)

    def scores(i, slot):
        v = place_ref[0] + i
        source = lax.rem(place_ref[1] - i + HEADS, HEADS)
        qs = halves(qg_ref[i])[0]
        gather_rows(v, in_ref, kall.at[slot], fetch_ref)
        top = None
        for c in range(0, KEYS, CHUNK):
            r = lax.dot_general(
                kall[slot, c : c + CHUNK, :], qs, NT, preferred_element_type=F32
            )
            for b in range(0, CHUNK, BLK):
                s = r[b : b + BLK, :]
                w = (c + b - TOK) // BLK
                if w >= 0:
                    s = masked(s, v, w, source, mask_ref)
                s_ref[slot, c + b : c + b + BLK, :] = s
                best = jnp.max(s.reshape(BLK // 8, 8, TOK), axis=0)
                top = best if top is None else jnp.maximum(top, best)
        top_ref[slot, 0:1, :] = jnp.max(top, axis=0, keepdims=True)

    def output(i, slot):
        gather_cols(place_ref[0] + i, vt, vsel, slice(HEAD_DIM, WIDE), fetch_ref)
        top = top_ref[slot, 0:1, :]
        for c in range(KEYS // BLK):
            rows = slice(c * BLK, (c + 1) * BLK)
            e_ref[slot, rows, :] = jnp.exp(s_ref[slot, rows, :] - top).astype(BF)
        o = jnp.dot(vsel[...], e_ref[slot], preferred_element_type=F32)
        share = 1.0 / o[0:1, :]
        attn = o[HEAD_DIM:, :] * share
        attn_ref[i, :, :] = side_by_side(attn).astype(BF)
        delta = jnp.sum(attn * qg_ref[i].T[HEAD_DIM:, :].astype(F32), axis=0, keepdims=True)
        stat_ref[i, 0:1, :] = top
        stat_ref[i, 1:2, :] = share
        stat_ref[i, 2:3, :] = delta

    def two_views(n, carry):
        i = 2 * n
        scores(i + 1, 1)
        output(i, 0)
        scores(jnp.minimum(i + 2, HEADS - 1), 0)
        output(i + 1, 1)
        return carry

    scores(0, 0)
    lax.fori_loop(0, HEADS // 2, two_views, 0)


def backward_kernel(
    fetch_ref, mask_ref, place_ref, in_ref, qg_ref, stat_ref, out_ref, kt, ksel, x_ref, acc, kall, qg2_ref
):
    for w in range(VIEWS):
        kt[:, w * TOK : (w + 1) * TOK] = in_ref[w, :, :].T[:HEAD_DIM, :]
        acc[w] = jnp.zeros((TOK, WIDE), F32)
        out_ref[w, TOK:BACK_ROWS, :] = jnp.zeros((BLK, WIDE), BF)

    def weights(i, slot):
        v = place_ref[0] + i
        source = lax.rem(place_ref[1] - i + HEADS, HEADS)
        low, high = halves(qg_ref[i])
        qg2_ref[slot, 0:TOK, :] = low
        qg2_ref[slot, TOK:, :] = high
        qg2 = qg2_ref[slot]
        top = stat_ref[i, 0:1, :]
        share = stat_ref[i, 1:2, :]
        delta = stat_ref[i, 2:3, :]
        gather_rows(v, in_ref, kall.at[slot], fetch_ref)
        for c in range(0, KEYS, BACK_CHUNK):
            r = lax.dot_general(
                kall[slot, c : c + BACK_CHUNK, :], qg2, NT, preferred_element_type=F32
            )
            for b in range(0, BACK_CHUNK, BLK):
                rows = slice(c + b, c + b + BLK)
                s = r[b : b + BLK, 0:TOK]
                w = (c + b - TOK) // BLK
                if w >= 0:
                    s = masked(s, v, w, source, mask_ref)
                prob = jnp.exp(s - top) * share
                x_ref[slot, rows, 0:TOK] = (prob * (r[b : b + BLK, TOK:] - delta)).astype(BF)
                x_ref[slot, rows, TOK:] = prob.astype(BF)

    def sums(i, slot):
        v = place_ref[0] + i
        for c in range(0, KEYS, BACK_CHUNK):
            g = jnp.dot(
                x_ref[slot, c : c + BACK_CHUNK, :], qg2_ref[slot], preferred_element_type=F32
            )
            for b in range(0, BACK_CHUNK, BLK):
                w = (c + b - TOK) // BLK
                if w >= 0:
                    acc[w, rows_of(v, w, fetch_ref), :] += g[b : b + BLK, :]
                else:
                    acc[v, c + b : c + b + BLK, :] += g[b : b + BLK, :]
        gather_cols(v, kt, ksel, slice(0, HEAD_DIM), fetch_ref)
        o = jnp.dot(ksel[...], x_ref[slot, :, 0:TOK], preferred_element_type=F32) * SCALE
        out_ref[v, TOK:BACK_ROWS, :] = side_by_side(o).astype(BF)

    def two_views(n, carry):
        i = 2 * n
        weights(i + 1, 1)
        sums(i, 0)
        weights(jnp.minimum(i + 2, HEADS - 1), 0)
        sums(i + 1, 1)
        return carry

    weights(0, 0)
    lax.fori_loop(0, HEADS // 2, two_views, 0)
    for w in range(VIEWS):
        out_ref[w, 0:TOK, :] = acc[w].astype(BF)


def project_kernel(core_ref, in_ref, go_ref, w_ref, layer_ref, mine_ref, other_ref, attn, term):
    for h in range(HEADS):
        c = slice(h * HEAD_DIM, (h + 1) * HEAD_DIM)
        both = in_ref[h]
        attn[0:BLK, c] = both[:, :HEAD_DIM]
        attn[BLK:, c] = both[:, HEAD_DIM:]
    layer_ref[...] = jnp.dot(attn[...], w_ref[...], preferred_element_type=F32).astype(BF)
    cols = [(z * Y + y) * COLS for y in range(Y) for z in range(ZLO)]
    go = jnp.concatenate([go_ref[:, c : c + COLS] for c in cols], axis=1)
    term[...] = lax.dot_general(
        attn[...], go, (((0,), (0,)), ((), ())), preferred_element_type=F32
    ).astype(BF)
    core = core_ref[0]
    own = INNER // (X * ZHI * CORES)
    wide = ZLO * COLS
    for x in range(X):
        for side, ref in ((core, mine_ref), (1 - core, other_ref)):
            for z in range(ZHI):
                at = pl.multiple_of((x * ZHI + z) * CORES * own + side * own, own)
                rows = term[pl.ds(at, own), :]
                for y in range(Y):
                    ref[x, y, z, :, :] = rows[:, y * wide : (y + 1) * wide]


def unpack_kernel(place_ref, in_ref, gq_ref, gk_ref, gv_ref):
    for h in range(HEADS):
        c = slice(h * HEAD_DIM, (h + 1) * HEAD_DIM)
        kv = in_ref[h, 0:TOK, :].astype(F32) + in_ref[HEADS + h, 0:TOK, :].astype(F32)
        kv = kv.astype(BF)
        gk_ref[:, c] = kv[:, :HEAD_DIM]
        gv_ref[:, c] = kv[:, HEAD_DIM:]
        both = in_ref[place_ref[0] + h, TOK:BACK_ROWS, :]
        gq_ref[0:BLK, c] = both[:, :HEAD_DIM]
        gq_ref[BLK:, c] = both[:, HEAD_DIM:]


def shape(*dims, dtype=BF):
    return jax.ShapeDtypeStruct(dims, dtype)


def call(kernel, outs, args, smem=0, scratch=(), mib=28, flops=0):
    return pl.pallas_call(
        kernel,
        out_shape=outs,
        in_specs=[SMEM] * smem + [VMEM] * (len(args) - smem),
        out_specs=jax.tree.map(lambda _: VMEM, outs),
        scratch_shapes=[pltpu.VMEM(dims, dtype) for dims, dtype in scratch],
        compiler_params=pltpu.CompilerParams(vmem_limit_bytes=mib * 1024 * 1024),
        cost_estimate=pl.CostEstimate(flops=flops, bytes_accessed=4 << 20, transcendentals=0),
    )(*args)


def forward(fetch, reads, place, keys, pieces):
    return call(
        forward_kernel,
        (
            shape(HEADS, BLK, WIDE),
            shape(HEADS, 8, TOK, dtype=F32),
            shape(HEADS, TOK, WIDE),
        ),
        (fetch, reads, place, keys, *pieces),
        smem=3,
        scratch=[
            ((HEAD_DIM, VIEWS * TOK), BF),
            ((WIDE, KEYS), BF),
            ((2, KEYS, TOK), F32),
            ((2, KEYS, TOK), BF),
            ((2, 8, TOK), F32),
            ((2, KEYS, WIDE), BF),
        ],
        flops=10**10,
    )


def backward(fetch, reads, place, keys, queries, stat):
    return call(
        backward_kernel,
        shape(VIEWS, BACK_ROWS, WIDE),
        (fetch, reads, place, keys, queries, stat),
        smem=3,
        scratch=[
            ((HEAD_DIM, VIEWS * TOK), BF),
            ((HEAD_DIM, KEYS), BF),
            ((2, KEYS, 2 * TOK), BF),
            ((VIEWS, TOK, WIDE), F32),
            ((2, KEYS, WIDE), BF),
            ((2, 2 * TOK, WIDE), BF),
        ],
        flops=2 * 10**10,
    )


def swap(rows, axis):
    return lax.all_to_all(rows, axis, split_axis=0, concat_axis=0, tiled=True)


def ring_sum(pieces, axis, count, size, step):
    here = (lax.axis_index(axis) // step) % size
    total = lax.dynamic_index_in_dim(pieces, here, 0, keepdims=False).astype(F32)
    for d in range(1, size):
        pairs = []
        for i in range(count):
            at = (i // step) % size
            pairs.append((i, i + ((at + d) % size - at) * step))
        send = lax.dynamic_index_in_dim(pieces, (here + d) % size, 0, keepdims=False)
        total = total + lax.ppermute(send, axis, pairs).astype(F32)
    return total


def on_device(query_rows, key_rows, value_rows, grad_out, out_weight, fetch_list, read_mask):
    go = grad_out[0, 0]
    fetch = fetch_list.reshape(VIEWS * VIEWS)
    view = lax.axis_index("view")
    side, own_slot = view // HEADS, view % HEADS
    place = jnp.stack([side * HEADS, own_slot]).astype(jnp.int32)
    keys = call(
        pack_keys_kernel, shape(VIEWS, TOK, WIDE), (key_rows[0, 0], value_rows[0, 0]), mib=60
    )
    keys = swap(keys, "view")
    queries = call(
        pack_queries_kernel,
        shape(HEADS, PACK_ROWS, WIDE),
        (query_rows[0, 0], go, out_weight, read_mask[0, 0]),
    )
    pieces = [lax.dynamic_index_in_dim(queries, own_slot, 0, keepdims=False)]
    for d in range(1, HEADS):
        send = lax.dynamic_index_in_dim(queries, (own_slot + d) % HEADS, 0, keepdims=False)
        pairs = [(a, a // HEADS * HEADS + (a % HEADS + d) % HEADS) for a in range(VIEWS)]
        pieces.append(lax.ppermute(send, "view", pairs))
    reads = [piece[r : r + 1, :VIEWS] for piece in pieces for r in (TOK, TOK + 8)]
    reads = jnp.concatenate(reads, axis=0).astype(jnp.int32).reshape(HEADS * 2 * VIEWS)
    attn, stat, queries = forward(fetch, reads, place, keys, pieces)
    sides = [list(range(u * HEADS, (u + 1) * HEADS)) for u in range(SIDES)]
    attn_home = lax.all_to_all(attn, "view", 0, 0, tiled=True, axis_index_groups=sides)
    back = backward(fetch, reads, place, keys, queries, stat)
    attn_home, back = lax.optimization_barrier((attn_home, back))
    core = (lax.axis_index("scene") % CORES).astype(jnp.int32)[None]
    own = INNER // (X * ZHI * CORES)
    piece = shape(X, Y, ZHI, own, ZLO * COLS)
    layer, mine, other = call(
        project_kernel,
        (shape(TOK, D), piece, piece),
        (core, attn_home, go, out_weight),
        smem=1,
        scratch=[((TOK, INNER), BF), ((INNER, D), BF)],
        flops=10**9,
    )
    home = swap(back, "view")
    scenes = X * ZHI * CORES
    other = lax.ppermute(other, "scene", [(i, i ^ 1) for i in range(scenes)])
    term = (mine.astype(F32) + other.astype(F32)).astype(BF)
    term = ring_sum(term, "scene", scenes, X, ZHI * CORES).astype(BF)
    term = ring_sum(term, "view", VIEWS, Y, 1).astype(BF)
    term, home = lax.optimization_barrier((term, home))
    term = term.reshape(ZHI, own, ZLO, COLS).transpose(0, 2, 1, 3).reshape(ZHI * ZLO, own, COLS)
    along_z = [
        [((x * ZHI + zh) * CORES + k) * VIEWS + zl * Y + y for zh in range(ZHI) for zl in range(ZLO)]
        for x in range(X)
        for k in range(CORES)
        for y in range(Y)
    ]
    term = lax.all_to_all(
        term, ("scene", "view"), 0, 0, tiled=True, axis_index_groups=along_z
    )
    share = jnp.sum(term.astype(F32), axis=0) * float(scenes * VIEWS * TOK) ** (-0.5)
    gq, gk, gv = call(unpack_kernel, (shape(TOK, INNER),) * 3, (place, home), smem=1)
    return (layer[None, None], gq[None, None], gk[None, None], gv[None, None], share)


def solution(mesh):
    rows = P("scene", "view", None, None)
    return jax.shard_map(
        on_device,
        mesh=mesh,
        in_specs=(rows, rows, rows, rows, P(), P("scene", None, None), rows),
        out_specs=(rows, rows, rows, rows, P("scene", "view")),
        check_vma=False,
    )
```

time: 158 us -> 146 us (0.924)
  waiting for transfers between devices: 56.5 us -> 26.6 us
  starting transfers between devices: 59.6 us -> 79.9 us
  Pallas kernels: 36.4 us -> 31.5 us
  local copies, waits for them, and re-layouts: 2.08 us -> 4.17 us
    all_to_all x3 -> x2, waiting for transfers between devices: 34.9 us -> 0.01 us  [swap(): return lax.all_to_all(rows, axis, split_axis=0, concat_axis=0, tiled=True)]
    ppermute x0 -> x7, starting transfers between devices: none -> 24.8 us  [on_device(): pieces.append(lax.ppermute(send, 'view', pairs))]
    all_to_all x3 -> x2, starting transfers between devices: 24.9 us -> 16.5 us  [swap(): return lax.all_to_all(rows, axis, split_axis=0, concat_axis=0, tiled=True)]
    ppermute x0 -> x7, waiting for transfers between devices: none -> 5.74 us  [on_device(): pieces.append(lax.ppermute(send, 'view', pairs))]
    pallas_call x5 -> x6, Pallas kernels: 36.4 us -> 31.5 us  [call(): pl.pallas_call(kernel, out_shape=outs, in_specs=[SMEM] * smem + [VMEM] *...]
    all_to_all x0 -> x1, starting transfers between devices: none -> 3.41 us  [on_device(): lax.all_to_all(attn, 'view', 0, 0, tiled=True, axis_index_groups=sides)]
    unnamed x12 -> x18, local copies, waits for them, and re-layouts: 1.79 us -> 3.71 us
  transfers between devices with their start and end apart: 11 -> 18, of which waited for: 7 -> 8; matrix products, arithmetic and copies ran while one was open for 0% -> 1% of each run, Pallas kernels for 13% -> 14%
where the time goes in v7:
time: 146 us; the launch traced here: 145 us
  starting transfers between devices  79.9 us (55%)
  Pallas kernels  31.5 us (22%)
  waiting for transfers between devices  26.6 us (18%)
  local copies, waits for them, and re-layouts  4.17 us (3%)
    pallas_call x6, Pallas kernels, call(): pl.pallas_call(kernel, out_shape=outs, in_specs=[SMEM] * smem + [VMEM] *...  31.5 us
    ppermute x7, starting transfers between devices, on_device(): pieces.append(lax.ppermute(send, 'view', pairs))  24.8 us
    ppermute x6, starting transfers between devices, ring_sum(): total = total + lax.ppermute(send, axis, pairs).astype(F32)  20.3 us
    all_to_all x2, starting transfers between devices, swap(): return lax.all_to_all(rows, axis, split_axis=0, concat_axis=0, tiled=True)  16.5 us
    all_to_all x1, starting transfers between devices, on_device(): lax.all_to_all(term, ('scene', 'view'), 0, 0, tiled=True, axis_index_grou...  12.9 us
    all_to_all x1, waiting for transfers between devices, on_device(): lax.all_to_all(term, ('scene', 'view'), 0, 0, tiled=True, axis_index_grou...  10.7 us
    ppermute x6, waiting for transfers between devices, ring_sum(): total = total + lax.ppermute(send, axis, pairs).astype(F32)  8.15 us
    ppermute x7, waiting for transfers between devices, on_device(): pieces.append(lax.ppermute(send, 'view', pairs))  5.74 us
  transfers between devices with their start and end apart: 18, of which 8 were waited for; matrix products, arithmetic and copies ran while one was open for 1% of the time, Pallas kernels for 14%

profile of v7, /device:TPU:6, one launch (start us, length us, event | category | flops | bytes accessed | tf_op | source)
XLA Modules:
  0.0 144.6 jit_solution(11948951149614639102)
XLA Ops:
  0.7 2.4 %shard_map.111 = bf16[16,256,128]{2,1,0:T(8,128)(2,1)} custom-call(bf16[256,512]{1,0:T(8,128)(2,1)} %bitcast.52, bf16[256,512]{1,0:T(8,128)(2,1)} %bitcast.53), custom_call_target="tpu_custom_call" | custom-call | bytes 4194304 | tf_op jit(solution)/shard_map/pallas_call | solution.py:252
  3.0 8.6 %all-to-all-start = ((bf16[16,256,128]{2,1,0:T(8,128)(2,1)}), bf16[16,256,128]{2,1,0:T(8,128)(2,1)S(1)}, u32[]{:S(2)}, u32[]{:S(2)}) async-start(bf16[16,256,128]{2,1,0:T(8,128)(2,1)} %shard_map.111), calls=%async_computation | async-start | bytes 2097152 | tf_op jit(solution)/shard_map/all_to_all | solution.py:304
  12.5 5.8 %collective-permute-start.6 = (bf16[272,128]{1,0:T(8,128)(2,1)S(1)}, bf16[272,128]{1,0:T(8,128)(2,1)S(1)}, u32[]{:S(2)}, u32[]{:S(2)}) collective-permute-start(bf16[272,128]{1,0:T(8,128)(2,1)S(1)} %get-tuple-element.31), channel_id=1, source_target_pairs={{0,7},{1,0},{2,1},{3,2},{4,3},{5,4},{6,5},{7,6},{8,15},{9,8},{10,9... | collective-permute-start | bytes 208904 | tf_op jit(solution)/shard_map/ppermute | solution.py:339
  18.3 2.8 %collective-permute-start.5 = (bf16[272,128]{1,0:T(8,128)(2,1)S(1)}, bf16[272,128]{1,0:T(8,128)(2,1)S(1)}, u32[]{:S(2)}, u32[]{:S(2)}) collective-permute-start(bf16[272,128]{1,0:T(8,128)(2,1)S(1)} %get-tuple-element.32), channel_id=1, source_target_pairs={{0,6},{1,7},{2,0},{3,1},{4,2},{5,3},{6,4},{7,5},{8,14},{9,15},{10,... | collective-permute-start | bytes 208904 | tf_op jit(solution)/shard_map/ppermute | solution.py:339
  21.1 2.8 %collective-permute-start.4 = (bf16[272,128]{1,0:T(8,128)(2,1)S(1)}, bf16[272,128]{1,0:T(8,128)(2,1)S(1)}, u32[]{:S(2)}, u32[]{:S(2)}) collective-permute-start(bf16[272,128]{1,0:T(8,128)(2,1)S(1)} %get-tuple-element.33), channel_id=1, source_target_pairs={{0,5},{1,6},{2,7},{3,0},{4,1},{5,2},{6,3},{7,4},{8,13},{9,14},{10,... | collective-permute-start | bytes 208904 | tf_op jit(solution)/shard_map/ppermute | solution.py:339
  23.8 3.4 %collective-permute-start.3 = (bf16[272,128]{1,0:T(8,128)(2,1)S(1)}, bf16[272,128]{1,0:T(8,128)(2,1)S(1)}, u32[]{:S(2)}, u32[]{:S(2)}) collective-permute-start(bf16[272,128]{1,0:T(8,128)(2,1)S(1)} %get-tuple-element.34), channel_id=1, source_target_pairs={{0,4},{1,5},{2,6},{3,7},{4,0},{5,1},{6,2},{7,3},{8,12},{9,13},{10,... | collective-permute-start | bytes 208904 | tf_op jit(solution)/shard_map/ppermute | solution.py:339
  27.2 3.4 %collective-permute-start.2 = (bf16[272,128]{1,0:T(8,128)(2,1)S(1)}, bf16[272,128]{1,0:T(8,128)(2,1)S(1)}, u32[]{:S(2)}, u32[]{:S(2)}) collective-permute-start(bf16[272,128]{1,0:T(8,128)(2,1)S(1)} %get-tuple-element.35), channel_id=1, source_target_pairs={{0,3},{1,4},{2,5},{3,6},{4,7},{5,0},{6,1},{7,2},{8,11},{9,12},{10,... | collective-permute-start | bytes 208904 | tf_op jit(solution)/shard_map/ppermute | solution.py:339
  31.3 3.7 %collective-permute-start.1 = (bf16[272,128]{1,0:T(8,128)(2,1)S(1)}, bf16[272,128]{1,0:T(8,128)(2,1)S(1)}, u32[]{:S(2)}, u32[]{:S(2)}) collective-permute-start(bf16[272,128]{1,0:T(8,128)(2,1)S(1)} %get-tuple-element.36), channel_id=1, source_target_pairs={{0,2},{1,3},{2,4},{3,5},{4,6},{5,7},{6,0},{7,1},{8,10},{9,11},{10,... | collective-permute-start | bytes 208904 | tf_op jit(solution)/shard_map/ppermute | solution.py:339
  35.1 3.0 %collective-permute-start = (bf16[272,128]{1,0:T(8,128)(2,1)S(1)}, bf16[272,128]{1,0:T(8,128)(2,1)S(1)}, u32[]{:S(2)}, u32[]{:S(2)}) collective-permute-start(bf16[272,128]{1,0:T(8,128)(2,1)S(1)} %get-tuple-element.37), channel_id=1, source_target_pairs={{0,1},{1,2},{2,3},{3,4},{4,5},{5,6},{6,7},{7,0},{8,9},{9,10},{10,1... | collective-permute-start | bytes 208904 | tf_op jit(solution)/shard_map/ppermute | solution.py:339
  40.5 2.9 %collective-permute-done.refs_1_ = bf16[272,128]{1,0:T(8,128)(2,1)S(1)} collective-permute-done((bf16[272,128]{1,0:T(8,128)(2,1)S(1)}, bf16[272,128]{1,0:T(8,128)(2,1)S(1)}, u32[]{:S(2)}, u32[]{:S(2)}) %collective-permute-start) | collective-permute-done | bytes 69664 | tf_op jit(solution)/shard_map/ppermute | solution.py:339
  43.6 8.9 %shard_map.112 = (bf16[8,128,128]{2,1,0:T(8,128)(2,1)}, f32[8,8,256]{2,1,0:T(8,128)S(1)}, bf16[8,256,128]{2,1,0:T(8,128)(2,1)S(1)}) custom-call(s32[256]{0:T(256)S(1)} %reshape.25.fetch_ref, s32[256]{0:T(256)S(1)} %reshape.27.mask_ref, s32[2]{0:T(128)S(1)} %pad_add_fusion.place_ref, bf16[16,256,128]{2,1,0:T(8,128)(2,1)S(1)} %all-to-all-done.in_ref, ...), custom_call_target="tpu_custom_call" | custom-call | flops 10000000000 | bytes 4194304 | tf_op jit(solution)/shard_map/pallas_call | solution.py:252
  53.3 3.4 %all-to-all-start.1 = ((bf16[8,128,128]{2,1,0:T(8,128)(2,1)}), bf16[8,128,128]{2,1,0:T(8,128)(2,1)S(1)}, u32[]{:S(2)}, u32[]{:S(2)}) async-start(bf16[8,128,128]{2,1,0:T(8,128)(2,1)} %get-tuple-element.18), calls=%async_computation.1 | async-start | bytes 524288 | tf_op jit(solution)/shard_map/all_to_all | solution.py:344
  57.7 16.1 %shard_map.113 = bf16[16,384,128]{2,1,0:T(8,128)(2,1)} custom-call(s32[256]{0:T(256)S(1)} %reshape.25.fetch_ref, s32[256]{0:T(256)S(1)} %reshape.27.mask_ref, s32[2]{0:T(128)S(1)} %pad_add_fusion.place_ref, bf16[16,256,128]{2,1,0:T(8,128)(2,1)S(1)} %all-to-all-done.in_ref, bf16[8,256,128]{2,1,0:T(8,128)(2,1)S(1)} %copy-done.6, ...), custom_call_target="tpu_custom_call" | custom-call | flops 20000000000 | bytes 4194304 | tf_op jit(solution)/shard_map/pallas_call | solution.py:252
  73.8 7.8 %all-to-all-start.2 = ((bf16[16,384,128]{2,1,0:T(8,128)(2,1)}), bf16[16,384,128]{2,1,0:T(8,128)(2,1)S(1)}, u32[]{:S(2)}, u32[]{:S(2)}) async-start(bf16[16,384,128]{2,1,0:T(8,128)(2,1)} %shard_map.113), calls=%async_computation.2 | async-start | bytes 3145728 | tf_op jit(solution)/shard_map/all_to_all | solution.py:304
  88.7 2.8 %collective-permute-start.8 = (bf16[4,4,16,256]{3,2,1,0:T(8,128)(2,1)S(1)}, bf16[4,4,16,256]{3,2,1,0:T(8,128)(2,1)S(1)}, u32[]{:S(2)}, u32[]{:S(2)}) collective-permute-start(bf16[4,4,16,256]{3,2,1,0:T(8,128)(2,1)S(1)} %get-tuple-element.39), channel_id=1, source_target_pairs={{0,128},{16,144},{32,160},{48,176},{64,192},{80,208},{96,224},{112... | collective-permute-start | bytes 393224 | tf_op jit(solution)/shard_map/ppermute | solution.py:316
  91.4 3.1 %collective-permute-start.10 = (bf16[4,4,16,256]{3,2,1,0:T(8,128)(2,1)S(1)}, bf16[4,4,16,256]{3,2,1,0:T(8,128)(2,1)S(1)}, u32[]{:S(2)}, u32[]{:S(2)}) collective-permute-start(bf16[4,4,16,256]{3,2,1,0:T(8,128)(2,1)S(1)} %get-tuple-element.40), channel_id=1, source_target_pairs={{0,384},{16,400},{32,416},{48,432},{64,448},{80,464},{96,480},{112... | collective-permute-start | bytes 393224 | tf_op jit(solution)/shard_map/ppermute | solution.py:316
  94.5 3.3 %collective-permute-start.9 = (bf16[4,4,16,256]{3,2,1,0:T(8,128)(2,1)S(1)}, bf16[4,4,16,256]{3,2,1,0:T(8,128)(2,1)S(1)}, u32[]{:S(2)}, u32[]{:S(2)}) collective-permute-start(bf16[4,4,16,256]{3,2,1,0:T(8,128)(2,1)S(1)} %get-tuple-element.41), channel_id=1, source_target_pairs={{0,256},{16,272},{32,288},{48,304},{64,320},{80,336},{96,352},{112... | collective-permute-start | bytes 393224 | tf_op jit(solution)/shard_map/ppermute | solution.py:316
  99.8 3.1 %collective-permute-done.9 = bf16[4,4,16,256]{3,2,1,0:T(8,128)(2,1)S(1)} collective-permute-done((bf16[4,4,16,256]{3,2,1,0:T(8,128)(2,1)S(1)}, bf16[4,4,16,256]{3,2,1,0:T(8,128)(2,1)S(1)}, u32[]{:S(2)}, u32[]{:S(2)}) %collective-permute-start.9) | collective-permute-done | bytes 131104 | tf_op jit(solution)/shard_map/ppermute | solution.py:316
  103.0 3.8 %collective-permute-start.11 = (bf16[4,16,256]{2,1,0:T(8,128)(2,1)S(1)}, bf16[4,16,256]{2,1,0:T(8,128)(2,1)S(1)}, u32[]{:S(2)}, u32[]{:S(2)}) collective-permute-start(bf16[4,16,256]{2,1,0:T(8,128)(2,1)S(1)} %get-tuple-element.42), channel_id=1, source_target_pairs={{0,1},{1,2},{2,3},{3,0},{4,5},{5,6},{6,7},{7,4},{8,9},{9,10},{10,1... | collective-permute-start | bytes 98312 | tf_op jit(solution)/shard_map/ppermute | solution.py:316
  106.8 3.2 %collective-permute-start.13 = (bf16[4,16,256]{2,1,0:T(8,128)(2,1)S(1)}, bf16[4,16,256]{2,1,0:T(8,128)(2,1)S(1)}, u32[]{:S(2)}, u32[]{:S(2)}) collective-permute-start(bf16[4,16,256]{2,1,0:T(8,128)(2,1)S(1)} %get-tuple-element.43), channel_id=1, source_target_pairs={{0,3},{1,0},{2,1},{3,2},{4,7},{5,4},{6,5},{7,6},{8,11},{9,8},{10,9... | collective-permute-start | bytes 98312 | tf_op jit(solution)/shard_map/ppermute | solution.py:316
  110.1 4.1 %collective-permute-start.12 = (bf16[4,16,256]{2,1,0:T(8,128)(2,1)S(1)}, bf16[4,16,256]{2,1,0:T(8,128)(2,1)S(1)}, u32[]{:S(2)}, u32[]{:S(2)}) collective-permute-start(bf16[4,16,256]{2,1,0:T(8,128)(2,1)S(1)} %get-tuple-element.44), channel_id=1, source_target_pairs={{0,2},{1,3},{2,0},{3,1},{4,6},{5,7},{6,4},{7,5},{8,10},{9,11},{10,... | collective-permute-start | bytes 98312 | tf_op jit(solution)/shard_map/ppermute | solution.py:316
  114.2 3.2 %collective-permute-done.12 = bf16[4,16,256]{2,1,0:T(8,128)(2,1)S(1)} collective-permute-done((bf16[4,16,256]{2,1,0:T(8,128)(2,1)S(1)}, bf16[4,16,256]{2,1,0:T(8,128)(2,1)S(1)}, u32[]{:S(2)}, u32[]{:S(2)}) %collective-permute-start.12) | collective-permute-done | bytes 32800 | tf_op jit(solution)/shard_map/ppermute | solution.py:316
  118.2 12.9 %all-to-all-start.3 = ((bf16[16,2,512]{2,1,0:T(2,128)(2,1)}), bf16[16,2,512]{2,1,0:T(2,128)(2,1)S(1)}, u32[]{:S(2)}, u32[]{:S(2)}) async-start(bf16[16,2,512]{2,1,0:T(2,128)(2,1)} %reshape.30), calls=%async_computation.3 | async-start | bytes 65536 | tf_op jit(solution)/shard_map/all_to_all | solution.py:372
  133.1 10.7 %all-to-all-done.3 = bf16[16,2,512]{2,1,0:T(2,128)(2,1)S(1)} async-done(((bf16[16,2,512]{2,1,0:T(2,128)(2,1)}), bf16[16,2,512]{2,1,0:T(2,128)(2,1)S(1)}, u32[]{:S(2)}, u32[]{:S(2)}) %all-to-all-start.3) | async-done | bytes 32800 | tf_op jit(solution)/shard_map/all_to_all | solution.py:372
  (59 shorter events, 17.9 us)
Async XLA Ops:
  0.6 11.2 %copy-start = (bf16[512,1024]{1,0:T(8,128)(2,1)S(1)}, bf16[512,1024]{1,0:T(8,128)(2,1)}, u32[]{:S(2)}) copy-start(bf16[512,1024]{1,0:T(8,128)(2,1)} %w_ref.3) | copy-start | bytes 3145732
  0.6 11.2 %copy-start.1 = (bf16[1,1,256,1024]{3,2,1,0:T(8,128)(2,1)S(1)}, bf16[1,1,256,1024]{3,2,1,0:T(8,128)(2,1)}, u32[]{:S(2)}) copy-start(bf16[1,1,256,1024]{3,2,1,0:T(8,128)(2,1)} %param.10) | copy-start | bytes 1572868
  0.7 11.2 %copy-start.3 = (bf16[1,1,256,512]{3,2,1,0:T(8,128)(2,1)S(1)}, bf16[1,1,256,512]{3,2,1,0:T(8,128)(2,1)}, u32[]{:S(2)}) copy-start(bf16[1,1,256,512]{3,2,1,0:T(8,128)(2,1)} %param.7) | copy-start | bytes 786436
  0.7 11.2 %copy-start.4 = (s32[1,1,2,16]{3,2,1,0:T(2,128)S(1)}, s32[1,1,2,16]{3,2,1,0:T(2,128)}, u32[]{:S(2)}) copy-start(s32[1,1,2,16]{3,2,1,0:T(2,128)} %param.13) | copy-start | bytes 388
  3.0 40.5 %all-to-all-start = ((bf16[16,256,128]{2,1,0:T(8,128)(2,1)}), bf16[16,256,128]{2,1,0:T(8,128)(2,1)S(1)}, u32[]{:S(2)}, u32[]{:S(2)}) async-start(bf16[16,256,128]{2,1,0:T(8,128)(2,1)} %shard_map.111), calls=%async_computation | async-start | bytes 2097152 | tf_op jit(solution)/shard_map/all_to_all | solution.py:304
  11.9 18.8 %copy-start.7 = (s32[1,16,16]{2,1,0:T(8,128)S(1)}, s32[1,16,16]{2,1,0:T(8,128)}, u32[]{:S(2)}) copy-start(s32[1,16,16]{2,1,0:T(8,128)} %param.12) | copy-start | bytes 3076
  12.5 18.8 %collective-permute-start.6 = (bf16[272,128]{1,0:T(8,128)(2,1)S(1)}, bf16[272,128]{1,0:T(8,128)(2,1)S(1)}, u32[]{:S(2)}, u32[]{:S(2)}) collective-permute-start(bf16[272,128]{1,0:T(8,128)(2,1)S(1)} %get-tuple-element.31), channel_id=1, source_target_pairs={{0,7},{1,0},{2,1},{3,2},{4,3},{5,4},{6,5},{7,6},{8,15},{9,8},{10,9... | collective-permute-start | bytes 208904 | tf_op jit(solution)/shard_map/ppermute | solution.py:339
  18.3 16.8 %collective-permute-start.5 = (bf16[272,128]{1,0:T(8,128)(2,1)S(1)}, bf16[272,128]{1,0:T(8,128)(2,1)S(1)}, u32[]{:S(2)}, u32[]{:S(2)}) collective-permute-start(bf16[272,128]{1,0:T(8,128)(2,1)S(1)} %get-tuple-element.32), channel_id=1, source_target_pairs={{0,6},{1,7},{2,0},{3,1},{4,2},{5,3},{6,4},{7,5},{8,14},{9,15},{10,... | collective-permute-start | bytes 208904 | tf_op jit(solution)/shard_map/ppermute | solution.py:339
  21.1 17.1 %collective-permute-start.4 = (bf16[272,128]{1,0:T(8,128)(2,1)S(1)}, bf16[272,128]{1,0:T(8,128)(2,1)S(1)}, u32[]{:S(2)}, u32[]{:S(2)}) collective-permute-start(bf16[272,128]{1,0:T(8,128)(2,1)S(1)} %get-tuple-element.33), channel_id=1, source_target_pairs={{0,5},{1,6},{2,7},{3,0},{4,1},{5,2},{6,3},{7,4},{8,13},{9,14},{10,... | collective-permute-start | bytes 208904 | tf_op jit(solution)/shard_map/ppermute | solution.py:339
  23.8 14.3 %collective-permute-start.3 = (bf16[272,128]{1,0:T(8,128)(2,1)S(1)}, bf16[272,128]{1,0:T(8,128)(2,1)S(1)}, u32[]{:S(2)}, u32[]{:S(2)}) collective-permute-start(bf16[272,128]{1,0:T(8,128)(2,1)S(1)} %get-tuple-element.34), channel_id=1, source_target_pairs={{0,4},{1,5},{2,6},{3,7},{4,0},{5,1},{6,2},{7,3},{8,12},{9,13},{10,... | collective-permute-start | bytes 208904 | tf_op jit(solution)/shard_map/ppermute | solution.py:339
  27.2 10.9 %collective-permute-start.2 = (bf16[272,128]{1,0:T(8,128)(2,1)S(1)}, bf16[272,128]{1,0:T(8,128)(2,1)S(1)}, u32[]{:S(2)}, u32[]{:S(2)}) collective-permute-start(bf16[272,128]{1,0:T(8,128)(2,1)S(1)} %get-tuple-element.35), channel_id=1, source_target_pairs={{0,3},{1,4},{2,5},{3,6},{4,7},{5,0},{6,1},{7,2},{8,11},{9,12},{10,... | collective-permute-start | bytes 208904 | tf_op jit(solution)/shard_map/ppermute | solution.py:339
  31.3 9.2 %collective-permute-start.1 = (bf16[272,128]{1,0:T(8,128)(2,1)S(1)}, bf16[272,128]{1,0:T(8,128)(2,1)S(1)}, u32[]{:S(2)}, u32[]{:S(2)}) collective-permute-start(bf16[272,128]{1,0:T(8,128)(2,1)S(1)} %get-tuple-element.36), channel_id=1, source_target_pairs={{0,2},{1,3},{2,4},{3,5},{4,6},{5,7},{6,0},{7,1},{8,10},{9,11},{10,... | collective-permute-start | bytes 208904 | tf_op jit(solution)/shard_map/ppermute | solution.py:339
  35.1 8.3 %collective-permute-start = (bf16[272,128]{1,0:T(8,128)(2,1)S(1)}, bf16[272,128]{1,0:T(8,128)(2,1)S(1)}, u32[]{:S(2)}, u32[]{:S(2)}) collective-permute-start(bf16[272,128]{1,0:T(8,128)(2,1)S(1)} %get-tuple-element.37), channel_id=1, source_target_pairs={{0,1},{1,2},{2,3},{3,4},{4,5},{5,6},{6,7},{7,0},{8,9},{9,10},{10,1... | collective-permute-start | bytes 208904 | tf_op jit(solution)/shard_map/ppermute | solution.py:339
  53.3 20.6 %all-to-all-start.1 = ((bf16[8,128,128]{2,1,0:T(8,128)(2,1)}), bf16[8,128,128]{2,1,0:T(8,128)(2,1)S(1)}, u32[]{:S(2)}, u32[]{:S(2)}) async-start(bf16[8,128,128]{2,1,0:T(8,128)(2,1)} %get-tuple-element.18), calls=%async_computation.1 | async-start | bytes 524288 | tf_op jit(solution)/shard_map/all_to_all | solution.py:344
  56.7 1.0 copy-start.6
  73.8 43.6 %all-to-all-start.2 = ((bf16[16,384,128]{2,1,0:T(8,128)(2,1)}), bf16[16,384,128]{2,1,0:T(8,128)(2,1)S(1)}, u32[]{:S(2)}, u32[]{:S(2)}) async-start(bf16[16,384,128]{2,1,0:T(8,128)(2,1)} %shard_map.113), calls=%async_computation.2 | async-start | bytes 3145728 | tf_op jit(solution)/shard_map/all_to_all | solution.py:304
  84.4 4.0 %collective-permute-start.7 = (bf16[4,4,4,16,256]{4,3,2,1,0:T(8,128)(2,1)}, bf16[4,4,4,16,256]{4,3,2,1,0:T(8,128)(2,1)S(1)}, u32[]{:S(2)}, u32[]{:S(2)}) collective-permute-start(bf16[4,4,4,16,256]{4,3,2,1,0:T(8,128)(2,1)} %get-tuple-element.24), channel_id=1, source_target_pairs={{0,16},{16,0},{32,48},{48,32},{64,80},{80,64},{96,112},{112,96},{1... | collective-permute-start | bytes 1572872 | tf_op jit(solution)/shard_map/ppermute | solution.py:360
  88.7 9.2 %collective-permute-start.8 = (bf16[4,4,16,256]{3,2,1,0:T(8,128)(2,1)S(1)}, bf16[4,4,16,256]{3,2,1,0:T(8,128)(2,1)S(1)}, u32[]{:S(2)}, u32[]{:S(2)}) collective-permute-start(bf16[4,4,16,256]{3,2,1,0:T(8,128)(2,1)S(1)} %get-tuple-element.39), channel_id=1, source_target_pairs={{0,128},{16,144},{32,160},{48,176},{64,192},{80,208},{96,224},{112... | collective-permute-start | bytes 393224 | tf_op jit(solution)/shard_map/ppermute | solution.py:316
  91.4 8.4 %collective-permute-start.10 = (bf16[4,4,16,256]{3,2,1,0:T(8,128)(2,1)S(1)}, bf16[4,4,16,256]{3,2,1,0:T(8,128)(2,1)S(1)}, u32[]{:S(2)}, u32[]{:S(2)}) collective-permute-start(bf16[4,4,16,256]{3,2,1,0:T(8,128)(2,1)S(1)} %get-tuple-element.40), channel_id=1, source_target_pairs={{0,384},{16,400},{32,416},{48,432},{64,448},{80,464},{96,480},{112... | collective-permute-start | bytes 393224 | tf_op jit(solution)/shard_map/ppermute | solution.py:316
  94.5 8.4 %collective-permute-start.9 = (bf16[4,4,16,256]{3,2,1,0:T(8,128)(2,1)S(1)}, bf16[4,4,16,256]{3,2,1,0:T(8,128)(2,1)S(1)}, u32[]{:S(2)}, u32[]{:S(2)}) collective-permute-start(bf16[4,4,16,256]{3,2,1,0:T(8,128)(2,1)S(1)} %get-tuple-element.41), channel_id=1, source_target_pairs={{0,256},{16,272},{32,288},{48,304},{64,320},{80,336},{96,352},{112... | collective-permute-start | bytes 393224 | tf_op jit(solution)/shard_map/ppermute | solution.py:316
  103.0 11.2 %collective-permute-start.11 = (bf16[4,16,256]{2,1,0:T(8,128)(2,1)S(1)}, bf16[4,16,256]{2,1,0:T(8,128)(2,1)S(1)}, u32[]{:S(2)}, u32[]{:S(2)}) collective-permute-start(bf16[4,16,256]{2,1,0:T(8,128)(2,1)S(1)} %get-tuple-element.42), channel_id=1, source_target_pairs={{0,1},{1,2},{2,3},{3,0},{4,5},{5,6},{6,7},{7,4},{8,9},{9,10},{10,1... | collective-permute-start | bytes 98312 | tf_op jit(solution)/shard_map/ppermute | solution.py:316
  106.8 7.4 %collective-permute-start.13 = (bf16[4,16,256]{2,1,0:T(8,128)(2,1)S(1)}, bf16[4,16,256]{2,1,0:T(8,128)(2,1)S(1)}, u32[]{:S(2)}, u32[]{:S(2)}) collective-permute-start(bf16[4,16,256]{2,1,0:T(8,128)(2,1)S(1)} %get-tuple-element.43), channel_id=1, source_target_pairs={{0,3},{1,0},{2,1},{3,2},{4,7},{5,4},{6,5},{7,6},{8,11},{9,8},{10,9... | collective-permute-start | bytes 98312 | tf_op jit(solution)/shard_map/ppermute | solution.py:316
  110.1 7.3 %collective-permute-start.12 = (bf16[4,16,256]{2,1,0:T(8,128)(2,1)S(1)}, bf16[4,16,256]{2,1,0:T(8,128)(2,1)S(1)}, u32[]{:S(2)}, u32[]{:S(2)}) collective-permute-start(bf16[4,16,256]{2,1,0:T(8,128)(2,1)S(1)} %get-tuple-element.44), channel_id=1, source_target_pairs={{0,2},{1,3},{2,0},{3,1},{4,6},{5,7},{6,4},{7,5},{8,10},{9,11},{10,... | collective-permute-start | bytes 98312 | tf_op jit(solution)/shard_map/ppermute | solution.py:316
  118.2 25.6 %all-to-all-start.3 = ((bf16[16,2,512]{2,1,0:T(2,128)(2,1)}), bf16[16,2,512]{2,1,0:T(2,128)(2,1)S(1)}, u32[]{:S(2)}, u32[]{:S(2)}) async-start(bf16[16,2,512]{2,1,0:T(2,128)(2,1)} %reshape.30), calls=%async_computation.3 | async-start | bytes 65536 | tf_op jit(solution)/shard_map/all_to_all | solution.py:372
  (2 other events, 1.8 us)

commit v8 on v7

--- a/solution.py
+++ b/solution.py
@@ -20,7 +20,7 @@
 SCALE = HEAD_DIM ** (-0.5)
 SIDES = 2
 PACK_ROWS = TOK + 16
-CHUNK = 768
+CHUNK = 384
 BACK_CHUNK = 256
 BACK_ROWS = TOK + BLK
 X, ZHI, CORES = 4, 4, 2
@@ -85,22 +85,28 @@
     return jnp.where(lane < HEAD_DIM, qg, zero), jnp.where(lane >= HEAD_DIM, qg, zero)
 
 
-def place_queries(place_ref, pieces, qg_ref):
-    for d, piece in enumerate(pieces):
-        at = lax.rem(place_ref[1] - d + HEADS, HEADS)
-        qg_ref[at, :, :] = piece[0:TOK, :]
+def place_queries(place_ref, near, far_ref, qg_ref):
+    for d, piece in enumerate(near):
+        along = lax.rem(place_ref[2] - d + Y, Y)
+        qg_ref[place_ref[1] * Y + along, :, :] = piece[0:TOK, :]
+        qg_ref[(1 - place_ref[1]) * Y + along, :, :] = far_ref[d, 0:TOK, :]
+
+
+def source_of(i, place_ref):
+    row, along = lax.div(i, Y), lax.rem(i, Y)
+    return jnp.where(row == place_ref[1], 0, Y) + lax.rem(place_ref[2] - along + Y, Y)
 
 
 def forward_kernel(fetch_ref, mask_ref, place_ref, in_ref, *refs):
-    attn_ref, stat_ref, qg_ref, vt, vsel, s_ref, e_ref, top_ref, kall = refs[HEADS:]
-    place_queries(place_ref, refs[:HEADS], qg_ref)
+    attn_ref, stat_ref, qg_ref, vt, vsel, s_ref, e_ref, top_ref, kall = refs[Y + 1 :]
+    place_queries(place_ref, refs[:Y], refs[Y], qg_ref)
     for w in range(VIEWS):
         vt[:, w * TOK : (w + 1) * TOK] = in_ref[w, :, :].T[HEAD_DIM:, :]
     vsel[0:HEAD_DIM, :] = jnp.ones((HEAD_DIM, KEYS), BF)
 
     def scores(i, slot):
         v = place_ref[0] + i
-        source = lax.rem(place_ref[1] - i + HEADS, HEADS)
+        source = source_of(i, place_ref)
         qs = halves(qg_ref[i])[0]
         gather_rows(v, in_ref, kall.at[slot], fetch_ref)
         top = None
@@ -155,7 +161,7 @@
 
     def weights(i, slot):
         v = place_ref[0] + i
-        source = lax.rem(place_ref[1] - i + HEADS, HEADS)
+        source = source_of(i, place_ref)
         low, high = halves(qg_ref[i])
         qg2_ref[slot, 0:TOK, :] = low
         qg2_ref[slot, TOK:, :] = high
@@ -321,8 +327,8 @@
     go = grad_out[0, 0]
     fetch = fetch_list.reshape(VIEWS * VIEWS)
     view = lax.axis_index("view")
-    side, own_slot = view // HEADS, view % HEADS
-    place = jnp.stack([side * HEADS, own_slot]).astype(jnp.int32)
+    side, row, along = view // HEADS, view // Y % 2, view % Y
+    place = jnp.stack([side * HEADS, row, along]).astype(jnp.int32)
     keys = call(
         pack_keys_kernel, shape(VIEWS, TOK, WIDE), (key_rows[0, 0], value_rows[0, 0]), mib=60
     )
@@ -332,13 +338,19 @@
         shape(HEADS, PACK_ROWS, WIDE),
         (query_rows[0, 0], go, out_weight, read_mask[0, 0]),
     )
-    pieces = [lax.dynamic_index_in_dim(queries, own_slot, 0, keepdims=False)]
-    for d in range(1, HEADS):
-        send = lax.dynamic_index_in_dim(queries, (own_slot + d) % HEADS, 0, keepdims=False)
-        pairs = [(a, a // HEADS * HEADS + (a % HEADS + d) % HEADS) for a in range(VIEWS)]
-        pieces.append(lax.ppermute(send, "view", pairs))
-    reads = [piece[r : r + 1, :VIEWS] for piece in pieces for r in (TOK, TOK + 8)]
+    queries = queries.reshape(2, Y, PACK_ROWS, WIDE)
+    moved = [lax.dynamic_index_in_dim(queries, along, 1, keepdims=False)]
+    for d in range(1, Y):
+        send = lax.dynamic_index_in_dim(queries, (along + d) % Y, 1, keepdims=False)
+        pairs = [(a, a // Y * Y + (a % Y + d) % Y) for a in range(VIEWS)]
+        moved.append(lax.ppermute(send, "view", pairs))
+    near = [lax.dynamic_index_in_dim(m, row, 0, keepdims=False) for m in moved]
+    far = jnp.stack([lax.dynamic_index_in_dim(m, 1 - row, 0, keepdims=False) for m in moved])
+    far = lax.ppermute(far, "view", [(a, a ^ Y) for a in range(VIEWS)])
+    reads = [piece[None] for piece in near] + [far]
+    reads = [piece[:, TOK::8, :VIEWS] for piece in reads]
     reads = jnp.concatenate(reads, axis=0).astype(jnp.int32).reshape(HEADS * 2 * VIEWS)
+    pieces = near + [far]
     attn, stat, queries = forward(fetch, reads, place, keys, pieces)
     sides = [list(range(u * HEADS, (u + 1) * HEADS)) for u in range(SIDES)]
     attn_home = lax.all_to_all(attn, "view", 0, 0, tiled=True, axis_index_groups=sides)

time: 146 us -> 144 us (0.986)
  starting transfers between devices: 79.9 us -> 73.9 us
  waiting for transfers between devices: 26.6 us -> 32.1 us
  local copies, waits for them, and re-layouts: 4.17 us -> 2.49 us
    ppermute x7 -> x4, starting transfers between devices: 24.8 us -> 16.7 us  [the longest x3 11.1 us: on_device(): moved.append(lax.ppermute(send, 'view', pairs))]
    ppermute x7 -> x4, waiting for transfers between devices: 5.74 us -> 11.3 us  [the longest x3 6.87 us: on_device(): moved.append(lax.ppermute(send, 'view', pairs))]
    unnamed x18, local copies, waits for them, and re-layouts: 3.71 us -> 1.92 us
  transfers between devices with their start and end apart: 18 -> 15, of which waited for: 8 -> 7; matrix products, arithmetic and copies ran while one was open for 1% -> 1% of each run, Pallas kernels for 14% -> 15%
where the time goes in v8:
time: 144 us; the launch traced here: 143 us
  starting transfers between devices  73.9 us (51%)
  Pallas kernels  32.1 us (22%)
  waiting for transfers between devices  32.1 us (22%)
  local copies, waits for them, and re-layouts  2.49 us (2%)
    pallas_call x6, Pallas kernels, call(): pl.pallas_call(kernel, out_shape=outs, in_specs=[SMEM] * smem + [VMEM] *...  32.1 us
    ppermute x6, starting transfers between devices, ring_sum(): total = total + lax.ppermute(send, axis, pairs).astype(F32)  20.3 us
    all_to_all x2, starting transfers between devices, swap(): return lax.all_to_all(rows, axis, split_axis=0, concat_axis=0, tiled=True)  16.5 us
    all_to_all x1, starting transfers between devices, on_device(): lax.all_to_all(term, ('scene', 'view'), 0, 0, tiled=True, axis_index_grou...  14 us
    ppermute x3, starting transfers between devices, on_device(): moved.append(lax.ppermute(send, 'view', pairs))  11.1 us
    all_to_all x1, waiting for transfers between devices, on_device(): lax.all_to_all(term, ('scene', 'view'), 0, 0, tiled=True, axis_index_grou...  10.6 us
    ppermute x6, waiting for transfers between devices, ring_sum(): total = total + lax.ppermute(send, axis, pairs).astype(F32)  8.23 us
    ppermute x3, waiting for transfers between devices, on_device(): moved.append(lax.ppermute(send, 'view', pairs))  6.87 us
  transfers between devices with their start and end apart: 15, of which 7 were waited for; matrix products, arithmetic and copies ran while one was open for 1% of the time, Pallas kernels for 15%

profile of v8, /device:TPU:6, one launch (start us, length us, event | category | flops | bytes accessed | tf_op | source)
XLA Modules:
  0.0 142.9 jit_solution(11966021137423489461)
XLA Ops:
  0.7 2.3 %shard_map.111 = bf16[16,256,128]{2,1,0:T(8,128)(2,1)} custom-call(bf16[256,512]{1,0:T(8,128)(2,1)} %bitcast.62, bf16[256,512]{1,0:T(8,128)(2,1)} %bitcast.63), custom_call_target="tpu_custom_call" | custom-call | bytes 4194304 | tf_op jit(solution)/shard_map/pallas_call | solution.py:258
  3.0 8.7 %all-to-all-start = ((bf16[16,256,128]{2,1,0:T(8,128)(2,1)}), bf16[16,256,128]{2,1,0:T(8,128)(2,1)}, u32[]{:S(2)}, u32[]{:S(2)}) async-start(bf16[16,256,128]{2,1,0:T(8,128)(2,1)} %shard_map.111), calls=%async_computation | async-start | bytes 2097152 | tf_op jit(solution)/shard_map/all_to_all | solution.py:310
  12.4 4.9 %collective-permute-start.2 = (bf16[2,272,128]{2,1,0:T(8,128)(2,1)S(1)}, bf16[2,272,128]{2,1,0:T(8,128)(2,1)S(1)}, u32[]{:S(2)}, u32[]{:S(2)}) collective-permute-start(bf16[2,272,128]{2,1,0:T(8,128)(2,1)S(1)} %get-tuple-element.34), channel_id=1, source_target_pairs={{0,3},{1,0},{2,1},{3,2},{4,7},{5,4},{6,5},{7,6},{8,11},{9,8},{10,9... | collective-permute-start | bytes 417800 | tf_op jit(solution)/shard_map/ppermute | solution.py:346
  17.4 1.9 %collective-permute-start = (bf16[2,272,128]{2,1,0:T(8,128)(2,1)S(1)}, bf16[2,272,128]{2,1,0:T(8,128)(2,1)S(1)}, u32[]{:S(2)}, u32[]{:S(2)}) collective-permute-start(bf16[2,272,128]{2,1,0:T(8,128)(2,1)S(1)} %get-tuple-element.35), channel_id=1, source_target_pairs={{0,1},{1,2},{2,3},{3,0},{4,5},{5,6},{6,7},{7,4},{8,9},{9,10},{10,1... | collective-permute-start | bytes 417800 | tf_op jit(solution)/shard_map/ppermute | solution.py:346
  19.3 4.2 %collective-permute-start.1 = (bf16[2,272,128]{2,1,0:T(8,128)(2,1)S(1)}, bf16[2,272,128]{2,1,0:T(8,128)(2,1)S(1)}, u32[]{:S(2)}, u32[]{:S(2)}) collective-permute-start(bf16[2,272,128]{2,1,0:T(8,128)(2,1)S(1)} %get-tuple-element.36), channel_id=1, source_target_pairs={{0,2},{1,3},{2,0},{3,1},{4,6},{5,7},{6,4},{7,5},{8,10},{9,11},{10,... | collective-permute-start | bytes 417800 | tf_op jit(solution)/shard_map/ppermute | solution.py:346
  23.8 6.9 %collective-permute-done = bf16[2,272,128]{2,1,0:T(8,128)(2,1)S(1)} collective-permute-done((bf16[2,272,128]{2,1,0:T(8,128)(2,1)S(1)}, bf16[2,272,128]{2,1,0:T(8,128)(2,1)S(1)}, u32[]{:S(2)}, u32[]{:S(2)}) %collective-permute-start) | collective-permute-done | bytes 139296 | tf_op jit(solution)/shard_map/ppermute | solution.py:346
  30.8 5.7 %collective-permute-start.3 = (bf16[4,272,128]{2,1,0:T(8,128)(2,1)S(1)}, bf16[4,272,128]{2,1,0:T(8,128)(2,1)S(1)}, u32[]{:S(2)}, u32[]{:S(2)}) collective-permute-start(bf16[4,272,128]{2,1,0:T(8,128)(2,1)S(1)} %pad_maximum_fusion), channel_id=1, source_target_pairs={{0,4},{1,5},{2,6},{3,7},{4,0},{5,1},{6,2},{7,3},{8,12},{9,13},{10,... | collective-permute-start | bytes 835592 | tf_op jit(solution)/shard_map/ppermute | solution.py:349
  36.6 4.4 %collective-permute-done.3.refs_4_ = bf16[4,272,128]{2,1,0:T(8,128)(2,1)S(1)} collective-permute-done((bf16[4,272,128]{2,1,0:T(8,128)(2,1)S(1)}, bf16[4,272,128]{2,1,0:T(8,128)(2,1)S(1)}, u32[]{:S(2)}, u32[]{:S(2)}) %collective-permute-start.3) | collective-permute-done | bytes 278560 | tf_op jit(solution)/shard_map/ppermute | solution.py:349
  41.2 8.8 %shard_map.112 = (bf16[8,128,128]{2,1,0:T(8,128)(2,1)}, f32[8,8,256]{2,1,0:T(8,128)S(1)}, bf16[8,256,128]{2,1,0:T(8,128)(2,1)S(1)}) custom-call(s32[256]{0:T(256)S(1)} %reshape.31.fetch_ref, s32[256]{0:T(256)S(1)} %reshape.34.mask_ref, s32[3]{0:T(128)S(1)} %pad_add_fusion.place_ref, bf16[16,256,128]{2,1,0:T(8,128)(2,1)} %all-to-all-done.in_ref, ...), custom_call_target="tpu_custom_call" | custom-call | flops 10000000000 | bytes 4194304 | tf_op jit(solution)/shard_map/pallas_call | solution.py:258
  50.0 4.4 %all-to-all-start.1 = ((bf16[8,128,128]{2,1,0:T(8,128)(2,1)}), bf16[8,128,128]{2,1,0:T(8,128)(2,1)S(1)}, u32[]{:S(2)}, u32[]{:S(2)}) async-start(bf16[8,128,128]{2,1,0:T(8,128)(2,1)} %get-tuple-element.18), calls=%async_computation.1 | async-start | bytes 524288 | tf_op jit(solution)/shard_map/all_to_all | solution.py:356
  54.4 16.8 %shard_map.113 = bf16[16,384,128]{2,1,0:T(8,128)(2,1)} custom-call(s32[256]{0:T(256)S(1)} %reshape.31.fetch_ref, s32[256]{0:T(256)S(1)} %reshape.34.mask_ref, s32[3]{0:T(128)S(1)} %pad_add_fusion.place_ref, bf16[16,256,128]{2,1,0:T(8,128)(2,1)} %all-to-all-done.in_ref, bf16[8,256,128]{2,1,0:T(8,128)(2,1)S(1)} %get-tuple-element.19.qg_ref, ...), custom_call_target="tpu_custom_call" | custom-call | flops 20000000000 | bytes 4194304 | tf_op jit(solution)/shard_map/pallas_call | solution.py:258
  71.3 7.8 %all-to-all-start.2 = ((bf16[16,384,128]{2,1,0:T(8,128)(2,1)}), bf16[16,384,128]{2,1,0:T(8,128)(2,1)S(1)}, u32[]{:S(2)}, u32[]{:S(2)}) async-start(bf16[16,384,128]{2,1,0:T(8,128)(2,1)} %shard_map.113), calls=%async_computation.2 | async-start | bytes 3145728 | tf_op jit(solution)/shard_map/all_to_all | solution.py:310
  81.8 1.9 %collective-permute-start.4 = (bf16[4,4,4,16,256]{4,3,2,1,0:T(8,128)(2,1)}, bf16[4,4,4,16,256]{4,3,2,1,0:T(8,128)(2,1)S(1)}, u32[]{:S(2)}, u32[]{:S(2)}) collective-permute-start(bf16[4,4,4,16,256]{4,3,2,1,0:T(8,128)(2,1)} %get-tuple-element.24), channel_id=1, source_target_pairs={{0,16},{16,0},{32,48},{48,32},{64,80},{80,64},{96,112},{112,96},{1... | collective-permute-start | bytes 1572872 | tf_op jit(solution)/shard_map/ppermute | solution.py:372
  83.8 2.0 %collective-permute-done.4 = bf16[4,4,4,16,256]{4,3,2,1,0:T(8,128)(2,1)S(1)} collective-permute-done((bf16[4,4,4,16,256]{4,3,2,1,0:T(8,128)(2,1)}, bf16[4,4,4,16,256]{4,3,2,1,0:T(8,128)(2,1)S(1)}, u32[]{:S(2)}, u32[]{:S(2)}) %collective-permute-start.4) | collective-permute-done | bytes 524320 | tf_op jit(solution)/shard_map/ppermute | solution.py:372
  86.0 1.9 %collective-permute-start.5 = (bf16[4,4,16,256]{3,2,1,0:T(8,128)(2,1)S(1)}, bf16[4,4,16,256]{3,2,1,0:T(8,128)(2,1)S(1)}, u32[]{:S(2)}, u32[]{:S(2)}) collective-permute-start(bf16[4,4,16,256]{3,2,1,0:T(8,128)(2,1)S(1)} %get-tuple-element.37), channel_id=1, source_target_pairs={{0,128},{16,144},{32,160},{48,176},{64,192},{80,208},{96,224},{112... | collective-permute-start | bytes 393224 | tf_op jit(solution)/shard_map/ppermute | solution.py:322
  88.0 3.9 %collective-permute-start.7 = (bf16[4,4,16,256]{3,2,1,0:T(8,128)(2,1)S(1)}, bf16[4,4,16,256]{3,2,1,0:T(8,128)(2,1)S(1)}, u32[]{:S(2)}, u32[]{:S(2)}) collective-permute-start(bf16[4,4,16,256]{3,2,1,0:T(8,128)(2,1)S(1)} %get-tuple-element.38), channel_id=1, source_target_pairs={{0,384},{16,400},{32,416},{48,432},{64,448},{80,464},{96,480},{112... | collective-permute-start | bytes 393224 | tf_op jit(solution)/shard_map/ppermute | solution.py:322
  91.9 3.3 %collective-permute-start.6 = (bf16[4,4,16,256]{3,2,1,0:T(8,128)(2,1)S(1)}, bf16[4,4,16,256]{3,2,1,0:T(8,128)(2,1)S(1)}, u32[]{:S(2)}, u32[]{:S(2)}) collective-permute-start(bf16[4,4,16,256]{3,2,1,0:T(8,128)(2,1)S(1)} %get-tuple-element.39), channel_id=1, source_target_pairs={{0,256},{16,272},{32,288},{48,304},{64,320},{80,336},{96,352},{112... | collective-permute-start | bytes 393224 | tf_op jit(solution)/shard_map/ppermute | solution.py:322
  96.6 3.7 %collective-permute-done.6 = bf16[4,4,16,256]{3,2,1,0:T(8,128)(2,1)S(1)} collective-permute-done((bf16[4,4,16,256]{3,2,1,0:T(8,128)(2,1)S(1)}, bf16[4,4,16,256]{3,2,1,0:T(8,128)(2,1)S(1)}, u32[]{:S(2)}, u32[]{:S(2)}) %collective-permute-start.6) | collective-permute-done | bytes 131104 | tf_op jit(solution)/shard_map/ppermute | solution.py:322
  100.4 3.8 %collective-permute-start.8 = (bf16[4,16,256]{2,1,0:T(8,128)(2,1)S(1)}, bf16[4,16,256]{2,1,0:T(8,128)(2,1)S(1)}, u32[]{:S(2)}, u32[]{:S(2)}) collective-permute-start(bf16[4,16,256]{2,1,0:T(8,128)(2,1)S(1)} %get-tuple-element.46), channel_id=1, source_target_pairs={{0,1},{1,2},{2,3},{3,0},{4,5},{5,6},{6,7},{7,4},{8,9},{9,10},{10,1... | collective-permute-start | bytes 98312 | tf_op jit(solution)/shard_map/ppermute | solution.py:322
  104.2 3.2 %collective-permute-start.10 = (bf16[4,16,256]{2,1,0:T(8,128)(2,1)S(1)}, bf16[4,16,256]{2,1,0:T(8,128)(2,1)S(1)}, u32[]{:S(2)}, u32[]{:S(2)}) collective-permute-start(bf16[4,16,256]{2,1,0:T(8,128)(2,1)S(1)} %get-tuple-element.47), channel_id=1, source_target_pairs={{0,3},{1,0},{2,1},{3,2},{4,7},{5,4},{6,5},{7,6},{8,11},{9,8},{10,9... | collective-permute-start | bytes 98312 | tf_op jit(solution)/shard_map/ppermute | solution.py:322
  107.4 4.1 %collective-permute-start.9 = (bf16[4,16,256]{2,1,0:T(8,128)(2,1)S(1)}, bf16[4,16,256]{2,1,0:T(8,128)(2,1)S(1)}, u32[]{:S(2)}, u32[]{:S(2)}) collective-permute-start(bf16[4,16,256]{2,1,0:T(8,128)(2,1)S(1)} %get-tuple-element.48), channel_id=1, source_target_pairs={{0,2},{1,3},{2,0},{3,1},{4,6},{5,7},{6,4},{7,5},{8,10},{9,11},{10,... | collective-permute-start | bytes 98312 | tf_op jit(solution)/shard_map/ppermute | solution.py:322
  111.6 3.2 %collective-permute-done.9 = bf16[4,16,256]{2,1,0:T(8,128)(2,1)S(1)} collective-permute-done((bf16[4,16,256]{2,1,0:T(8,128)(2,1)S(1)}, bf16[4,16,256]{2,1,0:T(8,128)(2,1)S(1)}, u32[]{:S(2)}, u32[]{:S(2)}) %collective-permute-start.9) | collective-permute-done | bytes 32800 | tf_op jit(solution)/shard_map/ppermute | solution.py:322
  115.6 14.0 %all-to-all-start.3 = ((bf16[16,2,512]{2,1,0:T(2,128)(2,1)}), bf16[16,2,512]{2,1,0:T(2,128)(2,1)S(1)}, u32[]{:S(2)}, u32[]{:S(2)}) async-start(bf16[16,2,512]{2,1,0:T(2,128)(2,1)} %reshape.37), calls=%async_computation.3 | async-start | bytes 65536 | tf_op jit(solution)/shard_map/all_to_all | solution.py:384
  131.5 10.6 %all-to-all-done.3 = bf16[16,2,512]{2,1,0:T(2,128)(2,1)S(1)} async-done(((bf16[16,2,512]{2,1,0:T(2,128)(2,1)}), bf16[16,2,512]{2,1,0:T(2,128)(2,1)S(1)}, u32[]{:S(2)}, u32[]{:S(2)}) %all-to-all-start.3) | async-done | bytes 32800 | tf_op jit(solution)/shard_map/all_to_all | solution.py:384
  (55 shorter events, 9.1 us)
Async XLA Ops:
  0.6 11.1 %copy-start = (bf16[512,1024]{1,0:T(8,128)(2,1)S(1)}, bf16[512,1024]{1,0:T(8,128)(2,1)}, u32[]{:S(2)}) copy-start(bf16[512,1024]{1,0:T(8,128)(2,1)} %w_ref.3) | copy-start | bytes 3145732
  0.6 11.1 %copy-start.1 = (bf16[1,1,256,1024]{3,2,1,0:T(8,128)(2,1)S(1)}, bf16[1,1,256,1024]{3,2,1,0:T(8,128)(2,1)}, u32[]{:S(2)}) copy-start(bf16[1,1,256,1024]{3,2,1,0:T(8,128)(2,1)} %param.10) | copy-start | bytes 1572868
  0.7 11.1 %copy-start.3 = (bf16[1,1,256,512]{3,2,1,0:T(8,128)(2,1)S(1)}, bf16[1,1,256,512]{3,2,1,0:T(8,128)(2,1)}, u32[]{:S(2)}) copy-start(bf16[1,1,256,512]{3,2,1,0:T(8,128)(2,1)} %param.7) | copy-start | bytes 786436
  0.7 11.1 %copy-start.4 = (s32[1,1,2,16]{3,2,1,0:T(2,128)S(1)}, s32[1,1,2,16]{3,2,1,0:T(2,128)}, u32[]{:S(2)}) copy-start(s32[1,1,2,16]{3,2,1,0:T(2,128)} %param.13) | copy-start | bytes 388
  3.0 38.2 %all-to-all-start = ((bf16[16,256,128]{2,1,0:T(8,128)(2,1)}), bf16[16,256,128]{2,1,0:T(8,128)(2,1)}, u32[]{:S(2)}, u32[]{:S(2)}) async-start(bf16[16,256,128]{2,1,0:T(8,128)(2,1)} %shard_map.111), calls=%async_computation | async-start | bytes 2097152 | tf_op jit(solution)/shard_map/all_to_all | solution.py:310
  11.8 11.9 %copy-start.5 = (s32[1,16,16]{2,1,0:T(8,128)S(1)}, s32[1,16,16]{2,1,0:T(8,128)}, u32[]{:S(2)}) copy-start(s32[1,16,16]{2,1,0:T(8,128)} %param.12) | copy-start | bytes 3076
  12.4 18.3 %collective-permute-start.2 = (bf16[2,272,128]{2,1,0:T(8,128)(2,1)S(1)}, bf16[2,272,128]{2,1,0:T(8,128)(2,1)S(1)}, u32[]{:S(2)}, u32[]{:S(2)}) collective-permute-start(bf16[2,272,128]{2,1,0:T(8,128)(2,1)S(1)} %get-tuple-element.34), channel_id=1, source_target_pairs={{0,3},{1,0},{2,1},{3,2},{4,7},{5,4},{6,5},{7,6},{8,11},{9,8},{10,9... | collective-permute-start | bytes 417800 | tf_op jit(solution)/shard_map/ppermute | solution.py:346
  17.4 13.3 %collective-permute-start = (bf16[2,272,128]{2,1,0:T(8,128)(2,1)S(1)}, bf16[2,272,128]{2,1,0:T(8,128)(2,1)S(1)}, u32[]{:S(2)}, u32[]{:S(2)}) collective-permute-start(bf16[2,272,128]{2,1,0:T(8,128)(2,1)S(1)} %get-tuple-element.35), channel_id=1, source_target_pairs={{0,1},{1,2},{2,3},{3,0},{4,5},{5,6},{6,7},{7,4},{8,9},{9,10},{10,1... | collective-permute-start | bytes 417800 | tf_op jit(solution)/shard_map/ppermute | solution.py:346
  19.3 11.5 %collective-permute-start.1 = (bf16[2,272,128]{2,1,0:T(8,128)(2,1)S(1)}, bf16[2,272,128]{2,1,0:T(8,128)(2,1)S(1)}, u32[]{:S(2)}, u32[]{:S(2)}) collective-permute-start(bf16[2,272,128]{2,1,0:T(8,128)(2,1)S(1)} %get-tuple-element.36), channel_id=1, source_target_pairs={{0,2},{1,3},{2,0},{3,1},{4,6},{5,7},{6,4},{7,5},{8,10},{9,11},{10,... | collective-permute-start | bytes 417800 | tf_op jit(solution)/shard_map/ppermute | solution.py:346
  30.8 10.2 %collective-permute-start.3 = (bf16[4,272,128]{2,1,0:T(8,128)(2,1)S(1)}, bf16[4,272,128]{2,1,0:T(8,128)(2,1)S(1)}, u32[]{:S(2)}, u32[]{:S(2)}) collective-permute-start(bf16[4,272,128]{2,1,0:T(8,128)(2,1)S(1)} %pad_maximum_fusion), channel_id=1, source_target_pairs={{0,4},{1,5},{2,6},{3,7},{4,0},{5,1},{6,2},{7,3},{8,12},{9,13},{10,... | collective-permute-start | bytes 835592 | tf_op jit(solution)/shard_map/ppermute | solution.py:349
  50.0 21.3 %all-to-all-start.1 = ((bf16[8,128,128]{2,1,0:T(8,128)(2,1)}), bf16[8,128,128]{2,1,0:T(8,128)(2,1)S(1)}, u32[]{:S(2)}, u32[]{:S(2)}) async-start(bf16[8,128,128]{2,1,0:T(8,128)(2,1)} %get-tuple-element.18), calls=%async_computation.1 | async-start | bytes 524288 | tf_op jit(solution)/shard_map/all_to_all | solution.py:356
  71.3 43.5 %all-to-all-start.2 = ((bf16[16,384,128]{2,1,0:T(8,128)(2,1)}), bf16[16,384,128]{2,1,0:T(8,128)(2,1)S(1)}, u32[]{:S(2)}, u32[]{:S(2)}) async-start(bf16[16,384,128]{2,1,0:T(8,128)(2,1)} %shard_map.113), calls=%async_computation.2 | async-start | bytes 3145728 | tf_op jit(solution)/shard_map/all_to_all | solution.py:310
  79.1 1.0 copy-start.2
  81.8 4.0 %collective-permute-start.4 = (bf16[4,4,4,16,256]{4,3,2,1,0:T(8,128)(2,1)}, bf16[4,4,4,16,256]{4,3,2,1,0:T(8,128)(2,1)S(1)}, u32[]{:S(2)}, u32[]{:S(2)}) collective-permute-start(bf16[4,4,4,16,256]{4,3,2,1,0:T(8,128)(2,1)} %get-tuple-element.24), channel_id=1, source_target_pairs={{0,16},{16,0},{32,48},{48,32},{64,80},{80,64},{96,112},{112,96},{1... | collective-permute-start | bytes 1572872 | tf_op jit(solution)/shard_map/ppermute | solution.py:372
  86.0 9.2 %collective-permute-start.5 = (bf16[4,4,16,256]{3,2,1,0:T(8,128)(2,1)S(1)}, bf16[4,4,16,256]{3,2,1,0:T(8,128)(2,1)S(1)}, u32[]{:S(2)}, u32[]{:S(2)}) collective-permute-start(bf16[4,4,16,256]{3,2,1,0:T(8,128)(2,1)S(1)} %get-tuple-element.37), channel_id=1, source_target_pairs={{0,128},{16,144},{32,160},{48,176},{64,192},{80,208},{96,224},{112... | collective-permute-start | bytes 393224 | tf_op jit(solution)/shard_map/ppermute | solution.py:322
  88.0 8.6 %collective-permute-start.7 = (bf16[4,4,16,256]{3,2,1,0:T(8,128)(2,1)S(1)}, bf16[4,4,16,256]{3,2,1,0:T(8,128)(2,1)S(1)}, u32[]{:S(2)}, u32[]{:S(2)}) collective-permute-start(bf16[4,4,16,256]{3,2,1,0:T(8,128)(2,1)S(1)} %get-tuple-element.38), channel_id=1, source_target_pairs={{0,384},{16,400},{32,416},{48,432},{64,448},{80,464},{96,480},{112... | collective-permute-start | bytes 393224 | tf_op jit(solution)/shard_map/ppermute | solution.py:322
  91.9 8.4 %collective-permute-start.6 = (bf16[4,4,16,256]{3,2,1,0:T(8,128)(2,1)S(1)}, bf16[4,4,16,256]{3,2,1,0:T(8,128)(2,1)S(1)}, u32[]{:S(2)}, u32[]{:S(2)}) collective-permute-start(bf16[4,4,16,256]{3,2,1,0:T(8,128)(2,1)S(1)} %get-tuple-element.39), channel_id=1, source_target_pairs={{0,256},{16,272},{32,288},{48,304},{64,320},{80,336},{96,352},{112... | collective-permute-start | bytes 393224 | tf_op jit(solution)/shard_map/ppermute | solution.py:322
  100.4 11.2 %collective-permute-start.8 = (bf16[4,16,256]{2,1,0:T(8,128)(2,1)S(1)}, bf16[4,16,256]{2,1,0:T(8,128)(2,1)S(1)}, u32[]{:S(2)}, u32[]{:S(2)}) collective-permute-start(bf16[4,16,256]{2,1,0:T(8,128)(2,1)S(1)} %get-tuple-element.46), channel_id=1, source_target_pairs={{0,1},{1,2},{2,3},{3,0},{4,5},{5,6},{6,7},{7,4},{8,9},{9,10},{10,1... | collective-permute-start | bytes 98312 | tf_op jit(solution)/shard_map/ppermute | solution.py:322
  104.2 7.4 %collective-permute-start.10 = (bf16[4,16,256]{2,1,0:T(8,128)(2,1)S(1)}, bf16[4,16,256]{2,1,0:T(8,128)(2,1)S(1)}, u32[]{:S(2)}, u32[]{:S(2)}) collective-permute-start(bf16[4,16,256]{2,1,0:T(8,128)(2,1)S(1)} %get-tuple-element.47), channel_id=1, source_target_pairs={{0,3},{1,0},{2,1},{3,2},{4,7},{5,4},{6,5},{7,6},{8,11},{9,8},{10,9... | collective-permute-start | bytes 98312 | tf_op jit(solution)/shard_map/ppermute | solution.py:322
  107.4 7.3 %collective-permute-start.9 = (bf16[4,16,256]{2,1,0:T(8,128)(2,1)S(1)}, bf16[4,16,256]{2,1,0:T(8,128)(2,1)S(1)}, u32[]{:S(2)}, u32[]{:S(2)}) collective-permute-start(bf16[4,16,256]{2,1,0:T(8,128)(2,1)S(1)} %get-tuple-element.48), channel_id=1, source_target_pairs={{0,2},{1,3},{2,0},{3,1},{4,6},{5,7},{6,4},{7,5},{8,10},{9,11},{10,... | collective-permute-start | bytes 98312 | tf_op jit(solution)/shard_map/ppermute | solution.py:322
  115.6 26.5 %all-to-all-start.3 = ((bf16[16,2,512]{2,1,0:T(2,128)(2,1)}), bf16[16,2,512]{2,1,0:T(2,128)(2,1)S(1)}, u32[]{:S(2)}, u32[]{:S(2)}) async-start(bf16[16,2,512]{2,1,0:T(2,128)(2,1)} %reshape.37), calls=%async_computation.3 | async-start | bytes 65536 | tf_op jit(solution)/shard_map/all_to_all | solution.py:384

commit v9 on v8

--- a/solution.py
+++ b/solution.py
@@ -87,14 +87,14 @@
 
 def place_queries(place_ref, near, far_ref, qg_ref):
     for d, piece in enumerate(near):
-        along = lax.rem(place_ref[2] - d + Y, Y)
+        along = lax.bitwise_xor(place_ref[2], d)
         qg_ref[place_ref[1] * Y + along, :, :] = piece[0:TOK, :]
         qg_ref[(1 - place_ref[1]) * Y + along, :, :] = far_ref[d, 0:TOK, :]
 
 
 def source_of(i, place_ref):
     row, along = lax.div(i, Y), lax.rem(i, Y)
-    return jnp.where(row == place_ref[1], 0, Y) + lax.rem(place_ref[2] - along + Y, Y)
+    return jnp.where(row == place_ref[1], 0, Y) + lax.bitwise_xor(place_ref[2], along)
 
 
 def forward_kernel(fetch_ref, mask_ref, place_ref, in_ref, *refs):
@@ -317,8 +317,8 @@
         pairs = []
         for i in range(count):
             at = (i // step) % size
-            pairs.append((i, i + ((at + d) % size - at) * step))
-        send = lax.dynamic_index_in_dim(pieces, (here + d) % size, 0, keepdims=False)
+            pairs.append((i, i + ((at ^ d) - at) * step))
+        send = lax.dynamic_index_in_dim(pieces, here ^ d, 0, keepdims=False)
         total = total + lax.ppermute(send, axis, pairs).astype(F32)
     return total
 
@@ -341,8 +341,8 @@
     queries = queries.reshape(2, Y, PACK_ROWS, WIDE)
     moved = [lax.dynamic_index_in_dim(queries, along, 1, keepdims=False)]
     for d in range(1, Y):
-        send = lax.dynamic_index_in_dim(queries, (along + d) % Y, 1, keepdims=False)
-        pairs = [(a, a // Y * Y + (a % Y + d) % Y) for a in range(VIEWS)]
+        send = lax.dynamic_index_in_dim(queries, along ^ d, 1, keepdims=False)
+        pairs = [(a, a ^ d) for a in range(VIEWS)]
         moved.append(lax.ppermute(send, "view", pairs))
     near = [lax.dynamic_index_in_dim(m, row, 0, keepdims=False) for m in moved]
     far = jnp.stack([lax.dynamic_index_in_dim(m, 1 - row, 0, keepdims=False) for m in moved])

time: 144 us -> 144 us (level)
  transfers between devices with their start and end apart: 15 -> 15, of which waited for: 7 -> 9; matrix products, arithmetic and copies ran while one was open for 1% -> 1% of each run, Pallas kernels for 15% -> 15%
where the time goes in v9:
time: 144 us; the launch traced here: 143 us
  starting transfers between devices  72.8 us (51%)
  waiting for transfers between devices  33.5 us (23%)
  Pallas kernels  32.1 us (22%)
  local copies, waits for them, and re-layouts  2.48 us (2%)
    pallas_call x6, Pallas kernels, call(): pl.pallas_call(kernel, out_shape=outs, in_specs=[SMEM] * smem + [VMEM] *...  32.1 us
    ppermute x6, starting transfers between devices, ring_sum(): total = total + lax.ppermute(send, axis, pairs).astype(F32)  20.1 us
    all_to_all x2, starting transfers between devices, swap(): return lax.all_to_all(rows, axis, split_axis=0, concat_axis=0, tiled=True)  16.8 us
    all_to_all x1, starting transfers between devices, on_device(): lax.all_to_all(term, ('scene', 'view'), 0, 0, tiled=True, axis_index_grou...  12.7 us
    all_to_all x1, waiting for transfers between devices, on_device(): lax.all_to_all(term, ('scene', 'view'), 0, 0, tiled=True, axis_index_grou...  10.7 us
    ppermute x3, starting transfers between devices, on_device(): moved.append(lax.ppermute(send, 'view', pairs))  10.4 us
    ppermute x6, waiting for transfers between devices, ring_sum(): total = total + lax.ppermute(send, axis, pairs).astype(F32)  9.07 us
    ppermute x3, waiting for transfers between devices, on_device(): moved.append(lax.ppermute(send, 'view', pairs))  7.15 us
  transfers between devices with their start and end apart: 15, of which 9 were waited for; matrix products, arithmetic and copies ran while one was open for 1% of the time, Pallas kernels for 15%

profile of v9, /device:TPU:6, one launch (start us, length us, event | category | flops | bytes accessed | tf_op | source)
XLA Modules:
  0.0 143.1 jit_solution(9063691387724495324)
XLA Ops:
  0.7 2.3 %shard_map.111 = bf16[16,256,128]{2,1,0:T(8,128)(2,1)} custom-call(bf16[256,512]{1,0:T(8,128)(2,1)} %bitcast.62, bf16[256,512]{1,0:T(8,128)(2,1)} %bitcast.63), custom_call_target="tpu_custom_call" | custom-call | bytes 4194304 | tf_op jit(solution)/shard_map/pallas_call | solution.py:258
  3.0 8.7 %all-to-all-start = ((bf16[16,256,128]{2,1,0:T(8,128)(2,1)}), bf16[16,256,128]{2,1,0:T(8,128)(2,1)}, u32[]{:S(2)}, u32[]{:S(2)}) async-start(bf16[16,256,128]{2,1,0:T(8,128)(2,1)} %shard_map.111), calls=%async_computation | async-start | bytes 2097152 | tf_op jit(solution)/shard_map/all_to_all | solution.py:310
  12.4 5.0 %collective-permute-start.2 = (bf16[2,272,128]{2,1,0:T(8,128)(2,1)S(1)}, bf16[2,272,128]{2,1,0:T(8,128)(2,1)S(1)}, u32[]{:S(2)}, u32[]{:S(2)}) collective-permute-start(bf16[2,272,128]{2,1,0:T(8,128)(2,1)S(1)} %get-tuple-element.34), channel_id=1, source_target_pairs={{0,3},{1,2},{2,1},{3,0},{4,7},{5,6},{6,5},{7,4},{8,11},{9,10},{10,... | collective-permute-start | bytes 417800 | tf_op jit(solution)/shard_map/ppermute | solution.py:346
  17.4 2.2 %collective-permute-start = (bf16[2,272,128]{2,1,0:T(8,128)(2,1)S(1)}, bf16[2,272,128]{2,1,0:T(8,128)(2,1)S(1)}, u32[]{:S(2)}, u32[]{:S(2)}) collective-permute-start(bf16[2,272,128]{2,1,0:T(8,128)(2,1)S(1)} %get-tuple-element.35), channel_id=1, source_target_pairs={{0,1},{1,0},{2,3},{3,2},{4,5},{5,4},{6,7},{7,6},{8,9},{9,8},{10,11... | collective-permute-start | bytes 417800 | tf_op jit(solution)/shard_map/ppermute | solution.py:346
  19.5 3.3 %collective-permute-start.1 = (bf16[2,272,128]{2,1,0:T(8,128)(2,1)S(1)}, bf16[2,272,128]{2,1,0:T(8,128)(2,1)S(1)}, u32[]{:S(2)}, u32[]{:S(2)}) collective-permute-start(bf16[2,272,128]{2,1,0:T(8,128)(2,1)S(1)} %get-tuple-element.36), channel_id=1, source_target_pairs={{0,2},{1,3},{2,0},{3,1},{4,6},{5,7},{6,4},{7,5},{8,10},{9,11},{10,... | collective-permute-start | bytes 417800 | tf_op jit(solution)/shard_map/ppermute | solution.py:346
  23.1 5.7 %collective-permute-done = bf16[2,272,128]{2,1,0:T(8,128)(2,1)S(1)} collective-permute-done((bf16[2,272,128]{2,1,0:T(8,128)(2,1)S(1)}, bf16[2,272,128]{2,1,0:T(8,128)(2,1)S(1)}, u32[]{:S(2)}, u32[]{:S(2)}) %collective-permute-start) | collective-permute-done | bytes 139296 | tf_op jit(solution)/shard_map/ppermute | solution.py:346
  30.4 5.9 %collective-permute-start.3 = (bf16[4,272,128]{2,1,0:T(8,128)(2,1)S(1)}, bf16[4,272,128]{2,1,0:T(8,128)(2,1)S(1)}, u32[]{:S(2)}, u32[]{:S(2)}) collective-permute-start(bf16[4,272,128]{2,1,0:T(8,128)(2,1)S(1)} %pad_maximum_fusion), channel_id=1, source_target_pairs={{0,4},{1,5},{2,6},{3,7},{4,0},{5,1},{6,2},{7,3},{8,12},{9,13},{10,... | collective-permute-start | bytes 835592 | tf_op jit(solution)/shard_map/ppermute | solution.py:349
  36.4 4.5 %collective-permute-done.3.refs_4_ = bf16[4,272,128]{2,1,0:T(8,128)(2,1)S(1)} collective-permute-done((bf16[4,272,128]{2,1,0:T(8,128)(2,1)S(1)}, bf16[4,272,128]{2,1,0:T(8,128)(2,1)S(1)}, u32[]{:S(2)}, u32[]{:S(2)}) %collective-permute-start.3) | collective-permute-done | bytes 278560 | tf_op jit(solution)/shard_map/ppermute | solution.py:349
  41.0 8.8 %shard_map.112 = (bf16[8,128,128]{2,1,0:T(8,128)(2,1)}, f32[8,8,256]{2,1,0:T(8,128)S(1)}, bf16[8,256,128]{2,1,0:T(8,128)(2,1)S(1)}) custom-call(s32[256]{0:T(256)S(1)} %reshape.31.fetch_ref, s32[256]{0:T(256)S(1)} %reshape.34.mask_ref, s32[3]{0:T(128)S(1)} %pad_add_fusion.place_ref, bf16[16,256,128]{2,1,0:T(8,128)(2,1)} %all-to-all-done.in_ref, ...), custom_call_target="tpu_custom_call" | custom-call | flops 10000000000 | bytes 4194304 | tf_op jit(solution)/shard_map/pallas_call | solution.py:258
  49.9 5.0 %all-to-all-start.1 = ((bf16[8,128,128]{2,1,0:T(8,128)(2,1)}), bf16[8,128,128]{2,1,0:T(8,128)(2,1)S(1)}, u32[]{:S(2)}, u32[]{:S(2)}) async-start(bf16[8,128,128]{2,1,0:T(8,128)(2,1)} %get-tuple-element.18), calls=%async_computation.1 | async-start | bytes 524288 | tf_op jit(solution)/shard_map/all_to_all | solution.py:356
  54.9 16.8 %shard_map.113 = bf16[16,384,128]{2,1,0:T(8,128)(2,1)} custom-call(s32[256]{0:T(256)S(1)} %reshape.31.fetch_ref, s32[256]{0:T(256)S(1)} %reshape.34.mask_ref, s32[3]{0:T(128)S(1)} %pad_add_fusion.place_ref, bf16[16,256,128]{2,1,0:T(8,128)(2,1)} %all-to-all-done.in_ref, bf16[8,256,128]{2,1,0:T(8,128)(2,1)S(1)} %get-tuple-element.19.qg_ref, ...), custom_call_target="tpu_custom_call" | custom-call | flops 20000000000 | bytes 4194304 | tf_op jit(solution)/shard_map/pallas_call | solution.py:258
  71.7 8.1 %all-to-all-start.2 = ((bf16[16,384,128]{2,1,0:T(8,128)(2,1)}), bf16[16,384,128]{2,1,0:T(8,128)(2,1)S(1)}, u32[]{:S(2)}, u32[]{:S(2)}) async-start(bf16[16,384,128]{2,1,0:T(8,128)(2,1)} %shard_map.113), calls=%async_computation.2 | async-start | bytes 3145728 | tf_op jit(solution)/shard_map/all_to_all | solution.py:310
  82.6 1.9 %collective-permute-start.4 = (bf16[4,4,4,16,256]{4,3,2,1,0:T(8,128)(2,1)}, bf16[4,4,4,16,256]{4,3,2,1,0:T(8,128)(2,1)S(1)}, u32[]{:S(2)}, u32[]{:S(2)}) collective-permute-start(bf16[4,4,4,16,256]{4,3,2,1,0:T(8,128)(2,1)} %get-tuple-element.24), channel_id=1, source_target_pairs={{0,16},{16,0},{32,48},{48,32},{64,80},{80,64},{96,112},{112,96},{1... | collective-permute-start | bytes 1572872 | tf_op jit(solution)/shard_map/ppermute | solution.py:372
  84.5 2.0 %collective-permute-done.4 = bf16[4,4,4,16,256]{4,3,2,1,0:T(8,128)(2,1)S(1)} collective-permute-done((bf16[4,4,4,16,256]{4,3,2,1,0:T(8,128)(2,1)}, bf16[4,4,4,16,256]{4,3,2,1,0:T(8,128)(2,1)S(1)}, u32[]{:S(2)}, u32[]{:S(2)}) %collective-permute-start.4) | collective-permute-done | bytes 524320 | tf_op jit(solution)/shard_map/ppermute | solution.py:372
  86.8 2.7 %collective-permute-start.5 = (bf16[4,4,16,256]{3,2,1,0:T(8,128)(2,1)S(1)}, bf16[4,4,16,256]{3,2,1,0:T(8,128)(2,1)S(1)}, u32[]{:S(2)}, u32[]{:S(2)}) collective-permute-start(bf16[4,4,16,256]{3,2,1,0:T(8,128)(2,1)S(1)} %get-tuple-element.37), channel_id=1, source_target_pairs={{0,128},{16,144},{32,160},{48,176},{64,192},{80,208},{96,224},{112... | collective-permute-start | bytes 393224 | tf_op jit(solution)/shard_map/ppermute | solution.py:322
  89.5 3.0 %collective-permute-start.7 = (bf16[4,4,16,256]{3,2,1,0:T(8,128)(2,1)S(1)}, bf16[4,4,16,256]{3,2,1,0:T(8,128)(2,1)S(1)}, u32[]{:S(2)}, u32[]{:S(2)}) collective-permute-start(bf16[4,4,16,256]{3,2,1,0:T(8,128)(2,1)S(1)} %get-tuple-element.38), channel_id=1, source_target_pairs={{0,384},{16,400},{32,416},{48,432},{64,448},{80,464},{96,480},{112... | collective-permute-start | bytes 393224 | tf_op jit(solution)/shard_map/ppermute | solution.py:322
  92.6 4.0 %collective-permute-start.6 = (bf16[4,4,16,256]{3,2,1,0:T(8,128)(2,1)S(1)}, bf16[4,4,16,256]{3,2,1,0:T(8,128)(2,1)S(1)}, u32[]{:S(2)}, u32[]{:S(2)}) collective-permute-start(bf16[4,4,16,256]{3,2,1,0:T(8,128)(2,1)S(1)} %get-tuple-element.39), channel_id=1, source_target_pairs={{0,256},{16,272},{32,288},{48,304},{64,320},{80,336},{96,352},{112... | collective-permute-start | bytes 393224 | tf_op jit(solution)/shard_map/ppermute | solution.py:322
  97.9 3.1 %collective-permute-done.6 = bf16[4,4,16,256]{3,2,1,0:T(8,128)(2,1)S(1)} collective-permute-done((bf16[4,4,16,256]{3,2,1,0:T(8,128)(2,1)S(1)}, bf16[4,4,16,256]{3,2,1,0:T(8,128)(2,1)S(1)}, u32[]{:S(2)}, u32[]{:S(2)}) %collective-permute-start.6) | collective-permute-done | bytes 131104 | tf_op jit(solution)/shard_map/ppermute | solution.py:322
  101.1 3.8 %collective-permute-start.8 = (bf16[4,16,256]{2,1,0:T(8,128)(2,1)S(1)}, bf16[4,16,256]{2,1,0:T(8,128)(2,1)S(1)}, u32[]{:S(2)}, u32[]{:S(2)}) collective-permute-start(bf16[4,16,256]{2,1,0:T(8,128)(2,1)S(1)} %get-tuple-element.46), channel_id=1, source_target_pairs={{0,1},{1,0},{2,3},{3,2},{4,5},{5,4},{6,7},{7,6},{8,9},{9,8},{10,11... | collective-permute-start | bytes 98312 | tf_op jit(solution)/shard_map/ppermute | solution.py:322
  104.9 4.0 %collective-permute-start.10 = (bf16[4,16,256]{2,1,0:T(8,128)(2,1)S(1)}, bf16[4,16,256]{2,1,0:T(8,128)(2,1)S(1)}, u32[]{:S(2)}, u32[]{:S(2)}) collective-permute-start(bf16[4,16,256]{2,1,0:T(8,128)(2,1)S(1)} %get-tuple-element.47), channel_id=1, source_target_pairs={{0,3},{1,2},{2,1},{3,0},{4,7},{5,6},{6,5},{7,4},{8,11},{9,10},{10,... | collective-permute-start | bytes 98312 | tf_op jit(solution)/shard_map/ppermute | solution.py:322
  108.9 2.5 %collective-permute-start.9 = (bf16[4,16,256]{2,1,0:T(8,128)(2,1)S(1)}, bf16[4,16,256]{2,1,0:T(8,128)(2,1)S(1)}, u32[]{:S(2)}, u32[]{:S(2)}) collective-permute-start(bf16[4,16,256]{2,1,0:T(8,128)(2,1)S(1)} %get-tuple-element.48), channel_id=1, source_target_pairs={{0,2},{1,3},{2,0},{3,1},{4,6},{5,7},{6,4},{7,5},{8,10},{9,11},{10,... | collective-permute-start | bytes 98312 | tf_op jit(solution)/shard_map/ppermute | solution.py:322
  111.9 4.3 %collective-permute-done.9 = bf16[4,16,256]{2,1,0:T(8,128)(2,1)S(1)} collective-permute-done((bf16[4,16,256]{2,1,0:T(8,128)(2,1)S(1)}, bf16[4,16,256]{2,1,0:T(8,128)(2,1)S(1)}, u32[]{:S(2)}, u32[]{:S(2)}) %collective-permute-start.9) | collective-permute-done | bytes 32800 | tf_op jit(solution)/shard_map/ppermute | solution.py:322
  117.0 12.7 %all-to-all-start.3 = ((bf16[16,2,512]{2,1,0:T(2,128)(2,1)}), bf16[16,2,512]{2,1,0:T(2,128)(2,1)S(1)}, u32[]{:S(2)}, u32[]{:S(2)}) async-start(bf16[16,2,512]{2,1,0:T(2,128)(2,1)} %reshape.37), calls=%async_computation.3 | async-start | bytes 65536 | tf_op jit(solution)/shard_map/all_to_all | solution.py:384
  131.6 10.7 %all-to-all-done.3 = bf16[16,2,512]{2,1,0:T(2,128)(2,1)S(1)} async-done(((bf16[16,2,512]{2,1,0:T(2,128)(2,1)}), bf16[16,2,512]{2,1,0:T(2,128)(2,1)S(1)}, u32[]{:S(2)}, u32[]{:S(2)}) %all-to-all-start.3) | async-done | bytes 32800 | tf_op jit(solution)/shard_map/all_to_all | solution.py:384
  (55 shorter events, 10.8 us)
Async XLA Ops:
  0.6 11.1 %copy-start = (bf16[512,1024]{1,0:T(8,128)(2,1)S(1)}, bf16[512,1024]{1,0:T(8,128)(2,1)}, u32[]{:S(2)}) copy-start(bf16[512,1024]{1,0:T(8,128)(2,1)} %w_ref.3) | copy-start | bytes 3145732
  0.6 11.1 %copy-start.1 = (bf16[1,1,256,1024]{3,2,1,0:T(8,128)(2,1)S(1)}, bf16[1,1,256,1024]{3,2,1,0:T(8,128)(2,1)}, u32[]{:S(2)}) copy-start(bf16[1,1,256,1024]{3,2,1,0:T(8,128)(2,1)} %param.10) | copy-start | bytes 1572868
  0.7 11.1 %copy-start.3 = (bf16[1,1,256,512]{3,2,1,0:T(8,128)(2,1)S(1)}, bf16[1,1,256,512]{3,2,1,0:T(8,128)(2,1)}, u32[]{:S(2)}) copy-start(bf16[1,1,256,512]{3,2,1,0:T(8,128)(2,1)} %param.7) | copy-start | bytes 786436
  0.7 11.1 %copy-start.4 = (s32[1,1,2,16]{3,2,1,0:T(2,128)S(1)}, s32[1,1,2,16]{3,2,1,0:T(2,128)}, u32[]{:S(2)}) copy-start(s32[1,1,2,16]{3,2,1,0:T(2,128)} %param.13) | copy-start | bytes 388
  3.0 38.0 %all-to-all-start = ((bf16[16,256,128]{2,1,0:T(8,128)(2,1)}), bf16[16,256,128]{2,1,0:T(8,128)(2,1)}, u32[]{:S(2)}, u32[]{:S(2)}) async-start(bf16[16,256,128]{2,1,0:T(8,128)(2,1)} %shard_map.111), calls=%async_computation | async-start | bytes 2097152 | tf_op jit(solution)/shard_map/all_to_all | solution.py:310
  11.8 11.3 %copy-start.5 = (s32[1,16,16]{2,1,0:T(8,128)S(1)}, s32[1,16,16]{2,1,0:T(8,128)}, u32[]{:S(2)}) copy-start(s32[1,16,16]{2,1,0:T(8,128)} %param.12) | copy-start | bytes 3076
  12.4 16.5 %collective-permute-start.2 = (bf16[2,272,128]{2,1,0:T(8,128)(2,1)S(1)}, bf16[2,272,128]{2,1,0:T(8,128)(2,1)S(1)}, u32[]{:S(2)}, u32[]{:S(2)}) collective-permute-start(bf16[2,272,128]{2,1,0:T(8,128)(2,1)S(1)} %get-tuple-element.34), channel_id=1, source_target_pairs={{0,3},{1,2},{2,1},{3,0},{4,7},{5,6},{6,5},{7,4},{8,11},{9,10},{10,... | collective-permute-start | bytes 417800 | tf_op jit(solution)/shard_map/ppermute | solution.py:346
  17.4 11.5 %collective-permute-start = (bf16[2,272,128]{2,1,0:T(8,128)(2,1)S(1)}, bf16[2,272,128]{2,1,0:T(8,128)(2,1)S(1)}, u32[]{:S(2)}, u32[]{:S(2)}) collective-permute-start(bf16[2,272,128]{2,1,0:T(8,128)(2,1)S(1)} %get-tuple-element.35), channel_id=1, source_target_pairs={{0,1},{1,0},{2,3},{3,2},{4,5},{5,4},{6,7},{7,6},{8,9},{9,8},{10,11... | collective-permute-start | bytes 417800 | tf_op jit(solution)/shard_map/ppermute | solution.py:346
  19.5 10.8 %collective-permute-start.1 = (bf16[2,272,128]{2,1,0:T(8,128)(2,1)S(1)}, bf16[2,272,128]{2,1,0:T(8,128)(2,1)S(1)}, u32[]{:S(2)}, u32[]{:S(2)}) collective-permute-start(bf16[2,272,128]{2,1,0:T(8,128)(2,1)S(1)} %get-tuple-element.36), channel_id=1, source_target_pairs={{0,2},{1,3},{2,0},{3,1},{4,6},{5,7},{6,4},{7,5},{8,10},{9,11},{10,... | collective-permute-start | bytes 417800 | tf_op jit(solution)/shard_map/ppermute | solution.py:346
  30.4 10.5 %collective-permute-start.3 = (bf16[4,272,128]{2,1,0:T(8,128)(2,1)S(1)}, bf16[4,272,128]{2,1,0:T(8,128)(2,1)S(1)}, u32[]{:S(2)}, u32[]{:S(2)}) collective-permute-start(bf16[4,272,128]{2,1,0:T(8,128)(2,1)S(1)} %pad_maximum_fusion), channel_id=1, source_target_pairs={{0,4},{1,5},{2,6},{3,7},{4,0},{5,1},{6,2},{7,3},{8,12},{9,13},{10,... | collective-permute-start | bytes 835592 | tf_op jit(solution)/shard_map/ppermute | solution.py:349
  49.9 21.9 %all-to-all-start.1 = ((bf16[8,128,128]{2,1,0:T(8,128)(2,1)}), bf16[8,128,128]{2,1,0:T(8,128)(2,1)S(1)}, u32[]{:S(2)}, u32[]{:S(2)}) async-start(bf16[8,128,128]{2,1,0:T(8,128)(2,1)} %get-tuple-element.18), calls=%async_computation.1 | async-start | bytes 524288 | tf_op jit(solution)/shard_map/all_to_all | solution.py:356
  71.7 44.5 %all-to-all-start.2 = ((bf16[16,384,128]{2,1,0:T(8,128)(2,1)}), bf16[16,384,128]{2,1,0:T(8,128)(2,1)S(1)}, u32[]{:S(2)}, u32[]{:S(2)}) async-start(bf16[16,384,128]{2,1,0:T(8,128)(2,1)} %shard_map.113), calls=%async_computation.2 | async-start | bytes 3145728 | tf_op jit(solution)/shard_map/all_to_all | solution.py:310
  79.8 1.0 copy-start.2
  82.6 4.0 %collective-permute-start.4 = (bf16[4,4,4,16,256]{4,3,2,1,0:T(8,128)(2,1)}, bf16[4,4,4,16,256]{4,3,2,1,0:T(8,128)(2,1)S(1)}, u32[]{:S(2)}, u32[]{:S(2)}) collective-permute-start(bf16[4,4,4,16,256]{4,3,2,1,0:T(8,128)(2,1)} %get-tuple-element.24), channel_id=1, source_target_pairs={{0,16},{16,0},{32,48},{48,32},{64,80},{80,64},{96,112},{112,96},{1... | collective-permute-start | bytes 1572872 | tf_op jit(solution)/shard_map/ppermute | solution.py:372
  86.8 9.9 %collective-permute-start.5 = (bf16[4,4,16,256]{3,2,1,0:T(8,128)(2,1)S(1)}, bf16[4,4,16,256]{3,2,1,0:T(8,128)(2,1)S(1)}, u32[]{:S(2)}, u32[]{:S(2)}) collective-permute-start(bf16[4,4,16,256]{3,2,1,0:T(8,128)(2,1)S(1)} %get-tuple-element.37), channel_id=1, source_target_pairs={{0,128},{16,144},{32,160},{48,176},{64,192},{80,208},{96,224},{112... | collective-permute-start | bytes 393224 | tf_op jit(solution)/shard_map/ppermute | solution.py:322
  89.5 8.4 %collective-permute-start.7 = (bf16[4,4,16,256]{3,2,1,0:T(8,128)(2,1)S(1)}, bf16[4,4,16,256]{3,2,1,0:T(8,128)(2,1)S(1)}, u32[]{:S(2)}, u32[]{:S(2)}) collective-permute-start(bf16[4,4,16,256]{3,2,1,0:T(8,128)(2,1)S(1)} %get-tuple-element.38), channel_id=1, source_target_pairs={{0,384},{16,400},{32,416},{48,432},{64,448},{80,464},{96,480},{112... | collective-permute-start | bytes 393224 | tf_op jit(solution)/shard_map/ppermute | solution.py:322
  92.6 8.4 %collective-permute-start.6 = (bf16[4,4,16,256]{3,2,1,0:T(8,128)(2,1)S(1)}, bf16[4,4,16,256]{3,2,1,0:T(8,128)(2,1)S(1)}, u32[]{:S(2)}, u32[]{:S(2)}) collective-permute-start(bf16[4,4,16,256]{3,2,1,0:T(8,128)(2,1)S(1)} %get-tuple-element.39), channel_id=1, source_target_pairs={{0,256},{16,272},{32,288},{48,304},{64,320},{80,336},{96,352},{112... | collective-permute-start | bytes 393224 | tf_op jit(solution)/shard_map/ppermute | solution.py:322
  101.1 10.4 %collective-permute-start.8 = (bf16[4,16,256]{2,1,0:T(8,128)(2,1)S(1)}, bf16[4,16,256]{2,1,0:T(8,128)(2,1)S(1)}, u32[]{:S(2)}, u32[]{:S(2)}) collective-permute-start(bf16[4,16,256]{2,1,0:T(8,128)(2,1)S(1)} %get-tuple-element.46), channel_id=1, source_target_pairs={{0,1},{1,0},{2,3},{3,2},{4,5},{5,4},{6,7},{7,6},{8,9},{9,8},{10,11... | collective-permute-start | bytes 98312 | tf_op jit(solution)/shard_map/ppermute | solution.py:322
  104.9 7.0 %collective-permute-start.10 = (bf16[4,16,256]{2,1,0:T(8,128)(2,1)S(1)}, bf16[4,16,256]{2,1,0:T(8,128)(2,1)S(1)}, u32[]{:S(2)}, u32[]{:S(2)}) collective-permute-start(bf16[4,16,256]{2,1,0:T(8,128)(2,1)S(1)} %get-tuple-element.47), channel_id=1, source_target_pairs={{0,3},{1,2},{2,1},{3,0},{4,7},{5,6},{6,5},{7,4},{8,11},{9,10},{10,... | collective-permute-start | bytes 98312 | tf_op jit(solution)/shard_map/ppermute | solution.py:322
  108.9 7.3 %collective-permute-start.9 = (bf16[4,16,256]{2,1,0:T(8,128)(2,1)S(1)}, bf16[4,16,256]{2,1,0:T(8,128)(2,1)S(1)}, u32[]{:S(2)}, u32[]{:S(2)}) collective-permute-start(bf16[4,16,256]{2,1,0:T(8,128)(2,1)S(1)} %get-tuple-element.48), channel_id=1, source_target_pairs={{0,2},{1,3},{2,0},{3,1},{4,6},{5,7},{6,4},{7,5},{8,10},{9,11},{10,... | collective-permute-start | bytes 98312 | tf_op jit(solution)/shard_map/ppermute | solution.py:322
  117.0 25.3 %all-to-all-start.3 = ((bf16[16,2,512]{2,1,0:T(2,128)(2,1)}), bf16[16,2,512]{2,1,0:T(2,128)(2,1)S(1)}, u32[]{:S(2)}, u32[]{:S(2)}) async-start(bf16[16,2,512]{2,1,0:T(2,128)(2,1)} %reshape.37), calls=%async_computation.3 | async-start | bytes 65536 | tf_op jit(solution)/shard_map/all_to_all | solution.py:384
